TPU v7x, 128 devices: a whole 4x4x4 slice. The times are simulated.
128 devices in a mesh: seq: 64 (over y, x, z), head: 2 (over core).
Axes of the slice: x: 4, y: 4, z: 4, core: 2. Of those that a mesh axis runs over, the one named last changes fastest.
Arguments:
- query_key: bfloat16 [32768, 1024], P('seq', 'head'), may hold values from -160 to 160
- value: bfloat16 [32768, 1024], P('seq', 'head'), may hold values from -6 to 6
- attended_cotangent: bfloat16 [32768, 1024], P('seq', 'head'), may hold values from -6 to 6
- send_rows: int32 [2, 49152], P(None, 'seq'), may hold values from 0 to 511, as said below
- arrival_count: int32 [2, 4096], P(None, 'seq'), may hold values from 4 to 12, as said below
- receive_slot: int32 [2, 32768], P(None, 'seq'), may hold values from 0 to 511, as said below
Outputs:
- attended: bfloat16 [32768, 1024], P('seq', 'head')
- query_key_gradient: bfloat16 [32768, 1024], P('seq', 'head')
- value_gradient: bfloat16 [32768, 1024], P('seq', 'head')
Inputs may be any that keep to these rules, and one draw needn't show every extreme that they name: `send_rows`: for each round and destination device d, the first n slots of the block d * 12 to d * 12 + 11 name the local rows sent to d, n being d's arrival_count for this device; every local row is sent once a round; the other slots name arbitrary local rows. `arrival_count`: the counts of a device, and the counts one source sends, sum to 512 in each round; in each round every source sends exactly 12 rows to one device, and every device sends the same numbers of rows in a drawn order of destinations. `receive_slot`: for each round and device, a permutation of the 512 arriving rows, counted in order of source device and then of slot.
All inputs are finite; a program needn't handle non-finite values.
Results may differ from a plain program's by a relative error of at most 0.006.
The roundings to bfloat16 on the way count: a program that leaves them out, or rounds other values in their place, can miss the bound.
Values may be sent and summed in bfloat16 or wider, within the bound.
No kernel may reach another device: no remote copies, remote signals or barrier semaphores. Data moves between devices by JAX's collectives and lax.ppermute only.
A program may use at most 128 MiB of HBM per device.

v0:
```python
import jax
import jax.numpy as jnp
from jax import lax
from jax.sharding import PartitionSpec as P

DH = 128
GROUP = 256


NEG_SELF = -100000.0
EPS_KEY = 1e-06


def shifted(block, axis, distance):
    devices = range(lax.axis_size(axis))
    route = [((i - distance) % len(devices), i) for i in devices]
    return lax.ppermute(block, axis, route)


def unit_rows(raw_rows):
    wide_rows = raw_rows.astype(jnp.float32)
    inverse = lax.rsqrt(jnp.sum(wide_rows * wide_rows, -1, keepdims=True) + EPS_KEY)
    return (wide_rows * inverse, inverse)


def chain_back(directions, inverse, unit_slope):
    return inverse * (unit_slope - directions * jnp.sum(directions * unit_slope, -1, keepdims=True))


def send_home(first_part, second_part):
    return (
        lax.all_to_all(first_part, "seq", split_axis=1, concat_axis=1, tiled=True),
        lax.all_to_all(second_part, "seq", split_axis=1, concat_axis=1, tiled=True),
    )


def into_slots(sorted_rows, slot_of, slot_total):

    def into_place_rows(slot_index, values):
        return jnp.zeros((slot_total,) + values.shape[1:], values.dtype).at[slot_index].set(values)

    return jax.vmap(into_place_rows)(slot_of, sorted_rows)


def from_slots(arrived, send_rows, rows_dev):

    def from_place_rows(slot_index, values):
        return jnp.zeros((rows_dev,) + values.shape[1:], values.dtype).at[slot_index].add(values)

    return jax.vmap(from_place_rows)(send_rows, arrived)


def per_device(query_key, value, attended_cotangent, send_rows, arrival_count, receive_slot):
    rows_dev, row_width = query_key.shape
    head_count = row_width // DH
    rounds = send_rows.shape[0]
    owners = lax.axis_size("seq")
    slot_total = send_rows.shape[1]
    capacity = slot_total // owners
    groups = rows_dev // GROUP
    running = jnp.cumsum(arrival_count, axis=1)
    source_of = jnp.sum((running[:, None, :] <= receive_slot[:, :, None]).astype(jnp.int32), axis=2)
    start_of = jnp.take_along_axis(running - arrival_count, source_of, axis=1)
    slot_of = source_of * capacity + receive_slot - start_of

    def grouped(sorted_rows):
        return sorted_rows.reshape(groups, GROUP, head_count, DH)

    leaving = [
        jnp.take(member, send_rows, axis=0) for member in (query_key, value, attended_cotangent)
    ]
    by_round = [
        (
            lax.all_to_all(leaving[0][hash_round], "seq", split_axis=0, concat_axis=0, tiled=True),
            lax.all_to_all(leaving[1][hash_round], "seq", split_axis=0, concat_axis=0, tiled=True),
            lax.all_to_all(leaving[2][hash_round], "seq", split_axis=0, concat_axis=0, tiled=True),
        )
        for hash_round in range(rounds)
    ]
    sorted_sets = [
        [jnp.take(member, slot_of[hash_round], axis=0) for member in by_round[hash_round]]
        for hash_round in range(rounds)
    ]
    edge_query, edge_value = shifted(
        (
            jnp.stack([round_set[0][-GROUP:] for round_set in sorted_sets]),
            jnp.stack([round_set[1][-GROUP:] for round_set in sorted_sets]),
        ),
        "seq",
        1,
    )
    self_mask = jnp.eye(GROUP, dtype=bool)[None, None]
    stored = []
    outputs = []
    log_totals = []
    for hash_round in range(rounds):
        queries = grouped(sorted_sets[hash_round][0])
        values_own = grouped(sorted_sets[hash_round][1])
        directions, inverse = unit_rows(queries)
        edge_dirs, edge_inverse = unit_rows(
            edge_query[hash_round].reshape(1, GROUP, head_count, DH)
        )
        keys_own = directions.astype(jnp.bfloat16)
        keys_prior = jnp.concatenate([edge_dirs, directions[:-1]]).astype(jnp.bfloat16)
        values_prior = jnp.concatenate(
            [edge_value[hash_round].reshape(1, GROUP, head_count, DH), values_own[:-1]]
        )
        scores_own = jnp.where(
            self_mask,
            NEG_SELF,
            jnp.einsum("nqhd,nkhd->nhqk", queries, keys_own, preferred_element_type=jnp.float32),
        )
        scores_prior = jnp.einsum(
            "nqhd,nkhd->nhqk", queries, keys_prior, preferred_element_type=jnp.float32
        )
        row_top = jnp.maximum(scores_own.max(-1), scores_prior.max(-1))
        log_total = row_top + jnp.log(
            jnp.sum(jnp.exp(scores_own - row_top[..., None]), -1)
            + jnp.sum(jnp.exp(scores_prior - row_top[..., None]), -1)
        )
        weights_own = jnp.exp(scores_own - log_total[..., None]).astype(jnp.bfloat16)
        weights_prior = jnp.exp(scores_prior - log_total[..., None]).astype(jnp.bfloat16)
        partial_value = jnp.einsum(
            "nhqk,nkhd->nqhd", weights_own, values_own, preferred_element_type=jnp.float32
        ) + jnp.einsum(
            "nhqk,nkhd->nqhd", weights_prior, values_prior, preferred_element_type=jnp.float32
        )
        outputs.append(partial_value.reshape(rows_dev, row_width))
        log_totals.append(jnp.transpose(log_total, (0, 2, 1)).reshape(rows_dev, head_count))
        stored.append(
            (
                queries,
                values_own,
                values_prior,
                directions,
                inverse,
                edge_dirs,
                edge_inverse,
                keys_own,
                keys_prior,
                scores_own,
                scores_prior,
            )
        )
    round_out, round_lse = send_home(
        into_slots(jnp.stack(outputs), slot_of, slot_total),
        into_slots(jnp.stack(log_totals), slot_of, slot_total),
    )
    round_out = from_slots(round_out, send_rows, rows_dev).reshape(rounds, rows_dev, head_count, DH)
    round_lse = from_slots(round_lse, send_rows, rows_dev)
    round_top = jnp.max(round_lse, axis=0)
    total_lse = round_top + jnp.log(jnp.sum(jnp.exp(round_lse - round_top), axis=0))
    shares = jnp.exp(round_lse - total_lse)
    combined = jnp.sum(shares[..., None] * round_out, axis=0)
    attended = combined.reshape(rows_dev, row_width).astype(jnp.bfloat16)
    upstream = attended_cotangent.reshape(rows_dev, head_count, DH).astype(jnp.float32)
    delta_rows = jnp.sum(upstream * combined, -1)
    stat_lse, stat_delta = (
        lax.all_to_all(
            jnp.take(total_lse, send_rows, axis=0), "seq", split_axis=1, concat_axis=1, tiled=True
        ),
        lax.all_to_all(
            jnp.take(delta_rows, send_rows, axis=0), "seq", split_axis=1, concat_axis=1, tiled=True
        ),
    )
    query_list = []
    key_list = []
    value_list = []
    edge_keys = []
    edge_values = []
    for hash_round in range(rounds):
        (
            queries,
            values_own,
            values_prior,
            directions,
            inverse,
            edge_dirs,
            edge_inverse,
            keys_own,
            keys_prior,
            scores_own,
            scores_prior,
        ) = stored[hash_round]
        lse_sorted = (
            jnp.take(stat_lse[hash_round], slot_of[hash_round], axis=0)
            .reshape(groups, GROUP, head_count)
            .transpose(0, 2, 1)
        )
        delta_sorted = (
            jnp.take(stat_delta[hash_round], slot_of[hash_round], axis=0)
            .reshape(groups, GROUP, head_count)
            .transpose(0, 2, 1)
        )
        upstream_rows = grouped(sorted_sets[hash_round][2])
        probs_own = jnp.exp(scores_own - lse_sorted[..., None])
        probs_prior = jnp.exp(scores_prior - lse_sorted[..., None])
        value_own_slope = jnp.einsum(
            "nhqk,nqhd->nkhd",
            probs_own.astype(jnp.bfloat16),
            upstream_rows,
            preferred_element_type=jnp.float32,
        )
        value_prior_slope = jnp.einsum(
            "nhqk,nqhd->nkhd",
            probs_prior.astype(jnp.bfloat16),
            upstream_rows,
            preferred_element_type=jnp.float32,
        )
        dots_own = jnp.einsum(
            "nqhd,nkhd->nhqk", upstream_rows, values_own, preferred_element_type=jnp.float32
        )
        dots_prior = jnp.einsum(
            "nqhd,nkhd->nhqk", upstream_rows, values_prior, preferred_element_type=jnp.float32
        )
        slopes_own = (probs_own * (dots_own - delta_sorted[..., None])).astype(jnp.bfloat16)
        slopes_prior = (probs_prior * (dots_prior - delta_sorted[..., None])).astype(jnp.bfloat16)
        query_slope = jnp.einsum(
            "nhqk,nkhd->nqhd", slopes_own, keys_own, preferred_element_type=jnp.float32
        ) + jnp.einsum(
            "nhqk,nkhd->nqhd", slopes_prior, keys_prior, preferred_element_type=jnp.float32
        )
        unit_own_slope = jnp.einsum(
            "nhqk,nqhd->nkhd", slopes_own, queries, preferred_element_type=jnp.float32
        )
        unit_prior_slope = jnp.einsum(
            "nhqk,nqhd->nkhd", slopes_prior, queries, preferred_element_type=jnp.float32
        )
        key_slope = unit_own_slope + jnp.concatenate(
            [unit_prior_slope[1:], jnp.zeros_like(unit_prior_slope[:1])]
        )
        value_slope = value_own_slope + jnp.concatenate(
            [value_prior_slope[1:], jnp.zeros_like(value_prior_slope[:1])]
        )
        edge_key = unit_prior_slope[:1]
        key_slope = chain_back(directions, inverse, key_slope)
        edge_key = chain_back(edge_dirs, edge_inverse, edge_key)
        query_list.append(query_slope)
        key_list.append(key_slope)
        value_list.append(value_slope)
        edge_keys.append(edge_key)
        edge_values.append(value_prior_slope[:1])
    incoming_key, incoming_value = (
        shifted(jnp.stack(edge_keys).astype(jnp.bfloat16), "seq", -1).astype(jnp.float32),
        shifted(jnp.stack(edge_values).astype(jnp.bfloat16), "seq", -1).astype(jnp.float32),
    )
    query_grads = jnp.stack(query_list).reshape(rounds, rows_dev, row_width)
    key_grads = (
        jnp.stack(key_list).at[:, -1:].add(incoming_key).reshape(rounds, rows_dev, row_width)
    )
    value_grads = (
        jnp.stack(value_list).at[:, -1:].add(incoming_value).reshape(rounds, rows_dev, row_width)
    )
    first_grads = query_grads + key_grads
    back_first, back_value = send_home(
        into_slots(first_grads, slot_of, slot_total), into_slots(value_grads, slot_of, slot_total)
    )
    back_first = from_slots(back_first, send_rows, rows_dev)
    back_value = from_slots(back_value, send_rows, rows_dev)
    gradient = jnp.sum(back_first, axis=0)
    return (
        attended,
        gradient.astype(jnp.bfloat16),
        jnp.sum(back_value, axis=0).astype(jnp.bfloat16),
    )


def solution(mesh):
    in_specs = (
        P("seq", "head"),
        P("seq", "head"),
        P("seq", "head"),
        P(None, "seq"),
        P(None, "seq"),
        P(None, "seq"),
    )
    out_specs = (P("seq", "head"), P("seq", "head"), P("seq", "head"))
    return jax.shard_map(
        per_device, mesh=mesh, in_specs=in_specs, out_specs=out_specs, check_vma=False
    )
```

profile of v0, /device:TPU:0, one launch (start us, length us, event | category | flops | bytes accessed | tf_op | source)
XLA Modules:
  0.0 615.0 jit_solution(7333291239509566594)
XLA Ops:
  24.8 11.5 %all-to-all-start.7 = ((bf16[64,12,512]{2,1,0:T(8,128)(2,1)}), bf16[64,12,512]{2,1,0:T(8,128)(2,1)S(1)}, u32[]{:S(2)}, u32[]{:S(2)}) async-start(bf16[64,12,512]{2,1,0:T(8,128)(2,1)} %all_to_all.81), calls=%async_computation.7 | async-start | bytes 2097152 | tf_op jit(solution)/shard_map/all_to_all | solution.py:76
  38.4 16.6 %all-to-all-done.7 = bf16[64,12,512]{2,1,0:T(8,128)(2,1)S(1)} async-done(((bf16[64,12,512]{2,1,0:T(8,128)(2,1)}), bf16[64,12,512]{2,1,0:T(8,128)(2,1)S(1)}, u32[]{:S(2)}, u32[]{:S(2)}) %all-to-all-start.7) | async-done | bytes 786464 | tf_op jit(solution)/shard_map/all_to_all | solution.py:76
  62.9 14.7 %all-to-all-done.9 = bf16[64,12,512]{2,1,0:T(8,128)(2,1)} async-done(((bf16[64,12,512]{2,1,0:T(8,128)(2,1)}), bf16[64,12,512]{2,1,0:T(8,128)(2,1)}, u32[]{:S(2)}, u32[]{:S(2)}) %all-to-all-start.9) | async-done | bytes 786464 | tf_op jit(solution)/shard_map/all_to_all | solution.py:76
  83.3 9.0 %gather_fusion = s32[1024]{0:T(1024)S(1)} fusion(s32[2,64]{1,0:T(2,128)S(1)} %sub.68, s32[1024]{0:T(1024)S(1)} %bitcast.163), kind=kCustom, calls=%fused_computation.15 | custom fusion | bytes 16384 | tf_op jit(solution)/shard_map/jit(take_along_axis)/gather | solution.py:63
  99.8 9.6 %all-to-all-start.3 = ((bf16[64,12,512]{2,1,0:T(8,128)(2,1)}), bf16[64,12,512]{2,1,0:T(8,128)(2,1)S(1)}, u32[]{:S(2)}, u32[]{:S(2)}) async-start(bf16[64,12,512]{2,1,0:T(8,128)(2,1)} %all_to_all.73), calls=%async_computation.3 | async-start | bytes 2097152 | tf_op jit(solution)/shard_map/all_to_all | solution.py:75
  109.6 16.0 %all-to-all-done.3 = bf16[64,12,512]{2,1,0:T(8,128)(2,1)S(1)} async-done(((bf16[64,12,512]{2,1,0:T(8,128)(2,1)}), bf16[64,12,512]{2,1,0:T(8,128)(2,1)S(1)}, u32[]{:S(2)}, u32[]{:S(2)}) %all-to-all-start.3) | async-done | bytes 786464 | tf_op jit(solution)/shard_map/all_to_all | solution.py:75
  131.2 16.1 %all-to-all-done = bf16[64,12,512]{2,1,0:T(8,128)(2,1)} async-done(((bf16[64,12,512]{2,1,0:T(8,128)(2,1)}), bf16[64,12,512]{2,1,0:T(8,128)(2,1)}, u32[]{:S(2)}, u32[]{:S(2)}) %all-to-all-start) | async-done | bytes 786464 | tf_op jit(solution)/shard_map/all_to_all | solution.py:74
  193.9 13.7 %collective-permute-done = bf16[2,256,512]{2,1,0:T(8,128)(2,1)} collective-permute-done((bf16[2,256,512]{2,1,0:T(8,128)(2,1)}, bf16[2,256,512]{2,1,0:T(8,128)(2,1)}, u32[]{:S(2)}, u32[]{:S(2)}) %collective-permute-start) | collective-permute-done | bytes 524320 | tf_op jit(solution)/shard_map/ppermute | solution.py:17
  252.2 7.3 %scatter_custom_fusion.2 = f32[1536,512]{1,0:T(8,128)} fusion(s32[1024]{0:T(1024)S(1)} %bitcast.235, f32[1024,512]{1,0:T(8,128)} %bitcast.199, f32[]{:T(128)} %constant.118.clone.1), kind=kCustom, calls=%fused_computation.63 | custom fusion | bytes 3146240
  265.5 10.8 %all-to-all-start.5 = ((f32[2,768,512]{2,0,1:T(2,128)}), f32[2,768,512]{2,0,1:T(2,128)}, u32[]{:S(2)}, u32[]{:S(2)}) async-start(f32[2,768,512]{2,0,1:T(2,128)} %copy.555), calls=%async_computation.5 | async-start | bytes 6291456 | tf_op jit(solution)/shard_map/all_to_all | solution.py:32
  279.4 9.5 %scatter_custom_fusion.1 = f32[1024,4]{1,0:T(8,128)S(1)} fusion(s32[1536]{0:T(1024)S(1)} %reshape.615, f32[1536,4]{1,0:T(8,128)} %copy.542, f32[]{:T(128)} %constant.118.clone.1), kind=kCustom, calls=%fused_computation.181 | custom fusion | flops 6144 | bytes 16896
  299.7 13.8 %all-to-all-done.5 = f32[2,768,512]{2,0,1:T(2,128)} async-done(((f32[2,768,512]{2,0,1:T(2,128)}), f32[2,768,512]{2,0,1:T(2,128)}, u32[]{:S(2)}, u32[]{:S(2)}) %all-to-all-start.5) | async-done | bytes 3145760 | tf_op jit(solution)/shard_map/all_to_all | solution.py:32
  317.7 11.7 %scatter_custom_fusion.3 = f32[1024,512]{1,0:T(8,128)} fusion(s32[1536]{0:T(1024)} %copy-done.58, f32[1536,512]{1,0:T(8,128)} %bitcast.185, f32[]{:T(128)} %constant.118.clone.1), kind=kCustom, calls=%fused_computation.122 | custom fusion | flops 786432 | bytes 2097664
  378.3 9.4 %all-to-all-done.8 = f32[2,768,4]{2,0,1:T(2,128)} async-done(((f32[2,768,4]{2,0,1:T(2,128)}), f32[2,768,4]{2,0,1:T(2,128)}, u32[]{:S(2)}, u32[]{:S(2)}) %all-to-all-start.8) | async-done | bytes 24608 | tf_op jit(solution)/shard_map/all_to_all | solution.py:162
  436.6 12.1 %fusion.21 = f32[1,2,256,4,128]{4,2,3,1,0:T(8,128)S(1)} fusion(f32[2,256,4,128]{3,1,2,0:T(8,128)} %fusion.26, f32[2,256,4]{1,2,0:T(4,128)S(1)} %add_rsqrt_fusion, bf16[2,256,4,128]{3,2,1,0:T(4,128)(2,1)S(1)} %copy-done.14), kind=kOutput, calls=%fused_computation.75 | output fusion | flops 2099327 | bytes 2629632 | tf_op jit(solution)/shard_map/mul | solution.py:27
  448.7 10.4 %fusion.17 = f32[1,2,256,4,128]{4,2,3,1,0:T(8,128)S(1)} fusion(f32[2,256,4,128]{3,1,2,0:T(8,128)S(1)} %copy-done.32, f32[2,256,4]{1,2,0:T(4,128)S(1)} %add_rsqrt_fusion.1, bf16[2,256,4,128]{3,2,1,0:T(4,128)(2,1)S(1)} %reshape.437), kind=kOutput, calls=%fused_computation.71 | output fusion | flops 2099327 | bytes 2629632 | tf_op jit(solution)/shard_map/mul | solution.py:27
  470.2 7.4 %scatter_custom_fusion.4 = f32[1536,512]{1,0:T(8,128)} fusion(s32[1024]{0:T(1024)} %bitcast.236, f32[1024,512]{1,0:T(8,128)} %bitcast.198, f32[]{:T(128)} %constant.118.clone.1), kind=kCustom, calls=%fused_computation.61 | custom fusion | bytes 3146240
  491.7 7.3 %collective-permute-start.3 = (bf16[2,1,256,4,128]{2,4,3,1,0:T(8,128)(2,1)S(1)}, bf16[2,1,256,4,128]{2,4,3,1,0:T(8,128)(2,1)S(1)}, u32[]{:S(2)}, u32[]{:S(2)}) collective-permute-start(bf16[2,1,256,4,128]{2,4,3,1,0:T(8,128)(2,1)S(1)} %pad_maximum_fusion.10), channel_id=1, source_target_pairs={{2,0},{4,2},{6,4},{8,6},{10,8},{12,10},{14,12},{16,14},{18,16},{20... | collective-permute-start | bytes 1572872 | tf_op jit(solution)/shard_map/ppermute | solution.py:17
  500.3 35.9 %collective-permute-done.3 = bf16[2,1,256,4,128]{2,4,3,1,0:T(8,128)(2,1)S(1)} collective-permute-done((bf16[2,1,256,4,128]{2,4,3,1,0:T(8,128)(2,1)S(1)}, bf16[2,1,256,4,128]{2,4,3,1,0:T(8,128)(2,1)S(1)}, u32[]{:S(2)}, u32[]{:S(2)}) %collective-permute-start.3) | collective-permute-done | bytes 524320 | tf_op jit(solution)/shard_map/ppermute | solution.py:17
  538.1 7.8 %scatter_custom_fusion.6 = f32[1536,512]{1,0:T(8,128)} fusion(s32[1024]{0:T(1024)} %bitcast.237, f32[128,8,4,128]{3,2,1,0:T(4,128)} %bitcast.173, f32[]{:T(128)} %constant.118.clone.1), kind=kCustom, calls=%fused_computation.32 | custom fusion | bytes 5243392
  552.0 7.8 %all-to-all-start.11 = ((f32[2,768,512]{2,0,1:T(2,128)}), f32[2,768,512]{2,0,1:T(2,128)}, u32[]{:S(2)}, u32[]{:S(2)}) async-start(f32[2,768,512]{2,0,1:T(2,128)} %copy.615), calls=%async_computation.11 | async-start | bytes 6291456 | tf_op jit(solution)/shard_map/all_to_all | solution.py:33
  563.9 10.7 %scatter_custom_fusion.5 = f32[1024,512]{1,0:T(8,128)S(1)} fusion(s32[1536]{0:T(1024)} %copy-done.58, f32[1536,512]{1,0:T(8,128)} %bitcast.186, f32[]{:T(128)} %constant.118.clone.1), kind=kCustom, calls=%fused_computation.120 | custom fusion | flops 786432 | bytes 2097664
  575.8 22.7 %all-to-all-done.11 = f32[2,768,512]{2,0,1:T(2,128)} async-done(((f32[2,768,512]{2,0,1:T(2,128)}), f32[2,768,512]{2,0,1:T(2,128)}, u32[]{:S(2)}, u32[]{:S(2)}) %all-to-all-start.11) | async-done | bytes 3145760 | tf_op jit(solution)/shard_map/all_to_all | solution.py:33
  602.6 10.8 %scatter_custom_fusion.7 = f32[1024,512]{1,0:T(8,128)S(1)} fusion(s32[1536]{0:T(1024)} %copy-done.58, f32[1536,512]{1,0:T(8,128)} %bitcast.184, f32[]{:T(128)} %constant.118.clone.1), kind=kCustom, calls=%fused_computation.118 | custom fusion | flops 786432 | bytes 2097664
  (346 shorter events, 310.0 us)
Async XLA Ops:
  1.4 18.2 %copy-start.55 = (pred[2,768]{1,0:T(4,128)(4,1)}, pred[2,768]{1,0:T(4,128)(4,1)S(1)}, u32[]{:S(2)}) copy-start(pred[2,768]{1,0:T(4,128)(4,1)S(1)} %compare_and_fusion) | copy-start | bytes 4612
  24.8 30.2 %all-to-all-start.7 = ((bf16[64,12,512]{2,1,0:T(8,128)(2,1)}), bf16[64,12,512]{2,1,0:T(8,128)(2,1)S(1)}, u32[]{:S(2)}, u32[]{:S(2)}) async-start(bf16[64,12,512]{2,1,0:T(8,128)(2,1)} %all_to_all.81), calls=%async_computation.7 | async-start | bytes 2097152 | tf_op jit(solution)/shard_map/all_to_all | solution.py:76
  38.4 24.3 %copy-start.63 = (s32[2,64]{1,0:T(2,128)S(1)}, s32[2,64]{1,0:T(2,128)}, u32[]{:S(2)}) copy-start(s32[2,64]{1,0:T(2,128)} %param.22) | copy-start | bytes 1540
  55.0 22.6 %all-to-all-start.9 = ((bf16[64,12,512]{2,1,0:T(8,128)(2,1)}), bf16[64,12,512]{2,1,0:T(8,128)(2,1)}, u32[]{:S(2)}, u32[]{:S(2)}) async-start(bf16[64,12,512]{2,1,0:T(8,128)(2,1)} %all_to_all.85), calls=%async_computation.9 | async-start | bytes 2097152 | tf_op jit(solution)/shard_map/all_to_all | solution.py:76
  60.6 22.6 %copy-start.57 = (s32[2,512]{1,0:T(2,128)S(1)}, s32[2,512]{1,0:T(2,128)}, u32[]{:S(2)}) copy-start(s32[2,512]{1,0:T(2,128)} %param.23) | copy-start | bytes 12292
  77.6 22.2 %all-to-all-start.4 = ((bf16[64,12,512]{2,1,0:T(8,128)(2,1)}), bf16[64,12,512]{2,1,0:T(8,128)(2,1)}, u32[]{:S(2)}, u32[]{:S(2)}) async-start(bf16[64,12,512]{2,1,0:T(8,128)(2,1)} %all_to_all.76), calls=%async_computation.4 | async-start | bytes 2097152 | tf_op jit(solution)/shard_map/all_to_all | solution.py:75
  99.8 25.9 %all-to-all-start.3 = ((bf16[64,12,512]{2,1,0:T(8,128)(2,1)}), bf16[64,12,512]{2,1,0:T(8,128)(2,1)S(1)}, u32[]{:S(2)}, u32[]{:S(2)}) async-start(bf16[64,12,512]{2,1,0:T(8,128)(2,1)} %all_to_all.73), calls=%async_computation.3 | async-start | bytes 2097152 | tf_op jit(solution)/shard_map/all_to_all | solution.py:75
  125.7 21.7 %copy-start.33 = (bf16[64,12,512]{2,1,0:T(8,128)(2,1)}, bf16[64,12,512]{2,1,0:T(8,128)(2,1)S(1)}, u32[]{:S(2)}) copy-start(bf16[64,12,512]{2,1,0:T(8,128)(2,1)S(1)} %all-to-all-done.3) | copy-start | bytes 2359300
  125.7 21.7 %all-to-all-start = ((bf16[64,12,512]{2,1,0:T(8,128)(2,1)}), bf16[64,12,512]{2,1,0:T(8,128)(2,1)}, u32[]{:S(2)}, u32[]{:S(2)}) async-start(bf16[64,12,512]{2,1,0:T(8,128)(2,1)} %all_to_all.66), calls=%async_computation | async-start | bytes 2097152 | tf_op jit(solution)/shard_map/all_to_all | solution.py:74
  131.2 43.3 %copy-start.61 = (pred[512]{0:T(512)(128)(4,1)}, pred[512]{0:T(512)(128)(4,1)S(1)}, u32[]{:S(2)}) copy-start(pred[512]{0:T(512)(128)(4,1)S(1)} %compare_and_fusion.1) | copy-start | bytes 1540
  147.4 23.1 %all-to-all-start.1 = ((bf16[64,12,512]{2,1,0:T(8,128)(2,1)}), bf16[64,12,512]{2,1,0:T(8,128)(2,1)}, u32[]{:S(2)}, u32[]{:S(2)}) async-start(bf16[64,12,512]{2,1,0:T(8,128)(2,1)} %all_to_all.69), calls=%async_computation.1 | async-start | bytes 2097152 | tf_op jit(solution)/shard_map/all_to_all | solution.py:74
  153.1 99.1 %copy-start.64 = (s32[1,4,2,128]{3,1,2,0:T(4,128)}, s32[1,4,2,128]{3,1,2,0:T(4,128)S(1)}, u32[]{:S(2)}) copy-start(s32[1,4,2,128]{3,1,2,0:T(4,128)S(1)} %copy.652) | copy-start | bytes 12292
  176.7 36.8 %copy-start.13 = (bf16[2,256,4,128]{3,2,1,0:T(4,128)(2,1)}, bf16[2,256,4,128]{3,2,1,0:T(4,128)(2,1)S(1)}, u32[]{:S(2)}) copy-start(bf16[2,256,4,128]{3,2,1,0:T(4,128)(2,1)S(1)} %reshape.438) | copy-start | bytes 1572868
  179.1 31.4 %collective-permute-start.1 = (bf16[2,256,512]{2,1,0:T(8,128)(2,1)}, bf16[2,256,512]{2,1,0:T(8,128)(2,1)}, u32[]{:S(2)}, u32[]{:S(2)}) collective-permute-start(bf16[2,256,512]{2,1,0:T(8,128)(2,1)} %pad_maximum_fusion.6), channel_id=1, source_target_pairs={{126,0},{0,2},{2,4},{4,6},{6,8},{8,10},{10,12},{12,14},{14,16},{16... | collective-permute-start | bytes 1572872 | tf_op jit(solution)/shard_map/ppermute | solution.py:17
  181.5 26.1 %collective-permute-start = (bf16[2,256,512]{2,1,0:T(8,128)(2,1)}, bf16[2,256,512]{2,1,0:T(8,128)(2,1)}, u32[]{:S(2)}, u32[]{:S(2)}) collective-permute-start(bf16[2,256,512]{2,1,0:T(8,128)(2,1)} %pad_maximum_fusion.3), channel_id=1, source_target_pairs={{126,0},{0,2},{2,4},{4,6},{6,8},{8,10},{10,12},{12,14},{14,16},{16... | collective-permute-start | bytes 1572872 | tf_op jit(solution)/shard_map/ppermute | solution.py:17
  192.3 31.5 %copy-start.41 = (bf16[1,256,4,128]{3,1,2,0:T(8,128)(2,1)}, bf16[1,256,4,128]{3,1,2,0:T(8,128)(2,1)S(1)}, u32[]{:S(2)}) copy-start(bf16[1,256,4,128]{3,1,2,0:T(8,128)(2,1)S(1)} %slice.257) | copy-start | bytes 786436
  234.5 31.0 %all-to-all-start.2 = ((f32[2,768,4]{2,0,1:T(2,128)}), f32[2,768,4]{2,0,1:T(2,128)}, u32[]{:S(2)}, u32[]{:S(2)}) async-start(f32[2,768,4]{2,0,1:T(2,128)} %copy.540), calls=%async_computation.2 | async-start | bytes 1572864 | tf_op jit(solution)/shard_map/all_to_all | solution.py:33
  265.5 48.1 %all-to-all-start.5 = ((f32[2,768,512]{2,0,1:T(2,128)}), f32[2,768,512]{2,0,1:T(2,128)}, u32[]{:S(2)}, u32[]{:S(2)}) async-start(f32[2,768,512]{2,0,1:T(2,128)} %copy.555), calls=%async_computation.5 | async-start | bytes 6291456 | tf_op jit(solution)/shard_map/all_to_all | solution.py:32
  347.8 20.0 %all-to-all-start.6 = ((f32[2,768,4]{2,0,1:T(2,128)}), f32[2,768,4]{2,0,1:T(2,128)S(1)}, u32[]{:S(2)}, u32[]{:S(2)}) async-start(f32[2,768,4]{2,0,1:T(2,128)} %get-tuple-element.61), calls=%async_computation.6 | async-start | bytes 1572864 | tf_op jit(solution)/shard_map/all_to_all | solution.py:159
  368.8 18.9 %all-to-all-start.8 = ((f32[2,768,4]{2,0,1:T(2,128)}), f32[2,768,4]{2,0,1:T(2,128)}, u32[]{:S(2)}, u32[]{:S(2)}) async-start(f32[2,768,4]{2,0,1:T(2,128)} %get-tuple-element.62), calls=%async_computation.8 | async-start | bytes 1572864 | tf_op jit(solution)/shard_map/all_to_all | solution.py:162
  415.3 44.0 %collective-permute-start.2 = (bf16[2,1,256,4,128]{4,2,3,1,0:T(8,128)(2,1)}, bf16[2,1,256,4,128]{4,2,3,1,0:T(8,128)(2,1)}, u32[]{:S(2)}, u32[]{:S(2)}) collective-permute-start(bf16[2,1,256,4,128]{4,2,3,1,0:T(8,128)(2,1)} %pad_maximum_fusion.9), channel_id=1, source_target_pairs={{2,0},{4,2},{6,4},{8,6},{10,8},{12,10},{14,12},{16,14},{18,16},{20... | collective-permute-start | bytes 1572872 | tf_op jit(solution)/shard_map/ppermute | solution.py:17
  483.6 68.3 %all-to-all-start.10 = ((f32[2,768,512]{2,0,1:T(2,128)}), f32[2,768,512]{2,0,1:T(2,128)}, u32[]{:S(2)}, u32[]{:S(2)}) async-start(f32[2,768,512]{2,0,1:T(2,128)} %copy.604), calls=%async_computation.10 | async-start | bytes 6291456 | tf_op jit(solution)/shard_map/all_to_all | solution.py:32
  491.7 44.4 %collective-permute-start.3 = (bf16[2,1,256,4,128]{2,4,3,1,0:T(8,128)(2,1)S(1)}, bf16[2,1,256,4,128]{2,4,3,1,0:T(8,128)(2,1)S(1)}, u32[]{:S(2)}, u32[]{:S(2)}) collective-permute-start(bf16[2,1,256,4,128]{2,4,3,1,0:T(8,128)(2,1)S(1)} %pad_maximum_fusion.10), channel_id=1, source_target_pairs={{2,0},{4,2},{6,4},{8,6},{10,8},{12,10},{14,12},{16,14},{18,16},{20... | collective-permute-start | bytes 1572872 | tf_op jit(solution)/shard_map/ppermute | solution.py:17
  552.0 46.5 %all-to-all-start.11 = ((f32[2,768,512]{2,0,1:T(2,128)}), f32[2,768,512]{2,0,1:T(2,128)}, u32[]{:S(2)}, u32[]{:S(2)}) async-start(f32[2,768,512]{2,0,1:T(2,128)} %copy.615), calls=%async_computation.11 | async-start | bytes 6291456 | tf_op jit(solution)/shard_map/all_to_all | solution.py:33
  (61 other events, 266.2 us)
where the time goes:
time: 626 us; the launch traced here: 615 us
  local copies, waits for them, and re-layouts  207 us (33%)
  waiting for transfers between devices  165 us (26%)
  other arithmetic  110 us (18%)
  starting transfers between devices  98.3 us (16%)
  matrix products  31.7 us (5%)
    ppermute x4, waiting for transfers between devices, shifted(): return lax.ppermute(block, axis, route)  49.5 us
    unnamed x11, other arithmetic  43 us
    unnamed x147, local copies, waits for them, and re-layouts  32.7 us
    all_to_all x2, waiting for transfers between devices, per_device(): lax.all_to_all(leaving[2][hash_round], 'seq', split_axis=0, concat_axis=0...  31.2 us
    all_to_all x2, waiting for transfers between devices, send_home(): lax.all_to_all(second_part, 'seq', split_axis=1, concat_axis=1, tiled=True)  22.7 us
    mul x2, other arithmetic, chain_back(): directions * jnp.sum(directions * unit_slope, -1, keepdims=True)  22.5 us
    scatter x4, local copies, waits for them, and re-layouts, into_place_rows(): jnp.zeros((slot_total,) + values.shape[1:], values.dtype).at[slot_index]  20.6 us
    gather x3, local copies, waits for them, and re-layouts, per_device(): jnp.take(member, send_rows, axis=0)  17.4 us
  transfers between devices with their start and end apart: 16, of which 11 were waited for; matrix products, arithmetic and copies ran while one was open for 28% of the time, Pallas kernels for 0%

commit v1 on v0

v1 whole, which is shorter than its diff:
```python
import functools

import jax
import jax.numpy as jnp
from jax import lax
from jax.experimental import pallas as pl
from jax.experimental.pallas import tpu as pltpu
from jax.sharding import PartitionSpec as P

DH = 128
GROUP = 256
NEG_SELF = -100000.0
EPS_KEY = 1e-06
LANES = 128
STAT = 8
PIECES = 3
MIB = 1 << 20


def dot(left, right, left_axis=1, right_axis=0):
    return lax.dot_general(
        left,
        right,
        (((left_axis,), (right_axis,)), ((), ())),
        preferred_element_type=jnp.float32,
    )


def params(mib=40):
    return pltpu.CompilerParams(vmem_limit_bytes=mib * MIB)


def cost(flops, moved, exps=0):
    return pl.CostEstimate(flops=int(flops), bytes_accessed=int(moved), transcendentals=int(exps))


def shifted(block, axis, distance):
    devices = range(lax.axis_size(axis))
    route = [((i - distance) % len(devices), i) for i in devices]
    return lax.ppermute(block, axis, route)


def exchange(block):
    return lax.all_to_all(block, "seq", split_axis=0, concat_axis=0, tiled=True)


def match(left, right):
    return jnp.where(left == right, 1.0, 0.0).astype(jnp.bfloat16)


def iota(shape, axis):
    return lax.broadcasted_iota(jnp.int32, shape, axis)


def pieces_of(wide):
    first = wide.astype(jnp.bfloat16)
    rest = wide - first.astype(jnp.float32)
    second = rest.astype(jnp.bfloat16)
    third = (rest - second.astype(jnp.float32)).astype(jnp.bfloat16)
    return first, second, third


def unit_rows(raw_rows):
    wide = raw_rows.astype(jnp.float32)
    inverse = lax.rsqrt(jnp.sum(wide * wide, -1, keepdims=True) + EPS_KEY)
    return wide * inverse, inverse


def pack_body(index_ref, *refs):
    sources, out_ref = refs[:-1], refs[-1]
    tokens, width = sources[0].shape
    chosen = match(index_ref[...], iota((out_ref.shape[0], tokens), 1))
    for place, source in enumerate(sources):
        out_ref[:, place * width : (place + 1) * width] = dot(chosen, source[...]).astype(
            jnp.bfloat16
        )


def pack(index_col, *sources):
    slots = index_col.shape[0]
    tokens, width = sources[0].shape
    block = slots // 6
    total = width * len(sources)
    return pl.pallas_call(
        pack_body,
        grid=(6,),
        in_specs=[pl.BlockSpec((block, 1), lambda i: (i, 0))]
        + [pl.BlockSpec((tokens, width), lambda i: (0, 0)) for _ in sources],
        out_specs=pl.BlockSpec((block, total), lambda i: (i, 0)),
        out_shape=jax.ShapeDtypeStruct((slots, total), jnp.bfloat16),
        compiler_params=params(),
        cost_estimate=cost(2 * slots * tokens * total, 2 * (slots + tokens) * total),
        name="pack_rows",
    )(index_col, *sources)


def sort_body(place_col_ref, arrival_row_ref, arrived_ref, sorted_ref, tail_ref, head_ref, chosen):
    step = pl.program_id(0)

    @pl.when(step == 0)
    def _():
        chosen[...] = match(place_col_ref[...], arrival_row_ref[...])

    rows = dot(chosen[...], arrived_ref[...]).astype(jnp.bfloat16)
    sorted_ref[...] = rows
    half = rows.shape[0] // 2
    tail_ref[:GROUP, :] = rows[half - GROUP : half]
    tail_ref[GROUP:, :] = rows[2 * half - GROUP :]

    @pl.when(step < 2)
    def _():
        head_ref[:GROUP, :] = rows[:GROUP]
        head_ref[GROUP:, :] = rows[half : half + GROUP]


def sort_rows(place_col, arrival_row, arrived):
    slots, width = arrived.shape
    rows = place_col.shape[0]
    wide = width // 4
    return pl.pallas_call(
        sort_body,
        grid=(4,),
        in_specs=[
            pl.BlockSpec((rows, 1), lambda i: (0, 0)),
            pl.BlockSpec((1, slots), lambda i: (0, 0)),
            pl.BlockSpec((slots, wide), lambda i: (0, i)),
        ],
        out_specs=[
            pl.BlockSpec((rows, wide), lambda i: (0, i)),
            pl.BlockSpec((2 * GROUP, wide), lambda i: (0, i)),
            pl.BlockSpec((2 * GROUP, wide), lambda i: (0, jnp.minimum(i, 1))),
        ],
        out_shape=[
            jax.ShapeDtypeStruct((rows, width), jnp.bfloat16),
            jax.ShapeDtypeStruct((2 * GROUP, width), jnp.bfloat16),
            jax.ShapeDtypeStruct((2 * GROUP, width // 2), jnp.bfloat16),
        ],
        scratch_shapes=[pltpu.VMEM((rows, slots), jnp.bfloat16)],
        compiler_params=params(),
        cost_estimate=cost(2 * slots * rows * width, 2 * (slots + 2 * rows) * width),
        name="sort_rows",
    )(place_col, arrival_row, arrived)


def forward_tile(query, keys, values):
    scores = dot(query, keys, 1, 1)
    own = iota((GROUP, 2 * GROUP), 1) == iota((GROUP, 2 * GROUP), 0) + GROUP
    scores = jnp.where(own, NEG_SELF, scores)
    top = jnp.max(scores, -1, keepdims=True)
    raised = jnp.exp(scores - top)
    total = jnp.sum(raised, -1, keepdims=True)
    weights = (raised * (1.0 / total)).astype(jnp.bfloat16)
    return dot(weights, values), top + jnp.log(total)


def forward_body(with_edge, *refs):
    if with_edge:
        query_ref, value_ref, tail_query_ref, tail_value_ref, out_ref, lse_ref = refs
    else:
        query_ref, value_ref, out_ref, lse_ref = refs
    pair = pl.program_id(1)
    lane = iota((GROUP, LANES), 1) % STAT

    for local in range(2):
        columns = slice(local * DH, (local + 1) * DH)
        if with_edge:
            raw = jnp.concatenate([tail_query_ref[:, columns], query_ref[:GROUP, columns]])
            values = jnp.concatenate([tail_value_ref[:, columns], value_ref[:GROUP, columns]])
            query = query_ref[:GROUP, columns]
        else:
            raw = query_ref[:, columns]
            values = value_ref[:, columns]
            query = query_ref[GROUP:, columns]
        keys = unit_rows(raw)[0].astype(jnp.bfloat16)
        partial, lse = forward_tile(query, keys, values)
        out_ref[:, columns] = partial
        at_head = lane == pair * 2 + local
        if local == 0:
            before = jnp.where(pair == 0, jnp.zeros((GROUP, LANES), jnp.float32), lse_ref[...])
        else:
            before = lse_ref[...]
        lse_ref[...] = jnp.where(at_head, lse, before)


def forward(rows_sorted, tail=None):
    with_edge = tail is not None
    rows, width = rows_sorted.shape
    per_round = rows // 2
    wide = 2 * DH
    in_specs = [
        pl.BlockSpec((per_round, wide), lambda r, p: (r, p)),
        pl.BlockSpec((per_round, wide), lambda r, p: (r, p + 2)),
    ]
    arguments = [rows_sorted, rows_sorted]
    if with_edge:
        in_specs += [
            pl.BlockSpec((GROUP, wide), lambda r, p: (r, p)),
            pl.BlockSpec((GROUP, wide), lambda r, p: (r, p + 2)),
        ]
        arguments += [tail, tail]
    return pl.pallas_call(
        functools.partial(forward_body, with_edge),
        grid=(2, 2),
        in_specs=in_specs,
        out_specs=[
            pl.BlockSpec((GROUP, wide), lambda r, p: (r, p)),
            pl.BlockSpec((GROUP, LANES), lambda r, p: (r, 0)),
        ],
        out_shape=[
            jax.ShapeDtypeStruct((2 * GROUP, width // 2), jnp.float32),
            jax.ShapeDtypeStruct((2 * GROUP, LANES), jnp.float32),
        ],
        compiler_params=params(),
        cost_estimate=cost(8 * 4 * GROUP * 2 * GROUP * DH, 4 * rows * width, 8 * GROUP * 512),
        name="forward_edge" if with_edge else "forward_own",
    )(*arguments)


def stats_body(
    place_col_ref,
    place_row_ref,
    arrival_row_ref,
    arrival_col_ref,
    arrived_ref,
    out_first_ref,
    out_second_ref,
    lse_first_ref,
    lse_second_ref,
    sorted_ref,
    head_ref,
    stats_ref,
):
    rows = place_col_ref.shape[0]
    per_round = rows // 2
    chosen = match(place_col_ref[...], arrival_row_ref[...])
    cotangent = dot(chosen, arrived_ref[...]).astype(jnp.bfloat16)
    sorted_ref[...] = cotangent
    lane = iota((GROUP, LANES), 1)
    parts = []
    for hash_round in range(2):
        kept = slice(hash_round * GROUP, (hash_round + 1) * GROUP)
        head_ref[kept, :] = cotangent[hash_round * per_round : hash_round * per_round + GROUP]
        for group, (out_ref, lse_ref) in enumerate(
            ((out_first_ref, lse_first_ref), (out_second_ref, lse_second_ref))
        ):
            start = hash_round * per_round + group * GROUP
            wide = cotangent[start : start + GROUP].astype(jnp.float32)
            product = wide * out_ref[kept, :]
            stat = lse_ref[kept, :]
            for head in range(4):
                own = jnp.sum(product[:, head * DH : (head + 1) * DH], -1, keepdims=True)
                stat = jnp.where(lane % STAT == 4 + head, own, stat)
            first, second, third = pieces_of(stat)
            piece = lane // (PIECES * STAT)
            parts.append(
                jnp.where(
                    piece == 0,
                    first.astype(jnp.float32),
                    jnp.where(
                        piece == 1,
                        second.astype(jnp.float32),
                        jnp.where(piece == 2, third.astype(jnp.float32), 0.0),
                    ),
                ).astype(jnp.bfloat16)
            )
    stats = jnp.concatenate(parts)
    third_slots = arrival_col_ref.shape[0] // 3
    lane_third = (iota((third_slots, LANES), 1) % (3 * STAT)) // STAT
    result = jnp.zeros((third_slots, LANES), jnp.float32)
    for third in range(3):
        back = match(
            arrival_col_ref[third * third_slots : (third + 1) * third_slots], place_row_ref[...]
        )
        result = jnp.where(lane_third == third, dot(back, stats), result)
    stats_ref[...] = result


def stats_out(place_col, place_row, arrival_row, arrival_col3, arrived, outs, lses):
    slots, width = arrived.shape
    rows = place_col.shape[0]
    return pl.pallas_call(
        stats_body,
        out_shape=[
            jax.ShapeDtypeStruct((rows, width), jnp.bfloat16),
            jax.ShapeDtypeStruct((2 * GROUP, width), jnp.bfloat16),
            jax.ShapeDtypeStruct((slots // 3, LANES), jnp.float32),
        ],
        compiler_params=params(),
        cost_estimate=cost(2 * slots * rows * (width + LANES), 4 * slots * width),
        name="cotangent_and_stats",
    )(place_col, place_row, arrival_row, arrival_col3, arrived, *outs, *lses)


def gather_stats(codes_row, per_slot_codes, stats):
    third_slots = stats.shape[0]
    narrow = stats.astype(jnp.bfloat16)
    total = None
    for third in range(3):
        chosen = match(per_slot_codes[third * third_slots : (third + 1) * third_slots], codes_row)
        found = dot(narrow, chosen, 0, 0)
        for piece in range(PIECES):
            at = piece * PIECES * STAT + third * STAT
            part = found[at : at + STAT]
            total = part if total is None else total + part
    return total


def total_body(tokens, slot_code_ref, arrived_ref, out_ref):
    slots = slot_code_ref.shape[0]
    found = gather_stats(iota((1, 2 * tokens), 1), slot_code_ref[...], arrived_ref[...])
    lse_first, lse_second = found[:4, :tokens], found[:4, tokens:]
    delta_first, delta_second = found[4:, :tokens], found[4:, tokens:]
    top = jnp.maximum(lse_first, lse_second)
    total = top + jnp.log(jnp.exp(lse_first - top) + jnp.exp(lse_second - top))
    delta = delta_first * jnp.exp(lse_first - total) + delta_second * jnp.exp(lse_second - total)
    stat = jnp.concatenate([total, delta])
    first, second, third_piece = [member.astype(jnp.float32) for member in pieces_of(stat)]
    spare = jnp.zeros((LANES - 9 * STAT, tokens), jnp.float32)
    table = jnp.concatenate(
        [first] * 3 + [second] * 3 + [third_piece] * 3 + [spare]
    ).astype(jnp.bfloat16)
    third_slots = slots // 3
    lane_third = (iota((third_slots, LANES), 1) % (3 * STAT)) // STAT
    result = jnp.zeros((third_slots, LANES), jnp.float32)
    for third in range(3):
        code = slot_code_ref[third * third_slots : (third + 1) * third_slots]
        row = jnp.where(code >= tokens, code - tokens, code)
        chosen = match(row, iota((third_slots, tokens), 1))
        result = jnp.where(lane_third == third, dot(chosen, table, 1, 1), result)
    owners = third_slots // STAT
    by_owner = result.reshape(owners, STAT, LANES)
    out_ref[:, :STAT, :] = by_owner
    out_ref[: owners - 1, STAT:, :] = by_owner[1:]
    out_ref[owners - 1 :, STAT:, :] = by_owner[:1]


def total_stats(slot_code, arrived, tokens):
    owners = arrived.shape[0] // STAT
    return pl.pallas_call(
        functools.partial(total_body, tokens),
        out_shape=jax.ShapeDtypeStruct((owners, 2 * STAT, LANES), jnp.float32),
        compiler_params=params(),
        cost_estimate=cost(2 * 1536 * 1536 * LANES, 1 << 20),
        name="total_stats",
    )(slot_code, arrived)


def backward_tile(query, upstream, keys, values, masked, total_row, delta_row):
    scores = dot(keys, query, 1, 1)
    if masked is not None:
        scores = jnp.where(masked, NEG_SELF, scores)
    probs = jnp.exp(scores - total_row)
    dots = dot(values, upstream, 1, 1)
    slopes = (probs * (dots - delta_row)).astype(jnp.bfloat16)
    return probs.astype(jnp.bfloat16), slopes


def backward_body(
    place_row_ref,
    next_row_ref,
    arrival_col_ref,
    arrival_col3_ref,
    next_col3_ref,
    stats_ref,
    query_ref,
    value_ref,
    cotangent_ref,
    tail_query_ref,
    tail_value_ref,
    next_query_ref,
    next_cotangent_ref,
    out_first_ref,
    out_second_ref,
    lse_first_ref,
    lse_second_ref,
    payload_ref,
    back,
    totals,
    next_totals,
    total_cols,
    shaped,
):
    pair = pl.program_id(0)
    hash_round = pl.program_id(1)
    rows = place_row_ref.shape[1]
    per_round = rows // 2

    @pl.when((pair == 0) & (hash_round == 0))
    def _():
        back[...] = match(arrival_col_ref[...], place_row_ref[...])
        own_stats = stats_ref[:, :STAT, :].reshape(-1, LANES)
        next_stats = stats_ref[:, STAT:, :].reshape(-1, LANES)
        found = gather_stats(place_row_ref[...], arrival_col3_ref[...], own_stats)
        edge = gather_stats(next_row_ref[...], next_col3_ref[...], next_stats)
        for each in range(2):
            totals[each] = found[:, each * per_round : (each + 1) * per_round]
            next_totals[each] = edge[:, each * GROUP : (each + 1) * GROUP]
        padded = jnp.concatenate([found, jnp.zeros((LANES - STAT, rows), jnp.float32)])
        total_cols[...] = padded.T.reshape(2, per_round, LANES)

    own = iota((2 * GROUP, GROUP), 0) == iota((2 * GROUP, GROUP), 1) + GROUP
    stat = totals[hash_round]
    edge_stat = next_totals[hash_round]
    columns_of_stat = total_cols[hash_round]
    sublane = iota((STAT, 1), 0)
    lane = iota((1, LANES), 1)

    def row_of(table, index):
        return jnp.sum(jnp.where(sublane == index, table, 0.0), 0, keepdims=True)

    def col_of(table, index):
        return jnp.sum(jnp.where(lane == index, table, 0.0), 1, keepdims=True)

    for local in range(2):
        columns = slice(local * DH, (local + 1) * DH)
        head = pair * 2 + local
        total_row, delta_row = row_of(stat, head), row_of(stat, head + 4)
        edge_total, edge_delta = row_of(edge_stat, head), row_of(edge_stat, head + 4)
        raw = query_ref[:, columns]
        values = value_ref[:, columns]
        upstream = cotangent_ref[:, columns]
        units, inverse = unit_rows(raw)
        keys = units.astype(jnp.bfloat16)
        tail_keys = unit_rows(tail_query_ref[:, columns])[0].astype(jnp.bfloat16)

        keys_first = jnp.concatenate([tail_keys, keys[:GROUP]])
        values_first = jnp.concatenate([tail_value_ref[:, columns], values[:GROUP]])
        probs, slopes = backward_tile(
            raw[:GROUP],
            upstream[:GROUP],
            keys_first,
            values_first,
            own,
            total_row[:, :GROUP],
            delta_row[:, :GROUP],
        )
        query_first = dot(slopes, keys_first, 0, 0)
        unit_first = dot(slopes[GROUP:], raw[:GROUP])
        value_first = dot(probs[GROUP:], upstream[:GROUP])

        probs, slopes = backward_tile(
            raw[GROUP:],
            upstream[GROUP:],
            keys,
            values,
            own,
            total_row[:, GROUP:],
            delta_row[:, GROUP:],
        )
        query_second = dot(slopes, keys, 0, 0)
        unit_both = dot(slopes, raw[GROUP:])
        value_both = dot(probs, upstream[GROUP:])

        next_query = next_query_ref[:, columns]
        next_upstream = next_cotangent_ref[:, columns]
        probs, slopes = backward_tile(
            next_query,
            next_upstream,
            keys[GROUP:],
            values[GROUP:],
            None,
            edge_total,
            edge_delta,
        )
        unit_last = dot(slopes, next_query)
        value_last = dot(probs, next_upstream)

        for group, (query_slope, unit_slope, value_slope, out_ref, lse_ref) in enumerate(
            (
                (
                    query_first,
                    unit_first + unit_both[:GROUP],
                    value_first + value_both[:GROUP],
                    out_first_ref,
                    lse_first_ref,
                ),
                (
                    query_second,
                    unit_both[GROUP:] + unit_last,
                    value_both[GROUP:] + value_last,
                    out_second_ref,
                    lse_second_ref,
                ),
            )
        ):
            kept = slice(group * GROUP, (group + 1) * GROUP)
            unit = units[kept]
            key_slope = inverse[kept] * (
                unit_slope - unit * jnp.sum(unit * unit_slope, -1, keepdims=True)
            )
            share = jnp.exp(col_of(lse_ref[...] - columns_of_stat[kept], head))
            wide = 2 * DH
            shaped[kept, columns] = (out_ref[:, columns] * share).astype(jnp.bfloat16)
            shaped[kept, wide + local * DH : wide + (local + 1) * DH] = (
                query_slope + key_slope
            ).astype(jnp.bfloat16)
            shaped[kept, 2 * wide + local * DH : 2 * wide + (local + 1) * DH] = (
                value_slope.astype(jnp.bfloat16)
            )

    @pl.when(hash_round == 0)
    def _():
        payload_ref[...] = dot(back[:, :per_round], shaped[...]).astype(jnp.bfloat16)

    @pl.when(hash_round == 1)
    def _():
        payload_ref[...] += dot(back[:, per_round:], shaped[...]).astype(jnp.bfloat16)


def backward(index, stats, rows_sorted, cotangent, tail, next_query, next_cotangent, outs, lses):
    rows, width = rows_sorted.shape
    per_round = rows // 2
    slots = index["arrival_col"].shape[0]
    wide = 2 * DH

    def whole(array):
        return pl.BlockSpec(array.shape, lambda p, r: (0,) * array.ndim)

    small = [
        index["place_row"],
        index["next_row"],
        index["arrival_col"],
        index["arrival_col3"],
        index["next_col3"],
        stats,
    ]
    group_spec = pl.BlockSpec((GROUP, wide), lambda p, r: (r, p))
    lse_spec = pl.BlockSpec((GROUP, LANES), lambda p, r: (r, 0))
    return pl.pallas_call(
        backward_body,
        grid=(2, 2),
        in_specs=[whole(array) for array in small]
        + [
            pl.BlockSpec((per_round, wide), lambda p, r: (r, p)),
            pl.BlockSpec((per_round, wide), lambda p, r: (r, p + 2)),
            pl.BlockSpec((per_round, wide), lambda p, r: (r, p)),
            group_spec,
            pl.BlockSpec((GROUP, wide), lambda p, r: (r, p + 2)),
            group_spec,
            group_spec,
            group_spec,
            group_spec,
            lse_spec,
            lse_spec,
        ],
        out_specs=pl.BlockSpec((slots, 3 * wide), lambda p, r: (0, p)),
        out_shape=jax.ShapeDtypeStruct((slots, 6 * wide), jnp.bfloat16),
        scratch_shapes=[
            pltpu.VMEM((slots, rows), jnp.bfloat16),
            pltpu.VMEM((2, STAT, per_round), jnp.float32),
            pltpu.VMEM((2, STAT, GROUP), jnp.float32),
            pltpu.VMEM((2, per_round, LANES), jnp.float32),
            pltpu.VMEM((per_round, 3 * wide), jnp.bfloat16),
        ],
        compiler_params=params(),
        cost_estimate=cost(8e9, 1.5e7, 3e6),
        name="backward",
    )(
        *small,
        rows_sorted,
        rows_sorted,
        cotangent,
        tail,
        tail,
        next_query,
        next_cotangent,
        *outs,
        *lses,
    )


def combine_body(index_row_ref, arrived_ref, *out_refs):
    tokens, wide = out_refs[0].shape
    chosen = match(iota((tokens, 1), 0), index_row_ref[...])
    found = dot(chosen, arrived_ref[...])
    for place, out_ref in enumerate(out_refs):
        out_ref[...] = found[:, place * wide : (place + 1) * wide].astype(jnp.bfloat16)


def combine(index_row, arrived, tokens):
    slots, width = arrived.shape
    wide = width // 6
    return pl.pallas_call(
        combine_body,
        grid=(2,),
        in_specs=[
            pl.BlockSpec((1, slots), lambda i: (0, 0)),
            pl.BlockSpec((slots, 3 * wide), lambda i: (0, i)),
        ],
        out_specs=[pl.BlockSpec((tokens, wide), lambda i: (0, i))] * 3,
        out_shape=[jax.ShapeDtypeStruct((tokens, 2 * wide), jnp.bfloat16)] * 3,
        compiler_params=params(),
        cost_estimate=cost(2 * slots * tokens * width, 2 * (slots + tokens) * width),
        name="combine_rows",
    )(index_row, arrived)


def per_device(query_key, value, attended_cotangent, send_rows, arrival_count, receive_slot):
    tokens, row_width = query_key.shape
    rounds = send_rows.shape[0]
    owners = lax.axis_size("seq")
    capacity = send_rows.shape[1] // owners
    per_owner = rounds * capacity
    slots = owners * per_owner

    code = (tokens * jnp.arange(rounds, dtype=jnp.int32))[:, None]

    def by_owner(table):
        return table.reshape(rounds, owners, capacity).transpose(1, 0, 2).reshape(owners, per_owner)

    def by_third(table):
        return table.reshape(owners, 3, STAT).transpose(1, 0, 2).reshape(slots, 1)

    send = by_owner(send_rows)
    send_code = by_owner(send_rows + code)
    running = jnp.cumsum(arrival_count, axis=1)
    within = jnp.arange(capacity, dtype=jnp.int32)
    arrival = (running - arrival_count + code)[:, :, None] + within
    arrival = by_owner(jnp.where(within < arrival_count[:, :, None], arrival, -1))
    place = receive_slot + code
    next_arrival = shifted(arrival, "seq", -1)
    next_place = shifted(place[:, :GROUP], "seq", -1)

    index = {
        "place_row": place.reshape(1, -1),
        "place_col": place.reshape(-1, 1),
        "arrival_row": arrival.reshape(1, slots),
        "arrival_col": arrival.reshape(slots, 1),
        "arrival_col3": by_third(arrival),
        "next_row": next_place.reshape(1, -1),
        "next_col3": by_third(next_arrival),
    }

    def sent(packed):
        return exchange(packed.reshape(owners, per_owner, -1)).reshape(slots, -1)

    send_col = send.reshape(slots, 1)
    arrived = sent(pack(send_col, query_key, value))
    rows_sorted, tail, head_query = sort_rows(index["place_col"], index["arrival_row"], arrived)
    arrived_cotangent = sent(pack(send_col, attended_cotangent))
    prior_tail = shifted(tail, "seq", 1)
    next_query = shifted(head_query, "seq", -1)
    out_second, lse_second = forward(rows_sorted)
    out_first, lse_first = forward(rows_sorted, prior_tail)
    outs, lses = (out_first, out_second), (lse_first, lse_second)
    cotangent, head_cotangent, stats = stats_out(
        index["place_col"],
        index["place_row"],
        index["arrival_row"],
        index["arrival_col3"],
        arrived_cotangent,
        outs,
        lses,
    )
    next_cotangent = shifted(head_cotangent, "seq", -1)
    home_stats = exchange(stats.reshape(owners, STAT, LANES)).reshape(-1, LANES)
    totals = exchange(total_stats(by_third(send_code), home_stats, tokens))
    payload = backward(
        index,
        totals,
        rows_sorted,
        cotangent,
        prior_tail,
        next_query,
        next_cotangent,
        outs,
        lses,
    )
    return tuple(combine(send.reshape(1, slots), sent(payload), tokens))


def solution(mesh):
    in_specs = (
        P("seq", "head"),
        P("seq", "head"),
        P("seq", "head"),
        P(None, "seq"),
        P(None, "seq"),
        P(None, "seq"),
    )
    out_specs = (P("seq", "head"), P("seq", "head"), P("seq", "head"))
    return jax.shard_map(
        per_device, mesh=mesh, in_specs=in_specs, out_specs=out_specs, check_vma=False
    )
```

time: 626 us -> 287 us (0.46); the launches traced: 615 us -> 283 us
  local copies, waits for them, and re-layouts: 207 us -> 47.6 us
  other arithmetic: 110 us -> 2.23 us
  Pallas kernels: 0 us -> 51 us
  waiting for transfers between devices: 165 us -> 122 us
  starting transfers between devices: 98.3 us -> 59.1 us
  matrix products: 31.7 us -> 0 us
    gather x17 -> x0, local copies, waits for them, and re-layouts: 55.1 us -> none  [the longest x3 17.4 us: per_device(): jnp.take(member, send_rows, axis=0)]
    pallas_call x0 -> x9, Pallas kernels: none -> 51 us  [the longest x1 18.1 us: backward(): pl.pallas_call(backward_body, grid=(2, 2), in_specs=[whole(array) for arr...]
    all_to_all x12 -> x5, starting transfers between devices: 85.4 us -> 41.3 us  [exchange(): return lax.all_to_all(block, 'seq', split_axis=0, concat_axis=0, tiled=True)]
    unnamed x11 -> x1, other arithmetic: 43 us -> 0.07 us
    dot_general x24 -> x0, matrix products: 31.7 us -> none  [the longest x2 5.49 us: per_device(): jnp.einsum('nqhd,nkhd->nhqk', upstream_rows, values_prior, preferred_elem...]
    all_to_all x17 -> x0, local copies, waits for them, and re-layouts: 31.4 us -> none  [the longest x2 8.3 us: send_home(): lax.all_to_all(first_part, 'seq', split_axis=1, concat_axis=1, tiled=True)]
    all_to_all x12 -> x5, waiting for transfers between devices: 116 us -> 89.5 us  [exchange(): return lax.all_to_all(block, 'seq', split_axis=0, concat_axis=0, tiled=True)]
    mul x3 -> x1, other arithmetic: 23.8 us -> 0.01 us  [per_device(): code = (tokens * jnp.arange(rounds, dtype=jnp.int32))[:, None]]
  transfers between devices with their start and end apart: 16 -> 10, of which waited for: 11 -> 4; matrix products, arithmetic and copies ran while one was open for 28% -> 6% of each run, Pallas kernels for 0% -> 7%
where the time goes in v1:
time: 287 us; the launch traced here: 283 us
  waiting for transfers between devices  122 us (43%)
  starting transfers between devices  59.1 us (21%)
  Pallas kernels  51 us (18%)
  local copies, waits for them, and re-layouts  47.6 us (17%)
    all_to_all x5, waiting for transfers between devices, exchange(): return lax.all_to_all(block, 'seq', split_axis=0, concat_axis=0, tiled=True)  89.5 us
    all_to_all x5, starting transfers between devices, exchange(): return lax.all_to_all(block, 'seq', split_axis=0, concat_axis=0, tiled=True)  41.3 us
    unnamed x77, local copies, waits for them, and re-layouts  33.6 us
    ppermute x5, waiting for transfers between devices, shifted(): return lax.ppermute(block, axis, route)  32.7 us
    pallas_call x1, Pallas kernels, backward(): pl.pallas_call(backward_body, grid=(2, 2), in_specs=[whole(array) for arr...  18.1 us
    ppermute x5, starting transfers between devices, shifted(): return lax.ppermute(block, axis, route)  17.8 us
    pallas_call x2, Pallas kernels, forward(): pl.pallas_call(functools.partial(forward_body, with_edge), grid=(2, 2), i...  9.74 us
    pallas_call x1, Pallas kernels, sort_rows(): pl.pallas_call(sort_body, grid=(4,), in_specs=[pl.BlockSpec((rows, 1), la...  6.09 us
  transfers between devices with their start and end apart: 10, of which 4 were waited for; matrix products, arithmetic and copies ran while one was open for 6% of the time, Pallas kernels for 7%

profile of v1, /device:TPU:0, one launch (start us, length us, event | category | flops | bytes accessed | tf_op | source)
XLA Modules:
  0.0 283.0 jit_solution(7206698072287036268)
XLA Ops:
  3.9 2.9 %pack_rows.3 = bf16[1536,1024]{1,0:T(8,128)(2,1)S(1)} custom-call(s32[1536,1]{1,0:T(8,128)S(1)} %reshape_reshape.15.index_ref, bf16[512,512]{1,0:T(8,128)(2,1)S(1)} %copy-done.20, bf16[512,512]{1,0:T(8,128)(2,1)S(1)} %copy-done.21), custom_call_target="tpu_custom_call" | custom-call | flops 1610612736 | bytes 4194304 | tf_op jit(solution)/shard_map/pack_rows/pallas_call | solution.py:84
  6.9 1.6 copy-done.2
  8.5 11.6 %all-to-all-start.1 = ((bf16[64,24,1024]{2,1,0:T(8,128)(2,1)}), bf16[64,24,1024]{2,1,0:T(8,128)(2,1)S(1)}, u32[]{:S(2)}, u32[]{:S(2)}) async-start(bf16[64,24,1024]{2,1,0:T(8,128)(2,1)} %bitcast.41), calls=%async_computation.1 | async-start | bytes 6291456 | tf_op jit(solution)/shard_map/all_to_all | solution.py:44
  23.2 2.1 pack_rows.2
  26.4 34.2 %all-to-all-done.1 = bf16[64,24,1024]{2,1,0:T(8,128)(2,1)S(1)} async-done(((bf16[64,24,1024]{2,1,0:T(8,128)(2,1)}), bf16[64,24,1024]{2,1,0:T(8,128)(2,1)S(1)}, u32[]{:S(2)}, u32[]{:S(2)}) %all-to-all-start.1) | async-done | bytes 3145760 | tf_op jit(solution)/shard_map/all_to_all | solution.py:44
  60.6 9.1 %all-to-all-start = ((bf16[64,24,512]{2,1,0:T(8,128)(2,1)}), bf16[64,24,512]{2,1,0:T(8,128)(2,1)}, u32[]{:S(2)}, u32[]{:S(2)}) async-start(bf16[64,24,512]{2,1,0:T(8,128)(2,1)} %bitcast.42), calls=%async_computation | async-start | bytes 3145728 | tf_op jit(solution)/shard_map/all_to_all | solution.py:44
  71.2 1.9 copy-done.1
  74.1 6.1 %sort_rows.1 = (bf16[1024,1024]{1,0:T(8,128)(2,1)S(1)}, bf16[512,1024]{1,0:T(8,128)(2,1)}, bf16[512,512]{1,0:T(8,128)(2,1)S(1)}) custom-call(s32[1024,1]{1,0:T(8,128)S(1)} %bitcast.43, s32[1,1536]{1,0:T(1,128)S(1)} %select_n.35.arrival_row_ref, bf16[1536,1024]{1,0:T(8,128)(2,1)S(1)} %bitcast.40), custom_call_target="tpu_custom_call" | custom-call | flops 3221225472 | bytes 7340032 | tf_op jit(solution)/shard_map/sort_rows/pallas_call | solution.py:120
  81.0 1.5 collective-permute-start.2
  84.5 4.8 %forward_own.1 = (f32[512,512]{1,0:T(8,128)S(1)}, f32[512,128]{1,0:T(8,128)S(1)}) custom-call(bf16[1024,1024]{1,0:T(8,128)(2,1)S(1)} %get-tuple-element.13.refs_0_.refs_1_.query_ref.value_ref, bf16[1024,1024]{1,0:T(8,128)(2,1)S(1)} %get-tuple-element.13.refs_0_.refs_1_.query_ref.value_ref), custom_call_target="tpu_custom_call" | custom-call | flops 536870912 | bytes 4194304 | tf_op jit(solution)/shard_map/forward_own/pallas_call | solution.py:201
  90.2 23.9 %collective-permute-done.2.refs_2_.refs_3_.tail_query_ref.tail_value_ref = bf16[512,1024]{1,0:T(8,128)(2,1)S(1)} collective-permute-done((bf16[512,1024]{1,0:T(8,128)(2,1)}, bf16[512,1024]{1,0:T(8,128)(2,1)S(1)}, u32[]{:S(2)}, u32[]{:S(2)}) %collective-permute-start.2) | collective-permute-done | bytes 1048608 | tf_op jit(solution)/shard_map/ppermute | solution.py:40
  114.2 5.0 %forward_edge.1 = (f32[512,512]{1,0:T(8,128)S(1)}, f32[512,128]{1,0:T(8,128)S(1)}) custom-call(bf16[1024,1024]{1,0:T(8,128)(2,1)S(1)} %get-tuple-element.13.refs_0_.refs_1_.query_ref.value_ref, bf16[1024,1024]{1,0:T(8,128)(2,1)S(1)} %get-tuple-element.13.refs_0_.refs_1_.query_ref.value_ref, ...), custom_call_target="tpu_custom_call" | custom-call | flops 536870912 | bytes 4194304 | tf_op jit(solution)/shard_map/forward_edge/pallas_call | solution.py:201
  126.5 5.4 %cotangent_and_stats.1 = (bf16[1024,512]{1,0:T(8,128)(2,1)S(1)}, bf16[512,512]{1,0:T(8,128)(2,1)S(1)}, f32[512,128]{1,0:T(8,128)}) custom-call(s32[1024,1]{1,0:T(8,128)S(1)} %bitcast.44, s32[1,1024]{1,0:T(1,128)S(1)} %bitcast.47, s32[1,1536]{1,0:T(1,128)S(1)} %select_n.35.arrival_row_ref, s32[1536,1]{1,0:T(8,128)S(1)} %copy-done.4, ...), custom_call_target="tpu_custom_call" | custom-call | flops 2013265920 | bytes 3145728 | tf_op jit(solution)/shard_map/cotangent_and_stats/pallas_call | solution.py:281
  133.7 4.6 %all-to-all-start.2 = ((f32[64,8,128]{2,1,0:T(8,128)}), f32[64,8,128]{2,1,0:T(8,128)S(1)}, u32[]{:S(2)}, u32[]{:S(2)}) async-start(f32[64,8,128]{2,1,0:T(8,128)} %bitcast.12), calls=%async_computation.2 | async-start | bytes 524288 | tf_op jit(solution)/shard_map/all_to_all | solution.py:44
  139.8 1.5 copy.21
  144.1 2.0 reshape.189.slot_code_ref
  146.1 7.3 %collective-permute-start.3 = (bf16[512,512]{1,0:T(8,128)(2,1)}, bf16[512,512]{1,0:T(8,128)(2,1)}, u32[]{:S(2)}, u32[]{:S(2)}) collective-permute-start(bf16[512,512]{1,0:T(8,128)(2,1)} %copy-done.23), channel_id=1, source_target_pairs={{2,0},{4,2},{6,4},{8,6},{10,8},{12,10},{14,12},{16,14},{18,16},{20... | collective-permute-start | bytes 1572872 | tf_op jit(solution)/shard_map/ppermute | solution.py:40
  157.7 5.5 %all-to-all-start.3 = ((f32[64,16,128]{2,1,0:T(8,128)}), f32[64,16,128]{2,1,0:T(8,128)}, u32[]{:S(2)}, u32[]{:S(2)}) async-start(f32[64,16,128]{2,1,0:T(8,128)} %copy-done.11), calls=%async_computation.3 | async-start | bytes 1048576 | tf_op jit(solution)/shard_map/all_to_all | solution.py:44
  164.8 7.2 %collective-permute-start.1 = (s32[64,24]{0,1:T(8,128)S(1)}, s32[64,24]{0,1:T(8,128)S(1)}, u32[]{:S(2)}, u32[]{:S(2)}) collective-permute-start(s32[64,24]{0,1:T(8,128)S(1)} %add_select_fusion), channel_id=1, source_target_pairs={{2,0},{4,2},{6,4},{8,6},{10,8},{12,10},{14,12},{16,14},{18,16},{20... | collective-permute-start | bytes 18440 | tf_op jit(solution)/shard_map/ppermute | solution.py:40
  174.8 8.8 %collective-permute-done = s32[2,256]{1,0:T(2,128)S(1)} collective-permute-done((s32[2,256]{1,0:T(2,128)S(1)}, s32[2,256]{1,0:T(2,128)S(1)}, u32[]{:S(2)}, u32[]{:S(2)}) %collective-permute-start) | collective-permute-done | bytes 2080 | tf_op jit(solution)/shard_map/ppermute | solution.py:40
  193.9 18.1 %backward.1 = bf16[1536,1536]{1,0:T(8,128)(2,1)} custom-call(s32[1,1024]{1,0:T(1,128)S(1)} %bitcast.48, s32[1,512]{1,0:T(1,128)S(1)} %bitcast.49, s32[1536,1]{1,0:T(8,128)S(1)} %copy-done.8, s32[1536,1]{1,0:T(8,128)S(1)} %copy-done.5, s32[1536,1]{1,0:T(8,128)S(1)} %copy-done.6, f32[64,16,128]{2,1,0:T(8,128)} %all-to-all-done.3.stats_ref, ...), custom_call_target="tpu_custom_call" | custom-call | flops 8000000000 | bytes 15000000 | tf_op jit(solution)/shard_map/backward/pallas_call | solution.py:529
  212.0 10.4 %all-to-all-start.4 = ((bf16[64,24,1536]{2,1,0:T(8,128)(2,1)}), bf16[64,24,1536]{2,1,0:T(8,128)(2,1)}, u32[]{:S(2)}, u32[]{:S(2)}) async-start(bf16[64,24,1536]{2,1,0:T(8,128)(2,1)} %bitcast.50), calls=%async_computation.4 | async-start | bytes 9437184 | tf_op jit(solution)/shard_map/all_to_all | solution.py:44
  222.5 55.2 %all-to-all-done.4 = bf16[64,24,1536]{2,1,0:T(8,128)(2,1)} async-done(((bf16[64,24,1536]{2,1,0:T(8,128)(2,1)}), bf16[64,24,1536]{2,1,0:T(8,128)(2,1)}, u32[]{:S(2)}, u32[]{:S(2)}) %all-to-all-start.4) | async-done | bytes 4718624 | tf_op jit(solution)/shard_map/all_to_all | solution.py:44
  277.8 5.2 %combine_rows.1 = (bf16[512,512]{1,0:T(8,128)(2,1)}, bf16[512,512]{1,0:T(8,128)(2,1)}, bf16[512,512]{1,0:T(8,128)(2,1)}) custom-call(s32[1,1536]{1,0:T(1,128)S(1)} %reshape_reshape.12.index_row_ref, bf16[1536,1536]{1,0:T(8,128)(2,1)} %bitcast.15.arrived_ref), custom_call_target="tpu_custom_call" | custom-call | flops 2415919104 | bytes 6291456 | tf_op jit(solution)/shard_map/combine_rows/pallas_call | solution.py:583
  (119 shorter events, 45.9 us)
Async XLA Ops:
  3.9 4.6 %copy-start.9 = (s32[1536,1]{1,0:T(8,128)}, s32[1536,1]{1,0:T(8,128)S(1)}, u32[]{:S(2)}) copy-start(s32[1536,1]{1,0:T(8,128)S(1)} %reshape_reshape.15.index_ref) | copy-start | bytes 18436
  6.9 1.6 copy-start.2
  8.5 11.7 %copy-start.35 = (s32[2,512]{1,0:T(2,128)S(1)}, s32[2,512]{1,0:T(2,128)}, u32[]{:S(2)}) copy-start(s32[2,512]{1,0:T(2,128)} %param.11) | copy-start | bytes 12292
  8.5 11.8 %copy-start.34 = (s32[2,64]{1,0:T(2,128)S(1)}, s32[2,64]{1,0:T(2,128)}, u32[]{:S(2)}) copy-start(s32[2,64]{1,0:T(2,128)} %param.10) | copy-start | bytes 1540
  8.5 52.1 %all-to-all-start.1 = ((bf16[64,24,1024]{2,1,0:T(8,128)(2,1)}), bf16[64,24,1024]{2,1,0:T(8,128)(2,1)S(1)}, u32[]{:S(2)}, u32[]{:S(2)}) async-start(bf16[64,24,1024]{2,1,0:T(8,128)(2,1)} %bitcast.41), calls=%async_computation.1 | async-start | bytes 6291456 | tf_op jit(solution)/shard_map/all_to_all | solution.py:44
  25.2 1.2 copy-start.3
  60.6 10.5 %copy-start = (bf16[64,24,1024]{2,1,0:T(8,128)(2,1)}, bf16[64,24,1024]{2,1,0:T(8,128)(2,1)S(1)}, u32[]{:S(2)}) copy-start(bf16[64,24,1024]{2,1,0:T(8,128)(2,1)S(1)} %all-to-all-done.1) | copy-start | bytes 9437188
  60.6 60.3 %all-to-all-start = ((bf16[64,24,512]{2,1,0:T(8,128)(2,1)}), bf16[64,24,512]{2,1,0:T(8,128)(2,1)}, u32[]{:S(2)}, u32[]{:S(2)}) async-start(bf16[64,24,512]{2,1,0:T(8,128)(2,1)} %bitcast.42), calls=%async_computation | async-start | bytes 3145728 | tf_op jit(solution)/shard_map/all_to_all | solution.py:44
  71.1 1.9 copy-start.1
  81.0 33.2 %collective-permute-start.2 = (bf16[512,1024]{1,0:T(8,128)(2,1)}, bf16[512,1024]{1,0:T(8,128)(2,1)S(1)}, u32[]{:S(2)}, u32[]{:S(2)}) collective-permute-start(bf16[512,1024]{1,0:T(8,128)(2,1)} %get-tuple-element.14), channel_id=1, source_target_pairs={{126,0},{0,2},{2,4},{4,6},{6,8},{8,10},{10,12},{12,14},{14,16},{16... | collective-permute-start | bytes 3145736 | tf_op jit(solution)/shard_map/ppermute | solution.py:40
  90.2 30.7 %copy-start.25 = (f32[512,128]{1,0:T(8,128)}, f32[512,128]{1,0:T(8,128)S(1)}, u32[]{:S(2)}) copy-start(f32[512,128]{1,0:T(8,128)S(1)} %get-tuple-element.18.lse_second_ref) | copy-start | bytes 786436
  120.9 1.1 copy-start.4
  123.1 1.2 copy-start.15
  124.3 1.2 copy-start.18
  133.7 20.6 %all-to-all-start.2 = ((f32[64,8,128]{2,1,0:T(8,128)}), f32[64,8,128]{2,1,0:T(8,128)S(1)}, u32[]{:S(2)}, u32[]{:S(2)}) async-start(f32[64,8,128]{2,1,0:T(8,128)} %bitcast.12), calls=%async_computation.2 | async-start | bytes 524288 | tf_op jit(solution)/shard_map/all_to_all | solution.py:44
  146.1 38.8 %collective-permute-start.3 = (bf16[512,512]{1,0:T(8,128)(2,1)}, bf16[512,512]{1,0:T(8,128)(2,1)}, u32[]{:S(2)}, u32[]{:S(2)}) collective-permute-start(bf16[512,512]{1,0:T(8,128)(2,1)} %copy-done.23), channel_id=1, source_target_pairs={{2,0},{4,2},{6,4},{8,6},{10,8},{12,10},{14,12},{16,14},{18,16},{20... | collective-permute-start | bytes 1572872 | tf_op jit(solution)/shard_map/ppermute | solution.py:40
  153.4 31.4 %collective-permute-start.4 = (bf16[512,512]{1,0:T(8,128)(2,1)}, bf16[512,512]{1,0:T(8,128)(2,1)}, u32[]{:S(2)}, u32[]{:S(2)}) collective-permute-start(bf16[512,512]{1,0:T(8,128)(2,1)} %copy-done.24), channel_id=1, source_target_pairs={{2,0},{4,2},{6,4},{8,6},{10,8},{12,10},{14,12},{16,14},{18,16},{20... | collective-permute-start | bytes 1572872 | tf_op jit(solution)/shard_map/ppermute | solution.py:40
  157.7 27.2 %all-to-all-start.3 = ((f32[64,16,128]{2,1,0:T(8,128)}), f32[64,16,128]{2,1,0:T(8,128)}, u32[]{:S(2)}, u32[]{:S(2)}) async-start(f32[64,16,128]{2,1,0:T(8,128)} %copy-done.11), calls=%async_computation.3 | async-start | bytes 1048576 | tf_op jit(solution)/shard_map/all_to_all | solution.py:44
  164.8 18.8 %collective-permute-start.1 = (s32[64,24]{0,1:T(8,128)S(1)}, s32[64,24]{0,1:T(8,128)S(1)}, u32[]{:S(2)}, u32[]{:S(2)}) collective-permute-start(s32[64,24]{0,1:T(8,128)S(1)} %add_select_fusion), channel_id=1, source_target_pairs={{2,0},{4,2},{6,4},{8,6},{10,8},{12,10},{14,12},{16,14},{18,16},{20... | collective-permute-start | bytes 18440 | tf_op jit(solution)/shard_map/ppermute | solution.py:40
  172.7 10.9 %collective-permute-start = (s32[2,256]{1,0:T(2,128)S(1)}, s32[2,256]{1,0:T(2,128)S(1)}, u32[]{:S(2)}, u32[]{:S(2)}) collective-permute-start(s32[2,256]{1,0:T(2,128)S(1)} %slice.4), channel_id=1, source_target_pairs={{2,0},{4,2},{6,4},{8,6},{10,8},{12,10},{14,12},{16,14},{18,16},{20... | collective-permute-start | bytes 6152 | tf_op jit(solution)/shard_map/ppermute | solution.py:40
  188.3 1.2 copy-start.16
  189.5 1.2 copy-start.19
  192.6 1.2 copy-start.31
  212.0 65.8 %all-to-all-start.4 = ((bf16[64,24,1536]{2,1,0:T(8,128)(2,1)}), bf16[64,24,1536]{2,1,0:T(8,128)(2,1)}, u32[]{:S(2)}, u32[]{:S(2)}) async-start(bf16[64,24,1536]{2,1,0:T(8,128)(2,1)} %bitcast.50), calls=%async_computation.4 | async-start | bytes 9437184 | tf_op jit(solution)/shard_map/all_to_all | solution.py:44
  (23 other events, 21.6 us)

commit v2 on v1

--- a/solution.py
+++ b/solution.py
@@ -26,7 +26,7 @@
     )
 
 
-def params(mib=40):
+def params(mib=62):
     return pltpu.CompilerParams(vmem_limit_bytes=mib * MIB)
 
 
@@ -34,10 +34,26 @@
     return pl.CostEstimate(flops=int(flops), bytes_accessed=int(moved), transcendentals=int(exps))
 
 
-def shifted(block, axis, distance):
-    devices = range(lax.axis_size(axis))
-    route = [((i - distance) % len(devices), i) for i in devices]
-    return lax.ppermute(block, axis, route)
+def routed(block, route_of):
+    owners, halves = lax.axis_size("seq"), lax.axis_size("head")
+    route = [
+        (i * halves + half, route_of(i, half, owners) * halves + half)
+        for i in range(owners)
+        for half in range(halves)
+    ]
+    return lax.ppermute(block, ("seq", "head"), route)
+
+
+def to_next(block):
+    return routed(block, lambda i, half, n: (i + (1 if half == 0 else -1)) % n)
+
+
+def to_prior(block):
+    return routed(block, lambda i, half, n: (i - (1 if half == 0 else -1)) % n)
+
+
+def to_place(block):
+    return routed(block, lambda i, half, n: i if half == 0 else n - 1 - i)
 
 
 def exchange(block):
@@ -46,6 +62,23 @@
 
 def match(left, right):
     return jnp.where(left == right, 1.0, 0.0).astype(jnp.bfloat16)
+
+
+ARRIVAL, ARRIVAL3, NEXT3, PLACE, NEXT_PLACE, SEND, SEND3, HALF = 0, 16, 32, 48, 56, 64, 80, 96
+SLOT_ROWS, PLACE_ROWS, NEXT_ROWS = 12, 8, 4
+
+
+def table_row(table_ref, start, count):
+    return jnp.concatenate([table_ref[start + i : start + i + 1, :] for i in range(count)], axis=1)
+
+
+def table_cols(table_ref, start, count):
+    turned = table_ref[...].T
+    return [turned[:, start + i : start + i + 1] for i in range(count)]
+
+
+def match_cols(cols, row):
+    return jnp.concatenate([match(col, row) for col in cols])
 
 
 def iota(shape, axis):
@@ -69,37 +102,42 @@
 def pack_body(index_ref, *refs):
     sources, out_ref = refs[:-1], refs[-1]
     tokens, width = sources[0].shape
-    chosen = match(index_ref[...], iota((out_ref.shape[0], tokens), 1))
+    turned = index_ref[...].T
+    cols = [turned[:, i : i + 1] for i in range(out_ref.shape[0] // LANES)]
+    chosen = match_cols(cols, iota((LANES, tokens), 1))
     for place, source in enumerate(sources):
         out_ref[:, place * width : (place + 1) * width] = dot(chosen, source[...]).astype(
             jnp.bfloat16
         )
 
 
-def pack(index_col, *sources):
-    slots = index_col.shape[0]
+def pack(index, *sources):
+    steps = index.shape[0] // STAT
+    slots = SLOT_ROWS * LANES
     tokens, width = sources[0].shape
-    block = slots // 6
+    block = slots // steps
     total = width * len(sources)
     return pl.pallas_call(
         pack_body,
-        grid=(6,),
-        in_specs=[pl.BlockSpec((block, 1), lambda i: (i, 0))]
+        grid=(steps,),
+        in_specs=[pl.BlockSpec((STAT, LANES), lambda i: (i, 0))]
         + [pl.BlockSpec((tokens, width), lambda i: (0, 0)) for _ in sources],
         out_specs=pl.BlockSpec((block, total), lambda i: (i, 0)),
         out_shape=jax.ShapeDtypeStruct((slots, total), jnp.bfloat16),
         compiler_params=params(),
         cost_estimate=cost(2 * slots * tokens * total, 2 * (slots + tokens) * total),
         name="pack_rows",
-    )(index_col, *sources)
-
-
-def sort_body(place_col_ref, arrival_row_ref, arrived_ref, sorted_ref, tail_ref, head_ref, chosen):
+    )(index, *sources)
+
+
+def sort_body(table_ref, arrived_ref, sorted_ref, tail_ref, head_ref, chosen):
     step = pl.program_id(0)
 
     @pl.when(step == 0)
     def _():
-        chosen[...] = match(place_col_ref[...], arrival_row_ref[...])
+        chosen[...] = match_cols(
+            table_cols(table_ref, PLACE, PLACE_ROWS), table_row(table_ref, ARRIVAL, SLOT_ROWS)
+        )
 
     rows = dot(chosen[...], arrived_ref[...]).astype(jnp.bfloat16)
     sorted_ref[...] = rows
@@ -113,16 +151,15 @@
         head_ref[GROUP:, :] = rows[half : half + GROUP]
 
 
-def sort_rows(place_col, arrival_row, arrived):
+def sort_rows(table, arrived):
     slots, width = arrived.shape
-    rows = place_col.shape[0]
+    rows = PLACE_ROWS * LANES
     wide = width // 4
     return pl.pallas_call(
         sort_body,
         grid=(4,),
         in_specs=[
-            pl.BlockSpec((rows, 1), lambda i: (0, 0)),
-            pl.BlockSpec((1, slots), lambda i: (0, 0)),
+            pl.BlockSpec((LANES, LANES), lambda i: (0, 0)),
             pl.BlockSpec((slots, wide), lambda i: (0, i)),
         ],
         out_specs=[
@@ -139,7 +176,7 @@
         compiler_params=params(),
         cost_estimate=cost(2 * slots * rows * width, 2 * (slots + 2 * rows) * width),
         name="sort_rows",
-    )(place_col, arrival_row, arrived)
+    )(table, arrived)
 
 
 def forward_tile(query, keys, values):
@@ -217,10 +254,7 @@
 
 
 def stats_body(
-    place_col_ref,
-    place_row_ref,
-    arrival_row_ref,
-    arrival_col_ref,
+    table_ref,
     arrived_ref,
     out_first_ref,
     out_second_ref,
@@ -230,9 +264,12 @@
     head_ref,
     stats_ref,
 ):
-    rows = place_col_ref.shape[0]
+    rows = sorted_ref.shape[0]
     per_round = rows // 2
-    chosen = match(place_col_ref[...], arrival_row_ref[...])
+    place_row = table_row(table_ref, PLACE, PLACE_ROWS)
+    chosen = match_cols(
+        table_cols(table_ref, PLACE, PLACE_ROWS), table_row(table_ref, ARRIVAL, SLOT_ROWS)
+    )
     cotangent = dot(chosen, arrived_ref[...]).astype(jnp.bfloat16)
     sorted_ref[...] = cotangent
     lane = iota((GROUP, LANES), 1)
@@ -264,20 +301,19 @@
                 ).astype(jnp.bfloat16)
             )
     stats = jnp.concatenate(parts)
-    third_slots = arrival_col_ref.shape[0] // 3
+    third_slots = stats_ref.shape[0]
+    arrival_cols = table_cols(table_ref, ARRIVAL3, SLOT_ROWS)
     lane_third = (iota((third_slots, LANES), 1) % (3 * STAT)) // STAT
     result = jnp.zeros((third_slots, LANES), jnp.float32)
     for third in range(3):
-        back = match(
-            arrival_col_ref[third * third_slots : (third + 1) * third_slots], place_row_ref[...]
-        )
+        back = match_cols(arrival_cols[4 * third : 4 * third + 4], place_row)
         result = jnp.where(lane_third == third, dot(back, stats), result)
     stats_ref[...] = result
 
 
-def stats_out(place_col, place_row, arrival_row, arrival_col3, arrived, outs, lses):
+def stats_out(table, arrived, outs, lses):
     slots, width = arrived.shape
-    rows = place_col.shape[0]
+    rows = PLACE_ROWS * LANES
     return pl.pallas_call(
         stats_body,
         out_shape=[
@@ -288,15 +324,14 @@
         compiler_params=params(),
         cost_estimate=cost(2 * slots * rows * (width + LANES), 4 * slots * width),
         name="cotangent_and_stats",
-    )(place_col, place_row, arrival_row, arrival_col3, arrived, *outs, *lses)
-
-
-def gather_stats(codes_row, per_slot_codes, stats):
-    third_slots = stats.shape[0]
+    )(table, arrived, *outs, *lses)
+
+
+def gather_stats(codes_row, slot_cols, stats):
     narrow = stats.astype(jnp.bfloat16)
     total = None
     for third in range(3):
-        chosen = match(per_slot_codes[third * third_slots : (third + 1) * third_slots], codes_row)
+        chosen = match_cols(slot_cols[4 * third : 4 * third + 4], codes_row)
         found = dot(narrow, chosen, 0, 0)
         for piece in range(PIECES):
             at = piece * PIECES * STAT + third * STAT
@@ -305,9 +340,9 @@
     return total
 
 
-def total_body(tokens, slot_code_ref, arrived_ref, out_ref):
-    slots = slot_code_ref.shape[0]
-    found = gather_stats(iota((1, 2 * tokens), 1), slot_code_ref[...], arrived_ref[...])
+def total_body(tokens, table_ref, arrived_ref, out_ref):
+    slot_cols = table_cols(table_ref, SEND3, SLOT_ROWS)
+    found = gather_stats(iota((1, 2 * tokens), 1), slot_cols, arrived_ref[...])
     lse_first, lse_second = found[:4, :tokens], found[:4, tokens:]
     delta_first, delta_second = found[4:, :tokens], found[4:, tokens:]
     top = jnp.maximum(lse_first, lse_second)
@@ -319,22 +354,24 @@
     table = jnp.concatenate(
         [first] * 3 + [second] * 3 + [third_piece] * 3 + [spare]
     ).astype(jnp.bfloat16)
-    third_slots = slots // 3
+    third_slots = arrived_ref.shape[0]
     lane_third = (iota((third_slots, LANES), 1) % (3 * STAT)) // STAT
     result = jnp.zeros((third_slots, LANES), jnp.float32)
     for third in range(3):
-        code = slot_code_ref[third * third_slots : (third + 1) * third_slots]
-        row = jnp.where(code >= tokens, code - tokens, code)
-        chosen = match(row, iota((third_slots, tokens), 1))
+        codes = slot_cols[4 * third : 4 * third + 4]
+        cols = [jnp.where(code >= tokens, code - tokens, code) for code in codes]
+        chosen = match_cols(cols, iota((LANES, tokens), 1))
         result = jnp.where(lane_third == third, dot(chosen, table, 1, 1), result)
     owners = third_slots // STAT
     by_owner = result.reshape(owners, STAT, LANES)
     out_ref[:, :STAT, :] = by_owner
-    out_ref[: owners - 1, STAT:, :] = by_owner[1:]
-    out_ref[owners - 1 :, STAT:, :] = by_owner[:1]
-
-
-def total_stats(slot_code, arrived, tokens):
+    above = jnp.concatenate([by_owner[1:], by_owner[:1]])
+    below = jnp.concatenate([by_owner[owners - 1 :], by_owner[: owners - 1]])
+    half = table_ref[HALF : HALF + 1, :]
+    out_ref[:, STAT:, :] = jnp.where(half[None] == 0, above, below)
+
+
+def total_stats(table, arrived, tokens):
     owners = arrived.shape[0] // STAT
     return pl.pallas_call(
         functools.partial(total_body, tokens),
@@ -342,7 +379,7 @@
         compiler_params=params(),
         cost_estimate=cost(2 * 1536 * 1536 * LANES, 1 << 20),
         name="total_stats",
-    )(slot_code, arrived)
+    )(table, arrived)
 
 
 def backward_tile(query, upstream, keys, values, masked, total_row, delta_row):
@@ -356,11 +393,7 @@
 
 
 def backward_body(
-    place_row_ref,
-    next_row_ref,
-    arrival_col_ref,
-    arrival_col3_ref,
-    next_col3_ref,
+    table_ref,
     stats_ref,
     query_ref,
     value_ref,
@@ -382,16 +415,18 @@
 ):
     pair = pl.program_id(0)
     hash_round = pl.program_id(1)
-    rows = place_row_ref.shape[1]
+    rows = PLACE_ROWS * LANES
     per_round = rows // 2
 
     @pl.when((pair == 0) & (hash_round == 0))
     def _():
-        back[...] = match(arrival_col_ref[...], place_row_ref[...])
+        place_row = table_row(table_ref, PLACE, PLACE_ROWS)
+        next_row = table_row(table_ref, NEXT_PLACE, NEXT_ROWS)
+        back[...] = match_cols(table_cols(table_ref, ARRIVAL, SLOT_ROWS), place_row)
         own_stats = stats_ref[:, :STAT, :].reshape(-1, LANES)
         next_stats = stats_ref[:, STAT:, :].reshape(-1, LANES)
-        found = gather_stats(place_row_ref[...], arrival_col3_ref[...], own_stats)
-        edge = gather_stats(next_row_ref[...], next_col3_ref[...], next_stats)
+        found = gather_stats(place_row, table_cols(table_ref, ARRIVAL3, SLOT_ROWS), own_stats)
+        edge = gather_stats(next_row, table_cols(table_ref, NEXT3, SLOT_ROWS), next_stats)
         for each in range(2):
             totals[each] = found[:, each * per_round : (each + 1) * per_round]
             next_totals[each] = edge[:, each * GROUP : (each + 1) * GROUP]
@@ -507,23 +542,16 @@
         payload_ref[...] += dot(back[:, per_round:], shaped[...]).astype(jnp.bfloat16)
 
 
-def backward(index, stats, rows_sorted, cotangent, tail, next_query, next_cotangent, outs, lses):
+def backward(table, stats, rows_sorted, cotangent, tail, next_query, next_cotangent, outs, lses):
     rows, width = rows_sorted.shape
     per_round = rows // 2
-    slots = index["arrival_col"].shape[0]
+    slots = SLOT_ROWS * LANES
     wide = 2 * DH
 
     def whole(array):
         return pl.BlockSpec(array.shape, lambda p, r: (0,) * array.ndim)
 
-    small = [
-        index["place_row"],
-        index["next_row"],
-        index["arrival_col"],
-        index["arrival_col3"],
-        index["next_col3"],
-        stats,
-    ]
+    small = [table, stats]
     group_spec = pl.BlockSpec((GROUP, wide), lambda p, r: (r, p))
     lse_spec = pl.BlockSpec((GROUP, LANES), lambda p, r: (r, 0))
     return pl.pallas_call(
@@ -569,22 +597,22 @@
     )
 
 
-def combine_body(index_row_ref, arrived_ref, *out_refs):
+def combine_body(table_ref, arrived_ref, *out_refs):
     tokens, wide = out_refs[0].shape
-    chosen = match(iota((tokens, 1), 0), index_row_ref[...])
+    chosen = match(iota((tokens, 1), 0), table_row(table_ref, SEND, SLOT_ROWS))
     found = dot(chosen, arrived_ref[...])
     for place, out_ref in enumerate(out_refs):
         out_ref[...] = found[:, place * wide : (place + 1) * wide].astype(jnp.bfloat16)
 
 
-def combine(index_row, arrived, tokens):
+def combine(table, arrived, tokens):
     slots, width = arrived.shape
     wide = width // 6
     return pl.pallas_call(
         combine_body,
         grid=(2,),
         in_specs=[
-            pl.BlockSpec((1, slots), lambda i: (0, 0)),
+            pl.BlockSpec((LANES, LANES), lambda i: (0, 0)),
             pl.BlockSpec((slots, 3 * wide), lambda i: (0, i)),
         ],
         out_specs=[pl.BlockSpec((tokens, wide), lambda i: (0, i))] * 3,
@@ -592,7 +620,7 @@
         compiler_params=params(),
         cost_estimate=cost(2 * slots * tokens * width, 2 * (slots + tokens) * width),
         name="combine_rows",
-    )(index_row, arrived)
+    )(table, arrived)
 
 
 def per_device(query_key, value, attended_cotangent, send_rows, arrival_count, receive_slot):
@@ -604,59 +632,65 @@
     slots = owners * per_owner
 
     code = (tokens * jnp.arange(rounds, dtype=jnp.int32))[:, None]
+    half = lax.axis_index("head")
 
     def by_owner(table):
         return table.reshape(rounds, owners, capacity).transpose(1, 0, 2).reshape(owners, per_owner)
 
-    def by_third(table):
-        return table.reshape(owners, 3, STAT).transpose(1, 0, 2).reshape(slots, 1)
-
+    def by_third(codes):
+        return codes.reshape(owners, 3, STAT).transpose(1, 0, 2)
+
+    def rows_of(codes, count):
+        rows = codes.reshape(-1, LANES)
+        return jnp.pad(rows, ((0, count - rows.shape[0]), (0, 0)), constant_values=-1)
+
+    def sent(packed):
+        return exchange(packed.reshape(owners, per_owner, -1)).reshape(slots, -1)
+
+    blocks = send_rows.reshape(rounds, owners, capacity)
+    send_rows = jnp.where(half == 0, blocks, blocks[:, ::-1]).reshape(rounds, -1)
     send = by_owner(send_rows)
-    send_code = by_owner(send_rows + code)
+    send_blocks = send.reshape(6, 2, LANES)
+    send_blocks = jnp.pad(send_blocks, ((0, 0), (0, STAT - 2), (0, 0))).reshape(-1, LANES)
+    packed = pack(send_blocks, query_key, value)
+    packed_cotangent = pack(send_blocks, attended_cotangent)
+
+    arrival_count = to_place(arrival_count)
+    receive_slot = to_place(receive_slot)
     running = jnp.cumsum(arrival_count, axis=1)
     within = jnp.arange(capacity, dtype=jnp.int32)
     arrival = (running - arrival_count + code)[:, :, None] + within
     arrival = by_owner(jnp.where(within < arrival_count[:, :, None], arrival, -1))
     place = receive_slot + code
-    next_arrival = shifted(arrival, "seq", -1)
-    next_place = shifted(place[:, :GROUP], "seq", -1)
-
-    index = {
-        "place_row": place.reshape(1, -1),
-        "place_col": place.reshape(-1, 1),
-        "arrival_row": arrival.reshape(1, slots),
-        "arrival_col": arrival.reshape(slots, 1),
-        "arrival_col3": by_third(arrival),
-        "next_row": next_place.reshape(1, -1),
-        "next_col3": by_third(next_arrival),
-    }
-
-    def sent(packed):
-        return exchange(packed.reshape(owners, per_owner, -1)).reshape(slots, -1)
-
-    send_col = send.reshape(slots, 1)
-    arrived = sent(pack(send_col, query_key, value))
-    rows_sorted, tail, head_query = sort_rows(index["place_col"], index["arrival_row"], arrived)
-    arrived_cotangent = sent(pack(send_col, attended_cotangent))
-    prior_tail = shifted(tail, "seq", 1)
-    next_query = shifted(head_query, "seq", -1)
+    next_arrival = to_prior(arrival)
+    next_place = to_prior(place[:, :GROUP])
+    table = jnp.concatenate(
+        [
+            rows_of(arrival, ARRIVAL3 - ARRIVAL),
+            rows_of(by_third(arrival), NEXT3 - ARRIVAL3),
+            rows_of(by_third(next_arrival), PLACE - NEXT3),
+            rows_of(place, NEXT_PLACE - PLACE),
+            rows_of(next_place, SEND - NEXT_PLACE),
+            rows_of(send, SEND3 - SEND),
+            rows_of(by_third(by_owner(send_rows + code)), HALF - SEND3),
+            jnp.full((LANES - HALF, LANES), half, jnp.int32),
+        ]
+    )
+
+    arrived, table = lax.optimization_barrier((sent(packed), table))
+    rows_sorted, tail, head_query = sort_rows(table, arrived)
+    prior_tail = to_next(tail)
+    arrived_cotangent = sent(packed_cotangent)
+    next_query = to_prior(head_query)
     out_second, lse_second = forward(rows_sorted)
     out_first, lse_first = forward(rows_sorted, prior_tail)
     outs, lses = (out_first, out_second), (lse_first, lse_second)
-    cotangent, head_cotangent, stats = stats_out(
-        index["place_col"],
-        index["place_row"],
-        index["arrival_row"],
-        index["arrival_col3"],
-        arrived_cotangent,
-        outs,
-        lses,
-    )
-    next_cotangent = shifted(head_cotangent, "seq", -1)
+    cotangent, head_cotangent, stats = stats_out(table, arrived_cotangent, outs, lses)
+    next_cotangent = to_prior(head_cotangent)
     home_stats = exchange(stats.reshape(owners, STAT, LANES)).reshape(-1, LANES)
-    totals = exchange(total_stats(by_third(send_code), home_stats, tokens))
+    totals = exchange(total_stats(table, home_stats, tokens))
     payload = backward(
-        index,
+        table,
         totals,
         rows_sorted,
         cotangent,
@@ -666,7 +700,7 @@
         outs,
         lses,
     )
-    return tuple(combine(send.reshape(1, slots), sent(payload), tokens))
+    return tuple(combine(table, sent(payload), tokens))
 
 
 def solution(mesh):

time: 287 us -> 244 us (0.85); the launches traced: 283 us -> 243 us
  waiting for transfers between devices: 122 us -> 59.7 us
  blocking collectives: 0 us -> 62 us
  local copies, waits for them, and re-layouts: 47.6 us -> 6.04 us
  Pallas kernels: 51 us -> 64.2 us
  starting transfers between devices: 59.1 us -> 49.7 us
    all_to_all x5 -> x4, waiting for transfers between devices: 89.5 us -> 18.7 us  [exchange(): return lax.all_to_all(block, 'seq', split_axis=0, concat_axis=0, tiled=True)]
    all_to_all x0 -> x1, blocking collectives: none -> 62 us  [exchange(): return lax.all_to_all(block, 'seq', split_axis=0, concat_axis=0, tiled=True)]
    unnamed x77 -> x23, local copies, waits for them, and re-layouts: 33.6 us -> 3.16 us
    all_to_all x5 -> x4, starting transfers between devices: 41.3 us -> 30.5 us  [exchange(): return lax.all_to_all(block, 'seq', split_axis=0, concat_axis=0, tiled=True)]
    ppermute x5 -> x7, waiting for transfers between devices: 32.7 us -> 41 us  [routed(): return lax.ppermute(block, ('seq', 'head'), route)]
    pallas_call x4, Pallas kernels: 16.3 us -> 23.7 us  [the longest x2 11.2 us: pack(): pl.pallas_call(pack_body, grid=(steps,), in_specs=[pl.BlockSpec((STAT, LA...]
    reshape x5 -> x7, local copies, waits for them, and re-layouts: 5.85 us -> 1.75 us  [the longest x1 0.8 us: per_device(): blocks = send_rows.reshape(rounds, owners, capacity)]
    pallas_call x2, Pallas kernels: 9.74 us -> 12.6 us  [forward(): pl.pallas_call(functools.partial(forward_body, with_edge), grid=(2, 2), i...]
  transfers between devices with their start and end apart: 10 -> 11, of which waited for: 4 -> 6; matrix products, arithmetic and copies ran while one was open for 6% -> 1% of each run, Pallas kernels for 7% -> 12%
where the time goes in v2:
time: 244 us; the launch traced here: 243 us
  Pallas kernels  64.2 us (26%)
  blocking collectives  62 us (25%)
  waiting for transfers between devices  59.7 us (24%)
  starting transfers between devices  49.7 us (20%)
  local copies, waits for them, and re-layouts  6.04 us (2%)
    all_to_all x1, blocking collectives, exchange(): return lax.all_to_all(block, 'seq', split_axis=0, concat_axis=0, tiled=True)  62 us
    ppermute x7, waiting for transfers between devices, routed(): return lax.ppermute(block, ('seq', 'head'), route)  41 us
    all_to_all x4, starting transfers between devices, exchange(): return lax.all_to_all(block, 'seq', split_axis=0, concat_axis=0, tiled=True)  30.5 us
    ppermute x7, starting transfers between devices, routed(): return lax.ppermute(block, ('seq', 'head'), route)  19.2 us
    all_to_all x4, waiting for transfers between devices, exchange(): return lax.all_to_all(block, 'seq', split_axis=0, concat_axis=0, tiled=True)  18.7 us
    pallas_call x1, Pallas kernels, backward(): pl.pallas_call(backward_body, grid=(2, 2), in_specs=[whole(array) for arr...  18.4 us
    pallas_call x2, Pallas kernels, forward(): pl.pallas_call(functools.partial(forward_body, with_edge), grid=(2, 2), i...  12.6 us
    pallas_call x2, Pallas kernels, pack(): pl.pallas_call(pack_body, grid=(steps,), in_specs=[pl.BlockSpec((STAT, LA...  11.2 us
  transfers between devices with their start and end apart: 11, of which 6 were waited for; matrix products, arithmetic and copies ran while one was open for 1% of the time, Pallas kernels for 12%

profile of v2, /device:TPU:0, one launch (start us, length us, event | category | flops | bytes accessed | tf_op | source)
XLA Modules:
  0.0 243.1 jit_solution(9599259770396292599)
XLA Ops:
  2.4 6.0 %pack_rows.2 = bf16[1536,1024]{1,0:T(8,128)(2,1)} custom-call(s32[48,128]{1,0:T(8,128)} %pad_bitcast_fusion.index_ref, bf16[512,512]{1,0:T(8,128)(2,1)} %refs_0_.2, bf16[512,512]{1,0:T(8,128)(2,1)} %refs_1_.1), custom_call_target="tpu_custom_call" | custom-call | flops 1610612736 | bytes 4194304 | tf_op jit(solution)/shard_map/pack_rows/pallas_call | solution.py:120
  8.4 11.9 %all-to-all-start = ((bf16[64,24,1024]{2,1,0:T(8,128)(2,1)}), bf16[64,24,1024]{2,1,0:T(8,128)(2,1)}, u32[]{:S(2)}, u32[]{:S(2)}) async-start(bf16[64,24,1024]{2,1,0:T(8,128)(2,1)} %bitcast.35), calls=%async_computation | async-start | bytes 6291456 | tf_op jit(solution)/shard_map/all_to_all | solution.py:60
  21.7 5.2 %pack_rows.3 = bf16[1536,512]{1,0:T(8,128)(2,1)} custom-call(s32[48,128]{1,0:T(8,128)} %pad_bitcast_fusion.index_ref, bf16[512,512]{1,0:T(8,128)(2,1)} %refs_0_.3), custom_call_target="tpu_custom_call" | custom-call | flops 805306368 | bytes 2097152 | tf_op jit(solution)/shard_map/pack_rows/pallas_call | solution.py:120
  27.8 7.3 %collective-permute-start.1 = (s32[64,24]{0,1:T(8,128)S(1)}, s32[64,24]{0,1:T(8,128)S(1)}, u32[]{:S(2)}, u32[]{:S(2)}) collective-permute-start(s32[64,24]{0,1:T(8,128)S(1)} %add_select_fusion.1), channel_id=1, source_target_pairs={{0,126},{1,3},{2,0},{3,5},{4,2},{5,7},{6,4},{7,9},{8,6},{9,11},{10... | collective-permute-start | bytes 18440 | tf_op jit(solution)/shard_map/ppermute | solution.py:44
  36.6 16.9 %collective-permute-done.3 = s32[2,256]{1,0:T(2,128)S(1)} collective-permute-done((s32[2,256]{1,0:T(2,128)S(1)}, s32[2,256]{1,0:T(2,128)S(1)}, u32[]{:S(2)}, u32[]{:S(2)}) %collective-permute-start.3) | collective-permute-done | bytes 2080 | tf_op jit(solution)/shard_map/ppermute | solution.py:44
  53.8 6.8 %all-to-all-done = bf16[64,24,1024]{2,1,0:T(8,128)(2,1)} async-done(((bf16[64,24,1024]{2,1,0:T(8,128)(2,1)}), bf16[64,24,1024]{2,1,0:T(8,128)(2,1)}, u32[]{:S(2)}, u32[]{:S(2)}) %all-to-all-start) | async-done | bytes 3145760 | tf_op jit(solution)/shard_map/all_to_all | solution.py:60
  60.6 9.2 %all-to-all-start.1 = ((bf16[64,24,512]{2,1,0:T(8,128)(2,1)}), bf16[64,24,512]{2,1,0:T(8,128)(2,1)}, u32[]{:S(2)}, u32[]{:S(2)}) async-start(bf16[64,24,512]{2,1,0:T(8,128)(2,1)} %bitcast.36), calls=%async_computation.1 | async-start | bytes 3145728 | tf_op jit(solution)/shard_map/all_to_all | solution.py:60
  70.5 7.3 %sort_rows.1 = (bf16[1024,1024]{1,0:T(8,128)(2,1)}, bf16[512,1024]{1,0:T(8,128)(2,1)}, bf16[512,512]{1,0:T(8,128)(2,1)}) custom-call(s32[128,128]{1,0:T(8,128)} %copy-done.3, bf16[1536,1024]{1,0:T(8,128)(2,1)} %bitcast.3.arrived_ref), custom_call_target="tpu_custom_call" | custom-call | flops 3221225472 | bytes 7340032 | tf_op jit(solution)/shard_map/sort_rows/pallas_call | solution.py:158
  77.7 1.5 collective-permute-start.4
  79.2 6.2 %forward_own.1 = (f32[512,512]{1,0:T(8,128)}, f32[512,128]{1,0:T(8,128)}) custom-call(bf16[1024,1024]{1,0:T(8,128)(2,1)} %get-tuple-element.17.refs_0_.refs_1_.query_ref.value_ref, bf16[1024,1024]{1,0:T(8,128)(2,1)} %get-tuple-element.17.refs_0_.refs_1_.query_ref.value_ref), custom_call_target="tpu_custom_call" | custom-call | flops 536870912 | bytes 4194304 | tf_op jit(solution)/shard_map/forward_own/pallas_call | solution.py:238
  85.5 20.9 %collective-permute-done.4.refs_2_.refs_3_.tail_query_ref.tail_value_ref = bf16[512,1024]{1,0:T(8,128)(2,1)S(1)} collective-permute-done((bf16[512,1024]{1,0:T(8,128)(2,1)}, bf16[512,1024]{1,0:T(8,128)(2,1)S(1)}, u32[]{:S(2)}, u32[]{:S(2)}) %collective-permute-start.4) | collective-permute-done | bytes 1048608 | tf_op jit(solution)/shard_map/ppermute | solution.py:44
  106.3 1.0 copy-done
  107.3 6.4 %forward_edge.1 = (f32[512,512]{1,0:T(8,128)}, f32[512,128]{1,0:T(8,128)}) custom-call(bf16[1024,1024]{1,0:T(8,128)(2,1)} %get-tuple-element.17.refs_0_.refs_1_.query_ref.value_ref, bf16[1024,1024]{1,0:T(8,128)(2,1)} %get-tuple-element.17.refs_0_.refs_1_.query_ref.value_ref, bf16[512,1024]{1,0:T(8,128)(2,1)} %copy-done, bf16[512,1024]{1,0:T(8,128)(2,1)} %copy-done), custom_call_target="tpu_custom_call" | custom-call | flops 536870912 | bytes 4194304 | tf_op jit(solution)/shard_map/forward_edge/pallas_call | solution.py:238
  113.7 6.3 %cotangent_and_stats.1 = (bf16[1024,512]{1,0:T(8,128)(2,1)}, bf16[512,512]{1,0:T(8,128)(2,1)}, f32[512,128]{1,0:T(8,128)}) custom-call(s32[128,128]{1,0:T(8,128)} %copy-done.3, bf16[1536,512]{1,0:T(8,128)(2,1)} %bitcast.12.arrived_ref, f32[512,512]{1,0:T(8,128)} %get-tuple-element.19.out_first_ref, f32[512,512]{1,0:T(8,128)} %get-tuple-element.20.out_second_ref, ...), custom_call_target="tpu_custom_call" | custom-call | flops 2013265920 | bytes 3145728 | tf_op jit(solution)/shard_map/cotangent_and_stats/pallas_call | solution.py:317
  120.1 4.8 %all-to-all-start.2 = ((f32[64,8,128]{2,1,0:T(8,128)}), f32[64,8,128]{2,1,0:T(8,128)S(1)}, u32[]{:S(2)}, u32[]{:S(2)}) async-start(f32[64,8,128]{2,1,0:T(8,128)} %bitcast.38), calls=%async_computation.2 | async-start | bytes 524288 | tf_op jit(solution)/shard_map/all_to_all | solution.py:60
  124.9 7.4 %collective-permute-start.5 = (bf16[512,512]{1,0:T(8,128)(2,1)S(1)}, bf16[512,512]{1,0:T(8,128)(2,1)S(1)}, u32[]{:S(2)}, u32[]{:S(2)}) collective-permute-start(bf16[512,512]{1,0:T(8,128)(2,1)S(1)} %copy-done.4), channel_id=1, source_target_pairs={{0,126},{1,3},{2,0},{3,5},{4,2},{5,7},{6,4},{7,9},{8,6},{9,11},{10... | collective-permute-start | bytes 1572872 | tf_op jit(solution)/shard_map/ppermute | solution.py:44
  133.1 3.2 %all-to-all-done.2 = f32[64,8,128]{2,1,0:T(8,128)S(1)} async-done(((f32[64,8,128]{2,1,0:T(8,128)}), f32[64,8,128]{2,1,0:T(8,128)S(1)}, u32[]{:S(2)}, u32[]{:S(2)}) %all-to-all-start.2) | async-done | bytes 262176 | tf_op jit(solution)/shard_map/all_to_all | solution.py:60
  137.1 3.2 %total_stats.1 = f32[64,16,128]{2,1,0:T(8,128)} custom-call(s32[128,128]{1,0:T(8,128)} %copy-done.3, f32[512,128]{1,0:T(8,128)} %bitcast.37), custom_call_target="tpu_custom_call" | custom-call | flops 603979776 | bytes 1048576 | tf_op jit(solution)/shard_map/total_stats/pallas_call | solution.py:376
  140.2 4.6 %all-to-all-start.3 = ((f32[64,16,128]{2,1,0:T(8,128)}), f32[64,16,128]{2,1,0:T(8,128)S(1)}, u32[]{:S(2)}, u32[]{:S(2)}) async-start(f32[64,16,128]{2,1,0:T(8,128)} %total_stats.1), calls=%async_computation.3 | async-start | bytes 1048576 | tf_op jit(solution)/shard_map/all_to_all | solution.py:60
  144.9 3.2 %collective-permute-done.6.next_cotangent_ref = bf16[512,512]{1,0:T(8,128)(2,1)} collective-permute-done((bf16[512,512]{1,0:T(8,128)(2,1)}, bf16[512,512]{1,0:T(8,128)(2,1)}, u32[]{:S(2)}, u32[]{:S(2)}) %collective-permute-start.6) | collective-permute-done | bytes 524320 | tf_op jit(solution)/shard_map/ppermute | solution.py:44
  148.1 8.6 %all-to-all-done.3.stats_ref = f32[64,16,128]{2,1,0:T(8,128)S(1)} async-done(((f32[64,16,128]{2,1,0:T(8,128)}), f32[64,16,128]{2,1,0:T(8,128)S(1)}, u32[]{:S(2)}, u32[]{:S(2)}) %all-to-all-start.3) | async-done | bytes 524320 | tf_op jit(solution)/shard_map/all_to_all | solution.py:60
  157.6 18.4 %backward.1 = bf16[1536,1536]{1,0:T(8,128)(2,1)} custom-call(s32[128,128]{1,0:T(8,128)} %copy-done.3, f32[64,16,128]{2,1,0:T(8,128)} %copy-done.1, bf16[1024,1024]{1,0:T(8,128)(2,1)} %get-tuple-element.17.refs_0_.refs_1_.query_ref.value_ref, bf16[1024,1024]{1,0:T(8,128)(2,1)} %get-tuple-element.17.refs_0_.refs_1_.query_ref.value_ref, ...), custom_call_target="tpu_custom_call" | custom-call | flops 8000000000 | bytes 15000000 | tf_op jit(solution)/shard_map/backward/pallas_call | solution.py:557
  175.9 62.0 %all_to_all.25 = bf16[64,24,1536]{2,1,0:T(8,128)(2,1)} all-to-all(bf16[64,24,1536]{2,1,0:T(8,128)(2,1)} %bitcast.33), channel_id=1, replica_groups=mesh['seq'=64,'head'=2] {'seq'}, dimensions={0} | all-to-all | bytes 9437184 | tf_op jit(solution)/shard_map/all_to_all | solution.py:60
  237.9 5.3 %combine_rows.1 = (bf16[512,512]{1,0:T(8,128)(2,1)}, bf16[512,512]{1,0:T(8,128)(2,1)}, bf16[512,512]{1,0:T(8,128)(2,1)}) custom-call(s32[128,128]{1,0:T(8,128)} %copy-done.3, bf16[1536,1536]{1,0:T(8,128)(2,1)} %bitcast.34), custom_call_target="tpu_custom_call" | custom-call | flops 2415919104 | bytes 6291456 | tf_op jit(solution)/shard_map/combine_rows/pallas_call | solution.py:611
  (69 shorter events, 8.7 us)
Async XLA Ops:
  8.4 11.9 %copy-start.7 = (s32[2,64]{1,0:T(2,128)S(1)}, s32[2,64]{1,0:T(2,128)}, u32[]{:S(2)}) copy-start(s32[2,64]{1,0:T(2,128)} %param.10) | copy-start | bytes 1540
  8.4 12.6 %copy-start.6 = (s32[2,512]{1,0:T(2,128)S(1)}, s32[2,512]{1,0:T(2,128)}, u32[]{:S(2)}) copy-start(s32[2,512]{1,0:T(2,128)} %param.11) | copy-start | bytes 12292
  8.4 52.2 %all-to-all-start = ((bf16[64,24,1024]{2,1,0:T(8,128)(2,1)}), bf16[64,24,1024]{2,1,0:T(8,128)(2,1)}, u32[]{:S(2)}, u32[]{:S(2)}) async-start(bf16[64,24,1024]{2,1,0:T(8,128)(2,1)} %bitcast.35), calls=%async_computation | async-start | bytes 6291456 | tf_op jit(solution)/shard_map/all_to_all | solution.py:60
  20.2 7.2 %collective-permute-start = (s32[2,64]{1,0:T(2,128)S(1)}, s32[2,64]{1,0:T(2,128)S(1)}, u32[]{:S(2)}, u32[]{:S(2)}) collective-permute-start(s32[2,64]{1,0:T(2,128)S(1)} %copy-done.7), channel_id=1, source_target_pairs={{0,0},{1,127},{2,2},{3,125},{4,4},{5,123},{6,6},{7,121},{8,8},{9,1... | collective-permute-start | bytes 1544 | tf_op jit(solution)/shard_map/ppermute | solution.py:44
  20.9 14.7 %collective-permute-start.2 = (s32[2,512]{1,0:T(2,128)S(1)}, s32[2,512]{1,0:T(2,128)S(1)}, u32[]{:S(2)}, u32[]{:S(2)}) collective-permute-start(s32[2,512]{1,0:T(2,128)S(1)} %copy-done.6), channel_id=1, source_target_pairs={{0,0},{1,127},{2,2},{3,125},{4,4},{5,123},{6,6},{7,121},{8,8},{9,1... | collective-permute-start | bytes 12296 | tf_op jit(solution)/shard_map/ppermute | solution.py:44
  27.8 25.7 %collective-permute-start.1 = (s32[64,24]{0,1:T(8,128)S(1)}, s32[64,24]{0,1:T(8,128)S(1)}, u32[]{:S(2)}, u32[]{:S(2)}) collective-permute-start(s32[64,24]{0,1:T(8,128)S(1)} %add_select_fusion.1), channel_id=1, source_target_pairs={{0,126},{1,3},{2,0},{3,5},{4,2},{5,7},{6,4},{7,9},{8,6},{9,11},{10... | collective-permute-start | bytes 18440 | tf_op jit(solution)/shard_map/ppermute | solution.py:44
  35.7 17.8 %collective-permute-start.3 = (s32[2,256]{1,0:T(2,128)S(1)}, s32[2,256]{1,0:T(2,128)S(1)}, u32[]{:S(2)}, u32[]{:S(2)}) collective-permute-start(s32[2,256]{1,0:T(2,128)S(1)} %slice.4), channel_id=1, source_target_pairs={{0,126},{1,3},{2,0},{3,5},{4,2},{5,7},{6,4},{7,9},{8,6},{9,11},{10... | collective-permute-start | bytes 6152 | tf_op jit(solution)/shard_map/ppermute | solution.py:44
  60.6 53.1 %all-to-all-start.1 = ((bf16[64,24,512]{2,1,0:T(8,128)(2,1)}), bf16[64,24,512]{2,1,0:T(8,128)(2,1)}, u32[]{:S(2)}, u32[]{:S(2)}) async-start(bf16[64,24,512]{2,1,0:T(8,128)(2,1)} %bitcast.36), calls=%async_computation.1 | async-start | bytes 3145728 | tf_op jit(solution)/shard_map/all_to_all | solution.py:60
  69.8 0.6 copy-start.3
  77.7 28.6 %collective-permute-start.4 = (bf16[512,1024]{1,0:T(8,128)(2,1)}, bf16[512,1024]{1,0:T(8,128)(2,1)S(1)}, u32[]{:S(2)}, u32[]{:S(2)}) collective-permute-start(bf16[512,1024]{1,0:T(8,128)(2,1)} %get-tuple-element.18), channel_id=1, source_target_pairs={{0,2},{1,127},{2,4},{3,1},{4,6},{5,3},{6,8},{7,5},{8,10},{9,7},{10... | collective-permute-start | bytes 3145736 | tf_op jit(solution)/shard_map/ppermute | solution.py:44
  106.3 1.0 copy-start
  113.7 11.1 %copy-start.4 = (bf16[512,512]{1,0:T(8,128)(2,1)S(1)}, bf16[512,512]{1,0:T(8,128)(2,1)}, u32[]{:S(2)}) copy-start(bf16[512,512]{1,0:T(8,128)(2,1)} %get-tuple-element.25) | copy-start | bytes 1572868
  120.1 16.3 %all-to-all-start.2 = ((f32[64,8,128]{2,1,0:T(8,128)}), f32[64,8,128]{2,1,0:T(8,128)S(1)}, u32[]{:S(2)}, u32[]{:S(2)}) async-start(f32[64,8,128]{2,1,0:T(8,128)} %bitcast.38), calls=%async_computation.2 | async-start | bytes 524288 | tf_op jit(solution)/shard_map/all_to_all | solution.py:60
  124.9 20.0 %collective-permute-start.5 = (bf16[512,512]{1,0:T(8,128)(2,1)S(1)}, bf16[512,512]{1,0:T(8,128)(2,1)S(1)}, u32[]{:S(2)}, u32[]{:S(2)}) collective-permute-start(bf16[512,512]{1,0:T(8,128)(2,1)S(1)} %copy-done.4), channel_id=1, source_target_pairs={{0,126},{1,3},{2,0},{3,5},{4,2},{5,7},{6,4},{7,9},{8,6},{9,11},{10... | collective-permute-start | bytes 1572872 | tf_op jit(solution)/shard_map/ppermute | solution.py:44
  132.3 15.9 %collective-permute-start.6 = (bf16[512,512]{1,0:T(8,128)(2,1)}, bf16[512,512]{1,0:T(8,128)(2,1)}, u32[]{:S(2)}, u32[]{:S(2)}) collective-permute-start(bf16[512,512]{1,0:T(8,128)(2,1)} %get-tuple-element.26), channel_id=1, source_target_pairs={{0,126},{1,3},{2,0},{3,5},{4,2},{5,7},{6,4},{7,9},{8,6},{9,11},{10... | collective-permute-start | bytes 1572872 | tf_op jit(solution)/shard_map/ppermute | solution.py:44
  136.3 0.7 copy-start.2
  140.2 16.5 %all-to-all-start.3 = ((f32[64,16,128]{2,1,0:T(8,128)}), f32[64,16,128]{2,1,0:T(8,128)S(1)}, u32[]{:S(2)}, u32[]{:S(2)}) async-start(f32[64,16,128]{2,1,0:T(8,128)} %total_stats.1), calls=%async_computation.3 | async-start | bytes 1048576 | tf_op jit(solution)/shard_map/all_to_all | solution.py:60
  144.9 11.9 %copy-start.5 = (bf16[512,512]{1,0:T(8,128)(2,1)}, bf16[512,512]{1,0:T(8,128)(2,1)S(1)}, u32[]{:S(2)}) copy-start(bf16[512,512]{1,0:T(8,128)(2,1)S(1)} %collective-permute-done.5.next_query_ref) | copy-start | bytes 1572868
  156.8 0.8 copy-start.1

commit v3 on v2

--- a/solution.py
+++ b/solution.py
@@ -50,6 +50,10 @@
 
 def to_prior(block):
     return routed(block, lambda i, half, n: (i - (1 if half == 0 else -1)) % n)
+
+
+def to_place_prior(block):
+    return routed(block, lambda i, half, n: (i - 1) % n if half == 0 else n - 1 - (i - 1) % n)
 
 
 def to_place(block):
@@ -130,52 +134,38 @@
     )(index, *sources)
 
 
-def sort_body(table_ref, arrived_ref, sorted_ref, tail_ref, head_ref, chosen):
-    step = pl.program_id(0)
-
-    @pl.when(step == 0)
+def place_cols(table_ref, group):
+    cols = table_cols(table_ref, PLACE, PLACE_ROWS)
+    each = GROUP // LANES
+    first, second = group * each, PLACE_ROWS // 2 + group * each
+    return cols[first : first + each], cols[second : second + each]
+
+
+def tail_body(table_ref, arrived_ref, tail_ref, chosen):
+    @pl.when(pl.program_id(0) == 0)
     def _():
-        chosen[...] = match_cols(
-            table_cols(table_ref, PLACE, PLACE_ROWS), table_row(table_ref, ARRIVAL, SLOT_ROWS)
-        )
-
-    rows = dot(chosen[...], arrived_ref[...]).astype(jnp.bfloat16)
-    sorted_ref[...] = rows
-    half = rows.shape[0] // 2
-    tail_ref[:GROUP, :] = rows[half - GROUP : half]
-    tail_ref[GROUP:, :] = rows[2 * half - GROUP :]
-
-    @pl.when(step < 2)
-    def _():
-        head_ref[:GROUP, :] = rows[:GROUP]
-        head_ref[GROUP:, :] = rows[half : half + GROUP]
-
-
-def sort_rows(table, arrived):
-    slots, width = arrived.shape
-    rows = PLACE_ROWS * LANES
+        first, second = place_cols(table_ref, 1)
+        chosen[...] = match_cols(first + second, table_row(table_ref, ARRIVAL, SLOT_ROWS))
+
+    tail_ref[...] = dot(chosen[...], arrived_ref[...]).astype(jnp.bfloat16)
+
+
+def sort_tail(table, arrived, width):
+    slots = arrived.shape[0]
     wide = width // 4
     return pl.pallas_call(
-        sort_body,
+        tail_body,
         grid=(4,),
         in_specs=[
             pl.BlockSpec((LANES, LANES), lambda i: (0, 0)),
             pl.BlockSpec((slots, wide), lambda i: (0, i)),
         ],
-        out_specs=[
-            pl.BlockSpec((rows, wide), lambda i: (0, i)),
-            pl.BlockSpec((2 * GROUP, wide), lambda i: (0, i)),
-            pl.BlockSpec((2 * GROUP, wide), lambda i: (0, jnp.minimum(i, 1))),
-        ],
-        out_shape=[
-            jax.ShapeDtypeStruct((rows, width), jnp.bfloat16),
-            jax.ShapeDtypeStruct((2 * GROUP, width), jnp.bfloat16),
-            jax.ShapeDtypeStruct((2 * GROUP, width // 2), jnp.bfloat16),
-        ],
-        scratch_shapes=[pltpu.VMEM((rows, slots), jnp.bfloat16)],
+        out_specs=pl.BlockSpec((2 * GROUP, wide), lambda i: (0, i)),
+        out_shape=jax.ShapeDtypeStruct((2 * GROUP, width), jnp.bfloat16),
+        scratch_shapes=[pltpu.VMEM((2 * GROUP, slots), jnp.bfloat16)],
         compiler_params=params(),
-        cost_estimate=cost(2 * slots * rows * width, 2 * (slots + 2 * rows) * width),
-        name="sort_rows",
+        cost_estimate=cost(4 * slots * GROUP * width, 2 * (slots + 2 * GROUP) * width),
+        name="sort_tail",
     )(table, arrived)
 
 
@@ -190,141 +180,176 @@
     return dot(weights, values), top + jnp.log(total)
 
 
-def forward_body(with_edge, *refs):
-    if with_edge:
-        query_ref, value_ref, tail_query_ref, tail_value_ref, out_ref, lse_ref = refs
-    else:
-        query_ref, value_ref, out_ref, lse_ref = refs
-    pair = pl.program_id(1)
+def forward_pair(pair, query, raw, values, cotangent, out_ref):
     lane = iota((GROUP, LANES), 1) % STAT
-
+    stat = jnp.zeros((GROUP, LANES), jnp.float32)
     for local in range(2):
         columns = slice(local * DH, (local + 1) * DH)
-        if with_edge:
-            raw = jnp.concatenate([tail_query_ref[:, columns], query_ref[:GROUP, columns]])
-            values = jnp.concatenate([tail_value_ref[:, columns], value_ref[:GROUP, columns]])
-            query = query_ref[:GROUP, columns]
-        else:
-            raw = query_ref[:, columns]
-            values = value_ref[:, columns]
-            query = query_ref[GROUP:, columns]
-        keys = unit_rows(raw)[0].astype(jnp.bfloat16)
-        partial, lse = forward_tile(query, keys, values)
+        keys = unit_rows(raw[:, columns])[0].astype(jnp.bfloat16)
+        partial, lse = forward_tile(query[:, columns], keys, values[:, columns])
         out_ref[:, columns] = partial
-        at_head = lane == pair * 2 + local
-        if local == 0:
-            before = jnp.where(pair == 0, jnp.zeros((GROUP, LANES), jnp.float32), lse_ref[...])
-        else:
-            before = lse_ref[...]
-        lse_ref[...] = jnp.where(at_head, lse, before)
-
-
-def forward(rows_sorted, tail=None):
-    with_edge = tail is not None
-    rows, width = rows_sorted.shape
-    per_round = rows // 2
-    wide = 2 * DH
-    in_specs = [
-        pl.BlockSpec((per_round, wide), lambda r, p: (r, p)),
-        pl.BlockSpec((per_round, wide), lambda r, p: (r, p + 2)),
-    ]
-    arguments = [rows_sorted, rows_sorted]
-    if with_edge:
-        in_specs += [
-            pl.BlockSpec((GROUP, wide), lambda r, p: (r, p)),
-            pl.BlockSpec((GROUP, wide), lambda r, p: (r, p + 2)),
-        ]
-        arguments += [tail, tail]
+        delta = jnp.sum(partial * cotangent[:, columns].astype(jnp.float32), -1, keepdims=True)
+        head = pair * 2 + local
+        stat = jnp.where(lane == head, lse, jnp.where(lane == head + 4, delta, stat))
+    return stat
+
+
+def own_body(
+    table_ref,
+    arrived_query_ref,
+    arrived_value_ref,
+    arrived_cotangent_ref,
+    tail_query_ref,
+    tail_value_ref,
+    head_query_ref,
+    head_value_ref,
+    head_cotangent_ref,
+    tail_cotangent_ref,
+    out_ref,
+    stat_ref,
+    chosen,
+):
+    pair = pl.program_id(0)
+    hash_round = pl.program_id(1)
+
+    @pl.when((pair == 0) & (hash_round == 0))
+    def _():
+        row = table_row(table_ref, ARRIVAL, SLOT_ROWS)
+        heads, tails = place_cols(table_ref, 0), place_cols(table_ref, 1)
+        for each in range(2):
+            chosen[each] = match_cols(heads[each] + tails[each], row)
+
+    select_head = chosen[hash_round, :GROUP]
+    query = dot(select_head, arrived_query_ref[...]).astype(jnp.bfloat16)
+    value = dot(select_head, arrived_value_ref[...]).astype(jnp.bfloat16)
+    cotangent = dot(chosen[hash_round], arrived_cotangent_ref[...]).astype(jnp.bfloat16)
+    head_query_ref[...] = query
+    head_value_ref[...] = value
+    head_cotangent_ref[...] = cotangent[:GROUP]
+    tail_cotangent_ref[...] = cotangent[GROUP:]
+    stat_ref[...] = forward_pair(
+        pair,
+        tail_query_ref[...],
+        jnp.concatenate([query, tail_query_ref[...]]),
+        jnp.concatenate([value, tail_value_ref[...]]),
+        cotangent[GROUP:],
+        out_ref,
+    )
+
+
+def group_spec(offset=0):
+    return pl.BlockSpec((GROUP, 2 * DH), lambda p, r: (r, p + offset))
+
+
+def stat_spec():
+    return pl.BlockSpec((GROUP, LANES), lambda p, r: (r, p))
+
+
+def forward_own(table, arrived, tail):
+    slots, width = arrived.shape
+    wide = width // 6
+    rows = 2 * GROUP
+    array = jax.ShapeDtypeStruct((rows, width // 3), jnp.bfloat16)
     return pl.pallas_call(
-        functools.partial(forward_body, with_edge),
+        own_body,
         grid=(2, 2),
-        in_specs=in_specs,
+        in_specs=[pl.BlockSpec((LANES, LANES), lambda p, r: (0, 0))]
+        + [pl.BlockSpec((slots, wide), lambda p, r, k=k: (0, p + 2 * k)) for k in range(3)]
+        + [group_spec(), group_spec(2)],
+        out_specs=[group_spec()] * 5 + [stat_spec()],
+        out_shape=[array] * 4
+        + [
+            jax.ShapeDtypeStruct((rows, width // 3), jnp.float32),
+            jax.ShapeDtypeStruct((rows, 2 * LANES), jnp.float32),
+        ],
+        scratch_shapes=[pltpu.VMEM((2, 2 * GROUP, slots), jnp.bfloat16)],
+        compiler_params=params(),
+        cost_estimate=cost(5e9, 1e7, 8 * GROUP * 512),
+        name="forward_own",
+    )(table, arrived, arrived, arrived, tail, tail)
+
+
+def edge_body(
+    table_ref,
+    query_ref,
+    value_ref,
+    cotangent_ref,
+    prior_query_ref,
+    prior_value_ref,
+    second_stat_ref,
+    out_ref,
+    stat_ref,
+    stats_ref,
+    both,
+):
+    pair = pl.program_id(0)
+    hash_round = pl.program_id(1)
+    stat = forward_pair(
+        pair,
+        query_ref[...],
+        jnp.concatenate([prior_query_ref[...], query_ref[...]]),
+        jnp.concatenate([prior_value_ref[...], value_ref[...]]),
+        cotangent_ref[...],
+        out_ref,
+    )
+    stat_ref[...] = stat
+
+    @pl.when(pair == 0)
+    def _():
+        both[hash_round, :GROUP] = stat
+        both[hash_round, GROUP:] = second_stat_ref[...]
+
+    @pl.when(pair == 1)
+    def _():
+        both[hash_round, :GROUP] += stat
+        both[hash_round, GROUP:] += second_stat_ref[...]
+
+    @pl.when((pair == 1) & (hash_round == 1))
+    def _():
+        rows = 4 * GROUP
+        piece = iota((rows, LANES), 1) // (PIECES * STAT)
+        first, second, third = pieces_of(both[...].reshape(rows, LANES))
+        nothing = jnp.zeros((rows, LANES), jnp.bfloat16)
+        stats = jnp.where(
+            piece == 0,
+            first,
+            jnp.where(piece == 1, second, jnp.where(piece == 2, third, nothing)),
+        )
+        place_row = table_row(table_ref, PLACE, PLACE_ROWS)
+        third_slots = stats_ref.shape[0]
+        arrival_cols = table_cols(table_ref, ARRIVAL3, SLOT_ROWS)
+        lane_third = (iota((third_slots, LANES), 1) % (3 * STAT)) // STAT
+        result = jnp.zeros((third_slots, LANES), jnp.float32)
+        for third in range(3):
+            back = match_cols(arrival_cols[4 * third : 4 * third + 4], place_row)
+            result = jnp.where(lane_third == third, dot(back, stats), result)
+        stats_ref[...] = result
+
+
+def forward_edge(table, query, value, cotangent, prior_tail, second_stat):
+    rows, width = query.shape
+    third_slots = SLOT_ROWS * LANES // 3
+    return pl.pallas_call(
+        edge_body,
+        grid=(2, 2),
+        in_specs=[pl.BlockSpec((LANES, LANES), lambda p, r: (0, 0))]
+        + [group_spec()] * 4
+        + [group_spec(2), stat_spec()],
         out_specs=[
-            pl.BlockSpec((GROUP, wide), lambda r, p: (r, p)),
-            pl.BlockSpec((GROUP, LANES), lambda r, p: (r, 0)),
+            group_spec(),
+            stat_spec(),
+            pl.BlockSpec((third_slots, LANES), lambda p, r: (0, 0)),
         ],
         out_shape=[
-            jax.ShapeDtypeStruct((2 * GROUP, width // 2), jnp.float32),
-            jax.ShapeDtypeStruct((2 * GROUP, LANES), jnp.float32),
+            jax.ShapeDtypeStruct((rows, width), jnp.float32),
+            jax.ShapeDtypeStruct((rows, 2 * LANES), jnp.float32),
+            jax.ShapeDtypeStruct((third_slots, LANES), jnp.float32),
         ],
+        scratch_shapes=[pltpu.VMEM((2, 2 * GROUP, LANES), jnp.float32)],
         compiler_params=params(),
-        cost_estimate=cost(8 * 4 * GROUP * 2 * GROUP * DH, 4 * rows * width, 8 * GROUP * 512),
-        name="forward_edge" if with_edge else "forward_own",
-    )(*arguments)
-
-
-def stats_body(
-    table_ref,
-    arrived_ref,
-    out_first_ref,
-    out_second_ref,
-    lse_first_ref,
-    lse_second_ref,
-    sorted_ref,
-    head_ref,
-    stats_ref,
-):
-    rows = sorted_ref.shape[0]
-    per_round = rows // 2
-    place_row = table_row(table_ref, PLACE, PLACE_ROWS)
-    chosen = match_cols(
-        table_cols(table_ref, PLACE, PLACE_ROWS), table_row(table_ref, ARRIVAL, SLOT_ROWS)
-    )
-    cotangent = dot(chosen, arrived_ref[...]).astype(jnp.bfloat16)
-    sorted_ref[...] = cotangent
-    lane = iota((GROUP, LANES), 1)
-    parts = []
-    for hash_round in range(2):
-        kept = slice(hash_round * GROUP, (hash_round + 1) * GROUP)
-        head_ref[kept, :] = cotangent[hash_round * per_round : hash_round * per_round + GROUP]
-        for group, (out_ref, lse_ref) in enumerate(
-            ((out_first_ref, lse_first_ref), (out_second_ref, lse_second_ref))
-        ):
-            start = hash_round * per_round + group * GROUP
-            wide = cotangent[start : start + GROUP].astype(jnp.float32)
-            product = wide * out_ref[kept, :]
-            stat = lse_ref[kept, :]
-            for head in range(4):
-                own = jnp.sum(product[:, head * DH : (head + 1) * DH], -1, keepdims=True)
-                stat = jnp.where(lane % STAT == 4 + head, own, stat)
-            first, second, third = pieces_of(stat)
-            piece = lane // (PIECES * STAT)
-            parts.append(
-                jnp.where(
-                    piece == 0,
-                    first.astype(jnp.float32),
-                    jnp.where(
-                        piece == 1,
-                        second.astype(jnp.float32),
-                        jnp.where(piece == 2, third.astype(jnp.float32), 0.0),
-                    ),
-                ).astype(jnp.bfloat16)
-            )
-    stats = jnp.concatenate(parts)
-    third_slots = stats_ref.shape[0]
-    arrival_cols = table_cols(table_ref, ARRIVAL3, SLOT_ROWS)
-    lane_third = (iota((third_slots, LANES), 1) % (3 * STAT)) // STAT
-    result = jnp.zeros((third_slots, LANES), jnp.float32)
-    for third in range(3):
-        back = match_cols(arrival_cols[4 * third : 4 * third + 4], place_row)
-        result = jnp.where(lane_third == third, dot(back, stats), result)
-    stats_ref[...] = result
-
-
-def stats_out(table, arrived, outs, lses):
-    slots, width = arrived.shape
-    rows = PLACE_ROWS * LANES
-    return pl.pallas_call(
-        stats_body,
-        out_shape=[
-            jax.ShapeDtypeStruct((rows, width), jnp.bfloat16),
-            jax.ShapeDtypeStruct((2 * GROUP, width), jnp.bfloat16),
-            jax.ShapeDtypeStruct((slots // 3, LANES), jnp.float32),
-        ],
-        compiler_params=params(),
-        cost_estimate=cost(2 * slots * rows * (width + LANES), 4 * slots * width),
-        name="cotangent_and_stats",
-    )(table, arrived, *outs, *lses)
+        cost_estimate=cost(2e9, 4e6, 8 * GROUP * 512),
+        name="forward_edge",
+    )(table, query, value, cotangent, prior_tail, prior_tail, second_stat)
 
 
 def gather_stats(codes_row, slot_cols, stats):
@@ -395,11 +420,14 @@
 def backward_body(
     table_ref,
     stats_ref,
-    query_ref,
-    value_ref,
-    cotangent_ref,
+    head_query_ref,
     tail_query_ref,
+    head_value_ref,
     tail_value_ref,
+    head_cotangent_ref,
+    tail_cotangent_ref,
+    prior_query_ref,
+    prior_value_ref,
     next_query_ref,
     next_cotangent_ref,
     out_first_ref,
@@ -451,15 +479,17 @@
         head = pair * 2 + local
         total_row, delta_row = row_of(stat, head), row_of(stat, head + 4)
         edge_total, edge_delta = row_of(edge_stat, head), row_of(edge_stat, head + 4)
-        raw = query_ref[:, columns]
-        values = value_ref[:, columns]
-        upstream = cotangent_ref[:, columns]
+        raw = jnp.concatenate([head_query_ref[:, columns], tail_query_ref[:, columns]])
+        values = jnp.concatenate([head_value_ref[:, columns], tail_value_ref[:, columns]])
+        upstream = jnp.concatenate(
+            [head_cotangent_ref[:, columns], tail_cotangent_ref[:, columns]]
+        )
         units, inverse = unit_rows(raw)
         keys = units.astype(jnp.bfloat16)
-        tail_keys = unit_rows(tail_query_ref[:, columns])[0].astype(jnp.bfloat16)
+        tail_keys = unit_rows(prior_query_ref[:, columns])[0].astype(jnp.bfloat16)
 
         keys_first = jnp.concatenate([tail_keys, keys[:GROUP]])
-        values_first = jnp.concatenate([tail_value_ref[:, columns], values[:GROUP]])
+        values_first = jnp.concatenate([prior_value_ref[:, columns], values[:GROUP]])
         probs, slopes = backward_tile(
             raw[:GROUP],
             upstream[:GROUP],
@@ -542,8 +572,8 @@
         payload_ref[...] += dot(back[:, per_round:], shaped[...]).astype(jnp.bfloat16)
 
 
-def backward(table, stats, rows_sorted, cotangent, tail, next_query, next_cotangent, outs, lses):
-    rows, width = rows_sorted.shape
+def backward(table, stats, heads, tail, tail_cotangent, prior_tail, nexts, outs, lses):
+    rows = PLACE_ROWS * LANES
     per_round = rows // 2
     slots = SLOT_ROWS * LANES
     wide = 2 * DH
@@ -552,25 +582,17 @@
         return pl.BlockSpec(array.shape, lambda p, r: (0,) * array.ndim)
 
     small = [table, stats]
-    group_spec = pl.BlockSpec((GROUP, wide), lambda p, r: (r, p))
-    lse_spec = pl.BlockSpec((GROUP, LANES), lambda p, r: (r, 0))
+    head_query, head_value, head_cotangent = heads
     return pl.pallas_call(
         backward_body,
         grid=(2, 2),
         in_specs=[whole(array) for array in small]
-        + [
-            pl.BlockSpec((per_round, wide), lambda p, r: (r, p)),
-            pl.BlockSpec((per_round, wide), lambda p, r: (r, p + 2)),
-            pl.BlockSpec((per_round, wide), lambda p, r: (r, p)),
-            group_spec,
-            pl.BlockSpec((GROUP, wide), lambda p, r: (r, p + 2)),
-            group_spec,
-            group_spec,
-            group_spec,
-            group_spec,
-            lse_spec,
-            lse_spec,
-        ],
+        + [group_spec()] * 3
+        + [group_spec(2)]
+        + [group_spec()] * 3
+        + [group_spec(2)]
+        + [group_spec()] * 4
+        + [stat_spec()] * 2,
         out_specs=pl.BlockSpec((slots, 3 * wide), lambda p, r: (0, p)),
         out_shape=jax.ShapeDtypeStruct((slots, 6 * wide), jnp.bfloat16),
         scratch_shapes=[
@@ -585,13 +607,15 @@
         name="backward",
     )(
         *small,
-        rows_sorted,
-        rows_sorted,
-        cotangent,
+        head_query,
         tail,
+        head_value,
         tail,
-        next_query,
-        next_cotangent,
+        head_cotangent,
+        tail_cotangent,
+        prior_tail,
+        prior_tail,
+        *nexts,
         *outs,
         *lses,
     )
@@ -652,8 +676,320 @@
     send = by_owner(send_rows)
     send_blocks = send.reshape(6, 2, LANES)
     send_blocks = jnp.pad(send_blocks, ((0, 0), (0, STAT - 2), (0, 0))).reshape(-1, LANES)
-    packed = pack(send_blocks, query_key, value)
-    packed_cotangent = pack(send_blocks, attended_cotangent)
+    packed = pack(send_blocks, query_key, value, attended_cotangent)
+
+    within = jnp.arange(capacity, dtype=jnp.int32)
+
+    def arrivals(counts):
+        start = jnp.cumsum(counts, axis=1) - counts + code
+        codes = jnp.where(within < counts[:, :, None], start[:, :, None] + within, -1)
+        return by_owner(codes)
+
+    arrival = arrivals(to_place(arrival_count))
+    next_arrival = arrivals(to_place_prior(arrival_count))
+    place = to_place(receive_slot) + code
+    next_place = to_place_prior(receive_slot[:, :GROUP]) + code
+    table = jnp.concatenate(
+        [first] * 3 + [second] * 3 + [third_piece] * 3 + [spare]
+    ).astype(jnp.bfloat16)
+    third_slots = arrived_ref.shape[0]
+    lane_third = (iota((third_slots, LANES), 1) % (3 * STAT)) // STAT
+    result = jnp.zeros((third_slots, LANES), jnp.float32)
+    for third in range(3):
+        codes = slot_cols[4 * third : 4 * third + 4]
+        cols = [jnp.where(code >= tokens, code - tokens, code) for code in codes]
+        chosen = match_cols(cols, iota((LANES, tokens), 1))
+        result = jnp.where(lane_third == third, dot(chosen, table, 1, 1), result)
+    owners = third_slots // STAT
+    by_owner = result.reshape(owners, STAT, LANES)
+    out_ref[:, :STAT, :] = by_owner
+    above = jnp.concatenate([by_owner[1:], by_owner[:1]])
+    below = jnp.concatenate([by_owner[owners - 1 :], by_owner[: owners - 1]])
+    half = table_ref[HALF : HALF + 1, :]
+    out_ref[:, STAT:, :] = jnp.where(half[None] == 0, above, below)
+
+
+def total_stats(table, arrived, tokens):
+    owners = arrived.shape[0] // STAT
+    return pl.pallas_call(
+        functools.partial(total_body, tokens),
+        out_shape=jax.ShapeDtypeStruct((owners, 2 * STAT, LANES), jnp.float32),
+        compiler_params=params(),
+        cost_estimate=cost(2 * 1536 * 1536 * LANES, 1 << 20),
+        name="total_stats",
+    )(table, arrived)
+
+
+def backward_tile(query, upstream, keys, values, masked, total_row, delta_row):
+    scores = dot(keys, query, 1, 1)
+    if masked is not None:
+        scores = jnp.where(masked, NEG_SELF, scores)
+    probs = jnp.exp(scores - total_row)
+    dots = dot(values, upstream, 1, 1)
+    slopes = (probs * (dots - delta_row)).astype(jnp.bfloat16)
+    return probs.astype(jnp.bfloat16), slopes
+
+
+def backward_body(
+    table_ref,
+    stats_ref,
+    head_query_ref,
+    tail_query_ref,
+    head_value_ref,
+    tail_value_ref,
+    head_cotangent_ref,
+    tail_cotangent_ref,
+    prior_query_ref,
+    prior_value_ref,
+    next_query_ref,
+    next_cotangent_ref,
+    out_first_ref,
+    out_second_ref,
+    lse_first_ref,
+    lse_second_ref,
+    payload_ref,
+    back,
+    totals,
+    next_totals,
+    total_cols,
+    shaped,
+):
+    pair = pl.program_id(0)
+    hash_round = pl.program_id(1)
+    rows = PLACE_ROWS * LANES
+    per_round = rows // 2
+
+    @pl.when((pair == 0) & (hash_round == 0))
+    def _():
+        place_row = table_row(table_ref, PLACE, PLACE_ROWS)
+        next_row = table_row(table_ref, NEXT_PLACE, NEXT_ROWS)
+        back[...] = match_cols(table_cols(table_ref, ARRIVAL, SLOT_ROWS), place_row)
+        own_stats = stats_ref[:, :STAT, :].reshape(-1, LANES)
+        next_stats = stats_ref[:, STAT:, :].reshape(-1, LANES)
+        found = gather_stats(place_row, table_cols(table_ref, ARRIVAL3, SLOT_ROWS), own_stats)
+        edge = gather_stats(next_row, table_cols(table_ref, NEXT3, SLOT_ROWS), next_stats)
+        for each in range(2):
+            totals[each] = found[:, each * per_round : (each + 1) * per_round]
+            next_totals[each] = edge[:, each * GROUP : (each + 1) * GROUP]
+        padded = jnp.concatenate([found, jnp.zeros((LANES - STAT, rows), jnp.float32)])
+        total_cols[...] = padded.T.reshape(2, per_round, LANES)
+
+    own = iota((2 * GROUP, GROUP), 0) == iota((2 * GROUP, GROUP), 1) + GROUP
+    stat = totals[hash_round]
+    edge_stat = next_totals[hash_round]
+    columns_of_stat = total_cols[hash_round]
+    sublane = iota((STAT, 1), 0)
+    lane = iota((1, LANES), 1)
+
+    def row_of(table, index):
+        return jnp.sum(jnp.where(sublane == index, table, 0.0), 0, keepdims=True)
+
+    def col_of(table, index):
+        return jnp.sum(jnp.where(lane == index, table, 0.0), 1, keepdims=True)
+
+    for local in range(2):
+        columns = slice(local * DH, (local + 1) * DH)
+        head = pair * 2 + local
+        total_row, delta_row = row_of(stat, head), row_of(stat, head + 4)
+        edge_total, edge_delta = row_of(edge_stat, head), row_of(edge_stat, head + 4)
+        raw = jnp.concatenate([head_query_ref[:, columns], tail_query_ref[:, columns]])
+        values = jnp.concatenate([head_value_ref[:, columns], tail_value_ref[:, columns]])
+        upstream = jnp.concatenate(
+            [head_cotangent_ref[:, columns], tail_cotangent_ref[:, columns]]
+        )
+        units, inverse = unit_rows(raw)
+        keys = units.astype(jnp.bfloat16)
+        tail_keys = unit_rows(prior_query_ref[:, columns])[0].astype(jnp.bfloat16)
+
+        keys_first = jnp.concatenate([tail_keys, keys[:GROUP]])
+        values_first = jnp.concatenate([prior_value_ref[:, columns], values[:GROUP]])
+        probs, slopes = backward_tile(
+            raw[:GROUP],
+            upstream[:GROUP],
+            keys_first,
+            values_first,
+            own,
+            total_row[:, :GROUP],
+            delta_row[:, :GROUP],
+        )
+        query_first = dot(slopes, keys_first, 0, 0)
+        unit_first = dot(slopes[GROUP:], raw[:GROUP])
+        value_first = dot(probs[GROUP:], upstream[:GROUP])
+
+        probs, slopes = backward_tile(
+            raw[GROUP:],
+            upstream[GROUP:],
+            keys,
+            values,
+            own,
+            total_row[:, GROUP:],
+            delta_row[:, GROUP:],
+        )
+        query_second = dot(slopes, keys, 0, 0)
+        unit_both = dot(slopes, raw[GROUP:])
+        value_both = dot(probs, upstream[GROUP:])
+
+        next_query = next_query_ref[:, columns]
+        next_upstream = next_cotangent_ref[:, columns]
+        probs, slopes = backward_tile(
+            next_query,
+            next_upstream,
+            keys[GROUP:],
+            values[GROUP:],
+            None,
+            edge_total,
+            edge_delta,
+        )
+        unit_last = dot(slopes, next_query)
+        value_last = dot(probs, next_upstream)
+
+        for group, (query_slope, unit_slope, value_slope, out_ref, lse_ref) in enumerate(
+            (
+                (
+                    query_first,
+                    unit_first + unit_both[:GROUP],
+                    value_first + value_both[:GROUP],
+                    out_first_ref,
+                    lse_first_ref,
+                ),
+                (
+                    query_second,
+                    unit_both[GROUP:] + unit_last,
+                    value_both[GROUP:] + value_last,
+                    out_second_ref,
+                    lse_second_ref,
+                ),
+            )
+        ):
+            kept = slice(group * GROUP, (group + 1) * GROUP)
+            unit = units[kept]
+            key_slope = inverse[kept] * (
+                unit_slope - unit * jnp.sum(unit * unit_slope, -1, keepdims=True)
+            )
+            share = jnp.exp(col_of(lse_ref[...] - columns_of_stat[kept], head))
+            wide = 2 * DH
+            shaped[kept, columns] = (out_ref[:, columns] * share).astype(jnp.bfloat16)
+            shaped[kept, wide + local * DH : wide + (local + 1) * DH] = (
+                query_slope + key_slope
+            ).astype(jnp.bfloat16)
+            shaped[kept, 2 * wide + local * DH : 2 * wide + (local + 1) * DH] = (
+                value_slope.astype(jnp.bfloat16)
+            )
+
+    @pl.when(hash_round == 0)
+    def _():
+        payload_ref[...] = dot(back[:, :per_round], shaped[...]).astype(jnp.bfloat16)
+
+    @pl.when(hash_round == 1)
+    def _():
+        payload_ref[...] += dot(back[:, per_round:], shaped[...]).astype(jnp.bfloat16)
+
+
+def backward(table, stats, heads, tail, tail_cotangent, prior_tail, nexts, outs, lses):
+    rows = PLACE_ROWS * LANES
+    per_round = rows // 2
+    slots = SLOT_ROWS * LANES
+    wide = 2 * DH
+
+    def whole(array):
+        return pl.BlockSpec(array.shape, lambda p, r: (0,) * array.ndim)
+
+    small = [table, stats]
+    head_query, head_value, head_cotangent = heads
+    return pl.pallas_call(
+        backward_body,
+        grid=(2, 2),
+        in_specs=[whole(array) for array in small]
+        + [group_spec()] * 3
+        + [group_spec(2)]
+        + [group_spec()] * 3
+        + [group_spec(2)]
+        + [group_spec()] * 4
+        + [stat_spec()] * 2,
+        out_specs=pl.BlockSpec((slots, 3 * wide), lambda p, r: (0, p)),
+        out_shape=jax.ShapeDtypeStruct((slots, 6 * wide), jnp.bfloat16),
+        scratch_shapes=[
+            pltpu.VMEM((slots, rows), jnp.bfloat16),
+            pltpu.VMEM((2, STAT, per_round), jnp.float32),
+            pltpu.VMEM((2, STAT, GROUP), jnp.float32),
+            pltpu.VMEM((2, per_round, LANES), jnp.float32),
+            pltpu.VMEM((per_round, 3 * wide), jnp.bfloat16),
+        ],
+        compiler_params=params(),
+        cost_estimate=cost(8e9, 1.5e7, 3e6),
+        name="backward",
+    )(
+        *small,
+        head_query,
+        tail,
+        head_value,
+        tail,
+        head_cotangent,
+        tail_cotangent,
+        prior_tail,
+        prior_tail,
+        *nexts,
+        *outs,
+        *lses,
+    )
+
+
+def combine_body(table_ref, arrived_ref, *out_refs):
+    tokens, wide = out_refs[0].shape
+    chosen = match(iota((tokens, 1), 0), table_row(table_ref, SEND, SLOT_ROWS))
+    found = dot(chosen, arrived_ref[...])
+    for place, out_ref in enumerate(out_refs):
+        out_ref[...] = found[:, place * wide : (place + 1) * wide].astype(jnp.bfloat16)
+
+
+def combine(table, arrived, tokens):
+    slots, width = arrived.shape
+    wide = width // 6
+    return pl.pallas_call(
+        combine_body,
+        grid=(2,),
+        in_specs=[
+            pl.BlockSpec((LANES, LANES), lambda i: (0, 0)),
+            pl.BlockSpec((slots, 3 * wide), lambda i: (0, i)),
+        ],
+        out_specs=[pl.BlockSpec((tokens, wide), lambda i: (0, i))] * 3,
+        out_shape=[jax.ShapeDtypeStruct((tokens, 2 * wide), jnp.bfloat16)] * 3,
+        compiler_params=params(),
+        cost_estimate=cost(2 * slots * tokens * width, 2 * (slots + tokens) * width),
+        name="combine_rows",
+    )(table, arrived)
+
+
+def per_device(query_key, value, attended_cotangent, send_rows, arrival_count, receive_slot):
+    tokens, row_width = query_key.shape
+    rounds = send_rows.shape[0]
+    owners = lax.axis_size("seq")
+    capacity = send_rows.shape[1] // owners
+    per_owner = rounds * capacity
+    slots = owners * per_owner
+
+    code = (tokens * jnp.arange(rounds, dtype=jnp.int32))[:, None]
+    half = lax.axis_index("head")
+
+    def by_owner(table):
+        return table.reshape(rounds, owners, capacity).transpose(1, 0, 2).reshape(owners, per_owner)
+
+    def by_third(codes):
+        return codes.reshape(owners, 3, STAT).transpose(1, 0, 2)
+
+    def rows_of(codes, count):
+        rows = codes.reshape(-1, LANES)
+        return jnp.pad(rows, ((0, count - rows.shape[0]), (0, 0)), constant_values=-1)
+
+    def sent(packed):
+        return exchange(packed.reshape(owners, per_owner, -1)).reshape(slots, -1)
+
+    blocks = send_rows.reshape(rounds, owners, capacity)
+    send_rows = jnp.where(half == 0, blocks, blocks[:, ::-1]).reshape(rounds, -1)
+    send = by_owner(send_rows)
+    send_blocks = send.reshape(6, 2, LANES)
+    send_blocks = jnp.pad(send_blocks, ((0, 0), (0, STAT - 2), (0, 0))).reshape(-1, LANES)
+    packed = pack(send_blocks, query_key, value, attended_cotangent)
 
     arrival_count = to_place(arrival_count)
     receive_slot = to_place(receive_slot)
@@ -678,27 +1014,28 @@
     )
 
     arrived, table = lax.optimization_barrier((sent(packed), table))
-    rows_sorted, tail, head_query = sort_rows(table, arrived)
+    tail = sort_tail(table, arrived, 2 * row_width)
     prior_tail = to_next(tail)
-    arrived_cotangent = sent(packed_cotangent)
+    head_query, head_value, head_cotangent, tail_cotangent, out_second, stat_second = forward_own(
+        table, arrived, tail
+    )
+    out_first, stat_first, stats = forward_edge(
+        table, head_query, head_value, head_cotangent, prior_tail, stat_second
+    )
     next_query = to_prior(head_query)
-    out_second, lse_second = forward(rows_sorted)
-    out_first, lse_first = forward(rows_sorted, prior_tail)
-    outs, lses = (out_first, out_second), (lse_first, lse_second)
-    cotangent, head_cotangent, stats = stats_out(table, arrived_cotangent, outs, lses)
     next_cotangent = to_prior(head_cotangent)
     home_stats = exchange(stats.reshape(owners, STAT, LANES)).reshape(-1, LANES)
     totals = exchange(total_stats(table, home_stats, tokens))
     payload = backward(
         table,
         totals,
-        rows_sorted,
-        cotangent,
+        (head_query, head_value, head_cotangent),
+        tail,
+        tail_cotangent,
         prior_tail,
-        next_query,
-        next_cotangent,
-        outs,
-        lses,
+        (next_query, next_cotangent),
+        (out_first, out_second),
+        (stat_first, stat_second),
     )
     return tuple(combine(table, sent(payload), tokens))
 

time: 244 us -> 246 us (level)
  waiting for transfers between devices: 59.7 us -> 72.3 us
  starting transfers between devices: 49.7 us -> 42 us
  Pallas kernels: 64.2 us -> 58.7 us
  blocking collectives: 62 us -> 65 us
    ppermute x7, waiting for transfers between devices: 41 us -> 49.1 us  [routed(): return lax.ppermute(block, ('seq', 'head'), route)]
    all_to_all x4 -> x3, starting transfers between devices: 30.5 us -> 24.3 us  [exchange(): return lax.all_to_all(block, 'seq', split_axis=0, concat_axis=0, tiled=True)]
    all_to_all x4 -> x3, waiting for transfers between devices: 18.7 us -> 23.2 us  [exchange(): return lax.all_to_all(block, 'seq', split_axis=0, concat_axis=0, tiled=True)]
    pallas_call x2 -> x1, Pallas kernels: 11.2 us -> 6.94 us  [pack(): pl.pallas_call(pack_body, grid=(steps,), in_specs=[pl.BlockSpec((STAT, LA...]
    all_to_all x1, blocking collectives: 62 us -> 65 us  [exchange(): return lax.all_to_all(block, 'seq', split_axis=0, concat_axis=0, tiled=True)]
    pallas_call x4 -> x3, Pallas kernels: 26.2 us -> 24.9 us  [the longest x1 11.2 us: forward_own(): pl.pallas_call(own_body, grid=(2, 2), in_specs=[pl.BlockSpec((LANES, LANE...]
  transfers between devices with their start and end apart: 11 -> 10, of which waited for: 6 -> 6; matrix products, arithmetic and copies ran while one was open for 1% -> 1% of each run, Pallas kernels for 12% -> 6%
where the time goes in v3:
time: 246 us; the launch traced here: 245 us
  waiting for transfers between devices  72.3 us (29%)
  blocking collectives  65 us (26%)
  Pallas kernels  58.7 us (24%)
  starting transfers between devices  42 us (17%)
  local copies, waits for them, and re-layouts  5.39 us (2%)
    all_to_all x1, blocking collectives, exchange(): return lax.all_to_all(block, 'seq', split_axis=0, concat_axis=0, tiled=True)  65 us
    ppermute x7, waiting for transfers between devices, routed(): return lax.ppermute(block, ('seq', 'head'), route)  49.1 us
    all_to_all x3, starting transfers between devices, exchange(): return lax.all_to_all(block, 'seq', split_axis=0, concat_axis=0, tiled=True)  24.3 us
    all_to_all x3, waiting for transfers between devices, exchange(): return lax.all_to_all(block, 'seq', split_axis=0, concat_axis=0, tiled=True)  23.2 us
    pallas_call x1, Pallas kernels, backward(): pl.pallas_call(backward_body, grid=(2, 2), in_specs=[whole(array) for arr...  18.4 us
    ppermute x7, starting transfers between devices, routed(): return lax.ppermute(block, ('seq', 'head'), route)  17.8 us
    pallas_call x1, Pallas kernels, forward_own(): pl.pallas_call(own_body, grid=(2, 2), in_specs=[pl.BlockSpec((LANES, LANE...  11.2 us
    pallas_call x1, Pallas kernels, forward_edge(): pl.pallas_call(edge_body, grid=(2, 2), in_specs=[pl.BlockSpec((LANES, LAN...  8.29 us
  transfers between devices with their start and end apart: 10, of which 6 were waited for; matrix products, arithmetic and copies ran while one was open for 1% of the time, Pallas kernels for 6%

profile of v3, /device:TPU:0, one launch (start us, length us, event | category | flops | bytes accessed | tf_op | source)
XLA Modules:
  0.0 244.9 jit_solution(11192862853944810858)
XLA Ops:
  0.6 0.8 reshape.78
  2.4 6.9 %pack_rows.1 = bf16[1536,1536]{1,0:T(8,128)(2,1)} custom-call(s32[48,128]{1,0:T(8,128)} %pad_bitcast_fusion.index_ref, bf16[512,512]{1,0:T(8,128)(2,1)} %refs_0_.1, bf16[512,512]{1,0:T(8,128)(2,1)} %refs_1_.1, bf16[512,512]{1,0:T(8,128)(2,1)} %refs_2_.1), custom_call_target="tpu_custom_call" | custom-call | flops 2415919104 | bytes 6291456 | tf_op jit(solution)/shard_map/pack_rows/pallas_call | solution.py:124
  9.3 11.9 %all-to-all-start = ((bf16[64,24,1536]{2,1,0:T(8,128)(2,1)}), bf16[64,24,1536]{2,1,0:T(8,128)(2,1)}, u32[]{:S(2)}, u32[]{:S(2)}) async-start(bf16[64,24,1536]{2,1,0:T(8,128)(2,1)} %bitcast.31), calls=%async_computation | async-start | bytes 9437184 | tf_op jit(solution)/shard_map/all_to_all | solution.py:64
  23.6 7.3 %collective-permute-start.1 = (s32[64,24]{0,1:T(8,128)S(1)}, s32[64,24]{0,1:T(8,128)S(1)}, u32[]{:S(2)}, u32[]{:S(2)}) collective-permute-start(s32[64,24]{0,1:T(8,128)S(1)} %add_select_fusion.1), channel_id=1, source_target_pairs={{0,126},{1,3},{2,0},{3,5},{4,2},{5,7},{6,4},{7,9},{8,6},{9,11},{10... | collective-permute-start | bytes 18440 | tf_op jit(solution)/shard_map/ppermute | solution.py:44
  31.5 0.9 collective-permute-start.3
  32.4 39.6 %collective-permute-done.3 = s32[2,256]{1,0:T(2,128)S(1)} collective-permute-done((s32[2,256]{1,0:T(2,128)S(1)}, s32[2,256]{1,0:T(2,128)S(1)}, u32[]{:S(2)}, u32[]{:S(2)}) %collective-permute-start.3) | collective-permute-done | bytes 2080 | tf_op jit(solution)/shard_map/ppermute | solution.py:44
  72.3 7.5 %all-to-all-done = bf16[64,24,1536]{2,1,0:T(8,128)(2,1)} async-done(((bf16[64,24,1536]{2,1,0:T(8,128)(2,1)}), bf16[64,24,1536]{2,1,0:T(8,128)(2,1)}, u32[]{:S(2)}, u32[]{:S(2)}) %all-to-all-start) | async-done | bytes 4718624 | tf_op jit(solution)/shard_map/all_to_all | solution.py:64
  79.7 5.3 %sort_tail.1.tail_query_ref.tail_value_ref = bf16[512,1024]{1,0:T(8,128)(2,1)} custom-call(s32[128,128]{1,0:T(8,128)} %copy-done.2, bf16[1536,1536]{1,0:T(8,128)(2,1)} %bitcast.3.arrived_ref.arrived_query_ref.arrived_value_ref.arrived_cotangent_ref), custom_call_target="tpu_custom_call" | custom-call | flops 1610612736 | bytes 4194304 | tf_op jit(solution)/shard_map/sort_tail/pallas_call | solution.py:156
  85.2 11.2 %forward_own.1 = (bf16[512,512]{1,0:T(8,128)(2,1)}, bf16[512,512]{1,0:T(8,128)(2,1)}, bf16[512,512]{1,0:T(8,128)(2,1)}, bf16[512,512]{1,0:T(8,128)(2,1)}, f32[512,512]{1,0:T(8,128)}, /*index=5*/f32[512,256]{1,0:T(8,128)}) custom-call(s32[128,128]{1,0:T(8,128)} %copy-done.2, ...), custom_call_target="tpu_custom_call" | custom-call | flops 5000000000 | bytes 10000000 | tf_op jit(solution)/shard_map/forward_own/pallas_call | solution.py:253
  96.4 9.1 %collective-permute-done.4.prior_query_ref.prior_value_ref = bf16[512,1024]{1,0:T(8,128)(2,1)S(1)} collective-permute-done((bf16[512,1024]{1,0:T(8,128)(2,1)}, bf16[512,1024]{1,0:T(8,128)(2,1)S(1)}, u32[]{:S(2)}, u32[]{:S(2)}) %collective-permute-start.4) | collective-permute-done | bytes 1048608 | tf_op jit(solution)/shard_map/ppermute | solution.py:44
  105.5 1.0 copy-done.3
  106.5 8.3 %forward_edge.1 = (f32[512,512]{1,0:T(8,128)}, f32[512,256]{1,0:T(8,128)}, f32[512,128]{1,0:T(8,128)}) custom-call(s32[128,128]{1,0:T(8,128)} %copy-done.2, bf16[512,512]{1,0:T(8,128)(2,1)} %get-tuple-element.16.query_ref.head_query_ref, bf16[512,512]{1,0:T(8,128)(2,1)} %get-tuple-element.17.value_ref.head_value_ref, ...), custom_call_target="tpu_custom_call" | custom-call | flops 2000000000 | bytes 4000000 | tf_op jit(solution)/shard_map/forward_edge/pallas_call | solution.py:332
  114.8 7.3 %all-to-all-start.1 = ((f32[64,8,128]{2,1,0:T(8,128)}), f32[64,8,128]{2,1,0:T(8,128)S(1)}, u32[]{:S(2)}, u32[]{:S(2)}) async-start(f32[64,8,128]{2,1,0:T(8,128)} %bitcast.35), calls=%async_computation.1 | async-start | bytes 524288 | tf_op jit(solution)/shard_map/all_to_all | solution.py:64
  122.1 7.4 %collective-permute-start.5 = (bf16[512,512]{1,0:T(8,128)(2,1)}, bf16[512,512]{1,0:T(8,128)(2,1)S(1)}, u32[]{:S(2)}, u32[]{:S(2)}) collective-permute-start(bf16[512,512]{1,0:T(8,128)(2,1)} %get-tuple-element.16.query_ref.head_query_ref), channel_id=1, source_target_pairs={{0,126},{1,3},{2,0},{3,5},{4,2},{5,7},{6,4},{7,9},{8,6},{9,11},{10... | collective-permute-start | bytes 1572872 | tf_op jit(solution)/shard_map/ppermute | solution.py:44
  129.5 0.9 collective-permute-start.6
  130.4 2.4 all-to-all-done.1
  132.7 0.7 copy-done.1
  133.4 3.2 %total_stats.1 = f32[64,16,128]{2,1,0:T(8,128)} custom-call(s32[128,128]{1,0:T(8,128)} %copy-done.2, f32[512,128]{1,0:T(8,128)} %bitcast.34), custom_call_target="tpu_custom_call" | custom-call | flops 603979776 | bytes 1048576 | tf_op jit(solution)/shard_map/total_stats/pallas_call | solution.py:714
  136.6 5.1 %all-to-all-start.2 = ((f32[64,16,128]{2,1,0:T(8,128)}), f32[64,16,128]{2,1,0:T(8,128)S(1)}, u32[]{:S(2)}, u32[]{:S(2)}) async-start(f32[64,16,128]{2,1,0:T(8,128)} %total_stats.1), calls=%async_computation.2 | async-start | bytes 1048576 | tf_op jit(solution)/shard_map/all_to_all | solution.py:64
  142.2 13.4 %all-to-all-done.2.stats_ref = f32[64,16,128]{2,1,0:T(8,128)S(1)} async-done(((f32[64,16,128]{2,1,0:T(8,128)}), f32[64,16,128]{2,1,0:T(8,128)S(1)}, u32[]{:S(2)}, u32[]{:S(2)}) %all-to-all-start.2) | async-done | bytes 524320 | tf_op jit(solution)/shard_map/all_to_all | solution.py:64
  155.5 0.8 copy-done
  156.3 18.4 %backward.1 = bf16[1536,1536]{1,0:T(8,128)(2,1)} custom-call(s32[128,128]{1,0:T(8,128)} %copy-done.2, f32[64,16,128]{2,1,0:T(8,128)} %copy-done, bf16[512,512]{1,0:T(8,128)(2,1)} %get-tuple-element.16.query_ref.head_query_ref, bf16[512,1024]{1,0:T(8,128)(2,1)} %sort_tail.1.tail_query_ref.tail_value_ref, ...), custom_call_target="tpu_custom_call" | custom-call | flops 8000000000 | bytes 15000000 | tf_op jit(solution)/shard_map/backward/pallas_call | solution.py:899
  174.7 65.0 %all_to_all.20 = bf16[64,24,1536]{2,1,0:T(8,128)(2,1)} all-to-all(bf16[64,24,1536]{2,1,0:T(8,128)(2,1)} %bitcast.32), channel_id=1, replica_groups=mesh['seq'=64,'head'=2] {'seq'}, dimensions={0} | all-to-all | bytes 9437184 | tf_op jit(solution)/shard_map/all_to_all | solution.py:64
  239.7 5.3 %combine_rows.1 = (bf16[512,512]{1,0:T(8,128)(2,1)}, bf16[512,512]{1,0:T(8,128)(2,1)}, bf16[512,512]{1,0:T(8,128)(2,1)}) custom-call(s32[128,128]{1,0:T(8,128)} %copy-done.2, bf16[1536,1536]{1,0:T(8,128)(2,1)} %bitcast.33), custom_call_target="tpu_custom_call" | custom-call | flops 2415919104 | bytes 6291456 | tf_op jit(solution)/shard_map/combine_rows/pallas_call | solution.py:948
  (65 shorter events, 4.6 us)
Async XLA Ops:
  9.3 11.9 %copy-start.7 = (s32[2,64]{1,0:T(2,128)S(1)}, s32[2,64]{1,0:T(2,128)}, u32[]{:S(2)}) copy-start(s32[2,64]{1,0:T(2,128)} %param.10) | copy-start | bytes 1540
  9.3 12.5 %copy-start.6 = (s32[2,512]{1,0:T(2,128)S(1)}, s32[2,512]{1,0:T(2,128)}, u32[]{:S(2)}) copy-start(s32[2,512]{1,0:T(2,128)} %param.11) | copy-start | bytes 12292
  9.3 70.4 %all-to-all-start = ((bf16[64,24,1536]{2,1,0:T(8,128)(2,1)}), bf16[64,24,1536]{2,1,0:T(8,128)(2,1)}, u32[]{:S(2)}, u32[]{:S(2)}) async-start(bf16[64,24,1536]{2,1,0:T(8,128)(2,1)} %bitcast.31), calls=%async_computation | async-start | bytes 9437184 | tf_op jit(solution)/shard_map/all_to_all | solution.py:64
  21.2 2.0 collective-permute-start
  21.9 9.5 %collective-permute-start.2 = (s32[2,512]{1,0:T(2,128)S(1)}, s32[2,512]{1,0:T(2,128)S(1)}, u32[]{:S(2)}, u32[]{:S(2)}) collective-permute-start(s32[2,512]{1,0:T(2,128)S(1)} %copy-done.6), channel_id=1, source_target_pairs={{0,0},{1,127},{2,2},{3,125},{4,4},{5,123},{6,6},{7,121},{8,8},{9,1... | collective-permute-start | bytes 12296 | tf_op jit(solution)/shard_map/ppermute | solution.py:44
  23.6 48.4 %collective-permute-start.1 = (s32[64,24]{0,1:T(8,128)S(1)}, s32[64,24]{0,1:T(8,128)S(1)}, u32[]{:S(2)}, u32[]{:S(2)}) collective-permute-start(s32[64,24]{0,1:T(8,128)S(1)} %add_select_fusion.1), channel_id=1, source_target_pairs={{0,126},{1,3},{2,0},{3,5},{4,2},{5,7},{6,4},{7,9},{8,6},{9,11},{10... | collective-permute-start | bytes 18440 | tf_op jit(solution)/shard_map/ppermute | solution.py:44
  31.5 40.5 %collective-permute-start.3 = (s32[2,256]{1,0:T(2,128)S(1)}, s32[2,256]{1,0:T(2,128)S(1)}, u32[]{:S(2)}, u32[]{:S(2)}) collective-permute-start(s32[2,256]{1,0:T(2,128)S(1)} %slice.4), channel_id=1, source_target_pairs={{0,126},{1,3},{2,0},{3,5},{4,2},{5,7},{6,4},{7,9},{8,6},{9,11},{10... | collective-permute-start | bytes 6152 | tf_op jit(solution)/shard_map/ppermute | solution.py:44
  72.3 7.5 %copy-start.2 = (s32[128,128]{1,0:T(8,128)}, s32[128,128]{1,0:T(8,128)S(1)}, u32[]{:S(2)}) copy-start(s32[128,128]{1,0:T(8,128)S(1)} %constant_dynamic-update-slice_fusion.table_ref) | copy-start | bytes 196612
  85.1 20.4 %collective-permute-start.4 = (bf16[512,1024]{1,0:T(8,128)(2,1)}, bf16[512,1024]{1,0:T(8,128)(2,1)S(1)}, u32[]{:S(2)}, u32[]{:S(2)}) collective-permute-start(bf16[512,1024]{1,0:T(8,128)(2,1)} %sort_tail.1.tail_query_ref.tail_value_ref), channel_id=1, source_target_pairs={{0,2},{1,127},{2,4},{3,1},{4,6},{5,3},{6,8},{7,5},{8,10},{9,7},{10... | collective-permute-start | bytes 3145736 | tf_op jit(solution)/shard_map/ppermute | solution.py:44
  105.5 1.0 copy-start.3
  114.8 17.9 %all-to-all-start.1 = ((f32[64,8,128]{2,1,0:T(8,128)}), f32[64,8,128]{2,1,0:T(8,128)S(1)}, u32[]{:S(2)}, u32[]{:S(2)}) async-start(f32[64,8,128]{2,1,0:T(8,128)} %bitcast.35), calls=%async_computation.1 | async-start | bytes 524288 | tf_op jit(solution)/shard_map/all_to_all | solution.py:64
  122.1 19.6 %collective-permute-start.5 = (bf16[512,512]{1,0:T(8,128)(2,1)}, bf16[512,512]{1,0:T(8,128)(2,1)S(1)}, u32[]{:S(2)}, u32[]{:S(2)}) collective-permute-start(bf16[512,512]{1,0:T(8,128)(2,1)} %get-tuple-element.16.query_ref.head_query_ref), channel_id=1, source_target_pairs={{0,126},{1,3},{2,0},{3,5},{4,2},{5,7},{6,4},{7,9},{8,6},{9,11},{10... | collective-permute-start | bytes 1572872 | tf_op jit(solution)/shard_map/ppermute | solution.py:44
  129.5 12.6 %collective-permute-start.6 = (bf16[512,512]{1,0:T(8,128)(2,1)}, bf16[512,512]{1,0:T(8,128)(2,1)S(1)}, u32[]{:S(2)}, u32[]{:S(2)}) collective-permute-start(bf16[512,512]{1,0:T(8,128)(2,1)} %get-tuple-element.18.cotangent_ref.head_cotangent_ref), channel_id=1, source_target_pairs={{0,126},{1,3},{2,0},{3,5},{4,2},{5,7},{6,4},{7,9},{8,6},{9,11},{10... | collective-permute-start | bytes 1572872 | tf_op jit(solution)/shard_map/ppermute | solution.py:44
  132.7 0.7 copy-start.1
  136.6 18.9 %all-to-all-start.2 = ((f32[64,16,128]{2,1,0:T(8,128)}), f32[64,16,128]{2,1,0:T(8,128)S(1)}, u32[]{:S(2)}, u32[]{:S(2)}) async-start(f32[64,16,128]{2,1,0:T(8,128)} %total_stats.1), calls=%async_computation.2 | async-start | bytes 1048576 | tf_op jit(solution)/shard_map/all_to_all | solution.py:64
  141.7 13.8 %copy-start.4 = (bf16[512,512]{1,0:T(8,128)(2,1)}, bf16[512,512]{1,0:T(8,128)(2,1)S(1)}, u32[]{:S(2)}) copy-start(bf16[512,512]{1,0:T(8,128)(2,1)S(1)} %collective-permute-done.5.next_query_ref) | copy-start | bytes 1572868
  142.1 13.4 %copy-start.5 = (bf16[512,512]{1,0:T(8,128)(2,1)}, bf16[512,512]{1,0:T(8,128)(2,1)S(1)}, u32[]{:S(2)}) copy-start(bf16[512,512]{1,0:T(8,128)(2,1)S(1)} %collective-permute-done.6.next_cotangent_ref) | copy-start | bytes 1572868
  155.5 0.8 copy-start

commit v4 on v3

v4 whole, which is shorter than its diff:
```python
import functools

import jax
import jax.numpy as jnp
from jax import lax
from jax.experimental import pallas as pl
from jax.experimental.pallas import tpu as pltpu
from jax.sharding import PartitionSpec as P

DH = 128
GROUP = 256
NEG_SELF = -100000.0
EPS_KEY = 1e-06
LANES = 128
STAT = 8
PIECES = 3
MIB = 1 << 20


def dot(left, right, left_axis=1, right_axis=0):
    return lax.dot_general(
        left,
        right,
        (((left_axis,), (right_axis,)), ((), ())),
        preferred_element_type=jnp.float32,
    )


def params(mib=62):
    return pltpu.CompilerParams(vmem_limit_bytes=mib * MIB)


def cost(flops, moved, exps=0):
    return pl.CostEstimate(flops=int(flops), bytes_accessed=int(moved), transcendentals=int(exps))


def routed(block, route_of):
    owners, halves = lax.axis_size("seq"), lax.axis_size("head")
    route = [
        (i * halves + half, route_of(i, half, owners) * halves + half)
        for i in range(owners)
        for half in range(halves)
    ]
    return lax.ppermute(block, ("seq", "head"), route)


def to_next(block):
    return routed(block, lambda i, half, n: (i + (1 if half == 0 else -1)) % n)


def to_prior(block):
    return routed(block, lambda i, half, n: (i - (1 if half == 0 else -1)) % n)


def to_place_prior(block):
    return routed(block, lambda i, half, n: (i - 1) % n if half == 0 else n - 1 - (i - 1) % n)


def to_place(block):
    return routed(block, lambda i, half, n: i if half == 0 else n - 1 - i)


def exchange(block):
    return lax.all_to_all(block, "seq", split_axis=0, concat_axis=0, tiled=True)


def match(left, right):
    return jnp.where(left == right, 1.0, 0.0).astype(jnp.bfloat16)


ARRIVAL, ARRIVAL3, NEXT3, PLACE, NEXT_PLACE, SEND, SEND3, HALF = 0, 12, 24, 36, 44, 48, 60, 72
FIRST16, LAST16, SEND_CODE = 73, 81, 89
SLOT_ROWS, PLACE_ROWS, NEXT_ROWS, PART_ROWS = 12, 8, 4, 8


def table_row(table_ref, start, count):
    return jnp.concatenate([table_ref[start + i : start + i + 1, :] for i in range(count)], axis=1)


def table_cols(table_ref, start, count):
    turned = table_ref[...].T
    return [turned[:, start + i : start + i + 1] for i in range(count)]


def match_cols(cols, row):
    return jnp.concatenate([match(col, row) for col in cols])


def anywhere(count):
    return [pl.BlockSpec(memory_space=pl.ANY) for _ in range(count)]


def table_spec():
    return pl.BlockSpec((LANES, LANES), lambda *_: (0, 0))


def started(sources, targets, sems, first=0):
    copies = [
        pltpu.make_async_copy(source, target, sems.at[first + i])
        for i, (source, target) in enumerate(zip(sources, targets))
    ]
    for copy in copies:
        copy.start()
    return copies


def iota(shape, axis):
    return lax.broadcasted_iota(jnp.int32, shape, axis)


def pieces_of(wide):
    first = wide.astype(jnp.bfloat16)
    rest = wide - first.astype(jnp.float32)
    second = rest.astype(jnp.bfloat16)
    third = (rest - second.astype(jnp.float32)).astype(jnp.bfloat16)
    return first, second, third


def unit_rows(raw_rows):
    wide = raw_rows.astype(jnp.float32)
    inverse = lax.rsqrt(jnp.sum(wide * wide, -1, keepdims=True) + EPS_KEY)
    return wide * inverse, inverse


def pack_body(index_ref, *refs):
    sources, out_ref, held, staged, load, store = refs[:3], *refs[3:]
    tokens, width = sources[0].shape
    arriving = started(sources, [held.at[i] for i in range(3)], load)
    turned = index_ref[...].T
    chosen = match_cols(
        [turned[:, i : i + 1] for i in range(SLOT_ROWS)], iota((LANES, tokens), 1)
    )
    steps = 4
    block = chosen.shape[0] // steps
    leaving = []
    for step in range(steps):
        rows = slice(step * block, (step + 1) * block)
        for place in range(3):
            if step == 0:
                arriving[place].wait()
            staged[rows, place * width : (place + 1) * width] = dot(
                chosen[rows], held[place]
            ).astype(jnp.bfloat16)
        leaving += started(
            [staged.at[pl.ds(step * block, block)]],
            [out_ref.at[pl.ds(step * block, block)]],
            store,
            step,
        )
    for copy in leaving:
        copy.wait()


def pack(index, *sources):
    slots = SLOT_ROWS * LANES
    tokens, width = sources[0].shape
    total = width * len(sources)
    return pl.pallas_call(
        pack_body,
        in_specs=[pl.BlockSpec(index.shape, lambda *_: (0, 0))] + anywhere(3),
        out_specs=anywhere(1)[0],
        out_shape=jax.ShapeDtypeStruct((slots, total), jnp.bfloat16),
        scratch_shapes=[
            pltpu.VMEM((3, tokens, width), jnp.bfloat16),
            pltpu.VMEM((slots, total), jnp.bfloat16),
            pltpu.SemaphoreType.DMA((3,)),
            pltpu.SemaphoreType.DMA((4,)),
        ],
        compiler_params=params(),
        cost_estimate=cost(2 * slots * tokens * total, 2 * (slots + tokens) * total),
        name="pack_rows",
    )(index, *sources)


def place_cols(table_ref, group):
    cols = table_cols(table_ref, PLACE, PLACE_ROWS)
    each = GROUP // LANES
    first, second = group * each, PLACE_ROWS // 2 + group * each
    return cols[first : first + each], cols[second : second + each]


def tail_body(table_ref, arrived_ref, tail_ref, held, staged, load, store):
    parts, _, wide = held.shape
    columns = [pl.ds(i * wide, wide) for i in range(parts)]
    arriving = started(
        [arrived_ref.at[:, each] for each in columns], [held.at[i] for i in range(parts)], load
    )
    first, second = place_cols(table_ref, 1)
    chosen = match_cols(first + second, table_row(table_ref, ARRIVAL, SLOT_ROWS))
    leaving = []
    for part in range(parts):
        arriving[part].wait()
        staged[part] = dot(chosen, held[part]).astype(jnp.bfloat16)
        leaving += started([staged.at[part]], [tail_ref.at[:, columns[part]]], store, part)
    for copy in leaving:
        copy.wait()


def sort_tail(table, arrived, width):
    slots = arrived.shape[0]
    wide = width // 4
    return pl.pallas_call(
        tail_body,
        in_specs=[table_spec()] + anywhere(1),
        out_specs=anywhere(1)[0],
        out_shape=jax.ShapeDtypeStruct((2 * GROUP, width), jnp.bfloat16),
        scratch_shapes=[
            pltpu.VMEM((4, slots, wide), jnp.bfloat16),
            pltpu.VMEM((4, 2 * GROUP, wide), jnp.bfloat16),
            pltpu.SemaphoreType.DMA((4,)),
            pltpu.SemaphoreType.DMA((4,)),
        ],
        compiler_params=params(),
        cost_estimate=cost(4 * slots * GROUP * width, 2 * (slots + 2 * GROUP) * width),
        name="sort_tail",
    )(table, arrived)


def forward_tile(query, keys, values):
    scores = dot(query, keys, 1, 1)
    own = iota((GROUP, 2 * GROUP), 1) == iota((GROUP, 2 * GROUP), 0) + GROUP
    scores = jnp.where(own, NEG_SELF, scores)
    top = jnp.max(scores, -1, keepdims=True)
    raised = jnp.exp(scores - top)
    total = jnp.sum(raised, -1, keepdims=True)
    weights = (raised * (1.0 / total)).astype(jnp.bfloat16)
    return dot(weights, values), top + jnp.log(total)


def forward_pair(pair, query, raw, values, cotangent, out_ref):
    lane = iota((GROUP, LANES), 1) % STAT
    stat = jnp.zeros((GROUP, LANES), jnp.float32)
    for local in range(2):
        columns = slice(local * DH, (local + 1) * DH)
        keys = unit_rows(raw[:, columns])[0].astype(jnp.bfloat16)
        partial, lse = forward_tile(query[:, columns], keys, values[:, columns])
        out_ref[:, columns] = partial
        delta = jnp.sum(partial * cotangent[:, columns].astype(jnp.float32), -1, keepdims=True)
        head = pair * 2 + local
        stat = jnp.where(lane == head, lse, jnp.where(lane == head + 4, delta, stat))
    return stat


def own_body(
    table_ref,
    arrived_query_ref,
    arrived_value_ref,
    arrived_cotangent_ref,
    tail_query_ref,
    tail_value_ref,
    head_query_ref,
    head_value_ref,
    head_cotangent_ref,
    tail_cotangent_ref,
    out_ref,
    stat_ref,
    chosen,
):
    pair = pl.program_id(0)
    hash_round = pl.program_id(1)

    @pl.when((pair == 0) & (hash_round == 0))
    def _():
        row = table_row(table_ref, ARRIVAL, SLOT_ROWS)
        heads, tails = place_cols(table_ref, 0), place_cols(table_ref, 1)
        for each in range(2):
            chosen[each] = match_cols(heads[each] + tails[each], row)

    select_head = chosen[hash_round, :GROUP]
    query = dot(select_head, arrived_query_ref[...]).astype(jnp.bfloat16)
    value = dot(select_head, arrived_value_ref[...]).astype(jnp.bfloat16)
    cotangent = dot(chosen[hash_round], arrived_cotangent_ref[...]).astype(jnp.bfloat16)
    head_query_ref[...] = query
    head_value_ref[...] = value
    head_cotangent_ref[...] = cotangent[:GROUP]
    tail_cotangent_ref[...] = cotangent[GROUP:]
    stat_ref[...] = forward_pair(
        pair,
        tail_query_ref[...],
        jnp.concatenate([query, tail_query_ref[...]]),
        jnp.concatenate([value, tail_value_ref[...]]),
        cotangent[GROUP:],
        out_ref,
    )


def group_spec(offset=0):
    return pl.BlockSpec((GROUP, 2 * DH), lambda p, r: (r, p + offset))


def stat_spec():
    return pl.BlockSpec((GROUP, LANES), lambda p, r: (r, p))


def forward_own(table, arrived, tail):
    slots, width = arrived.shape
    wide = width // 6
    rows = 2 * GROUP
    array = jax.ShapeDtypeStruct((rows, width // 3), jnp.bfloat16)
    return pl.pallas_call(
        own_body,
        grid=(2, 2),
        in_specs=[pl.BlockSpec((LANES, LANES), lambda p, r: (0, 0))]
        + [pl.BlockSpec((slots, wide), lambda p, r, k=k: (0, p + 2 * k)) for k in range(3)]
        + [group_spec(), group_spec(2)],
        out_specs=[group_spec()] * 5 + [stat_spec()],
        out_shape=[array] * 4
        + [
            jax.ShapeDtypeStruct((rows, width // 3), jnp.float32),
            jax.ShapeDtypeStruct((rows, 2 * LANES), jnp.float32),
        ],
        scratch_shapes=[pltpu.VMEM((2, 2 * GROUP, slots), jnp.bfloat16)],
        compiler_params=params(),
        cost_estimate=cost(5e9, 1e7, 8 * GROUP * 512),
        name="forward_own",
    )(table, arrived, arrived, arrived, tail, tail)


def edge_body(
    table_ref,
    query_ref,
    value_ref,
    cotangent_ref,
    prior_query_ref,
    prior_value_ref,
    second_stat_ref,
    out_ref,
    stat_ref,
    stats_ref,
    both,
):
    pair = pl.program_id(0)
    hash_round = pl.program_id(1)
    stat = forward_pair(
        pair,
        query_ref[...],
        jnp.concatenate([prior_query_ref[...], query_ref[...]]),
        jnp.concatenate([prior_value_ref[...], value_ref[...]]),
        cotangent_ref[...],
        out_ref,
    )
    stat_ref[...] = stat

    @pl.when(pair == 0)
    def _():
        both[hash_round, :GROUP] = stat
        both[hash_round, GROUP:] = second_stat_ref[...]

    @pl.when(pair == 1)
    def _():
        both[hash_round, :GROUP] += stat
        both[hash_round, GROUP:] += second_stat_ref[...]

    @pl.when((pair == 1) & (hash_round == 1))
    def _():
        rows = 4 * GROUP
        piece = iota((rows, LANES), 1) // (PIECES * STAT)
        first, second, third = pieces_of(both[...].reshape(rows, LANES))
        nothing = jnp.zeros((rows, LANES), jnp.bfloat16)
        stats = jnp.where(
            piece == 0,
            first,
            jnp.where(piece == 1, second, jnp.where(piece == 2, third, nothing)),
        )
        place_row = table_row(table_ref, PLACE, PLACE_ROWS)
        third_slots = stats_ref.shape[0]
        arrival_cols = table_cols(table_ref, ARRIVAL3, SLOT_ROWS)
        lane_third = (iota((third_slots, LANES), 1) % (3 * STAT)) // STAT
        result = jnp.zeros((third_slots, LANES), jnp.float32)
        for third in range(3):
            back = match_cols(arrival_cols[4 * third : 4 * third + 4], place_row)
            result = jnp.where(lane_third == third, dot(back, stats), result)
        stats_ref[...] = result


def forward_edge(table, query, value, cotangent, prior_tail, second_stat):
    rows, width = query.shape
    third_slots = SLOT_ROWS * LANES // 3
    return pl.pallas_call(
        edge_body,
        grid=(2, 2),
        in_specs=[pl.BlockSpec((LANES, LANES), lambda p, r: (0, 0))]
        + [group_spec()] * 4
        + [group_spec(2), stat_spec()],
        out_specs=[
            group_spec(),
            stat_spec(),
            pl.BlockSpec((third_slots, LANES), lambda p, r: (0, 0)),
        ],
        out_shape=[
            jax.ShapeDtypeStruct((rows, width), jnp.float32),
            jax.ShapeDtypeStruct((rows, 2 * LANES), jnp.float32),
            jax.ShapeDtypeStruct((third_slots, LANES), jnp.float32),
        ],
        scratch_shapes=[pltpu.VMEM((2, 2 * GROUP, LANES), jnp.float32)],
        compiler_params=params(),
        cost_estimate=cost(2e9, 4e6, 8 * GROUP * 512),
        name="forward_edge",
    )(table, query, value, cotangent, prior_tail, prior_tail, second_stat)


def gather_stats(codes_row, slot_cols, stats):
    narrow = stats.astype(jnp.bfloat16)
    total = None
    for third in range(3):
        chosen = match_cols(slot_cols[4 * third : 4 * third + 4], codes_row)
        found = dot(narrow, chosen, 0, 0)
        for piece in range(PIECES):
            at = piece * PIECES * STAT + third * STAT
            part = found[at : at + STAT]
            total = part if total is None else total + part
    return total


def found_at_tokens(tokens, table_ref, stats):
    slot_cols = table_cols(table_ref, SEND3, SLOT_ROWS)
    found = gather_stats(iota((1, 2 * tokens), 1), slot_cols, stats)
    lse_first, lse_second = found[:4, :tokens], found[:4, tokens:]
    top = jnp.maximum(lse_first, lse_second)
    total = top + jnp.log(jnp.exp(lse_first - top) + jnp.exp(lse_second - top))
    shares = jnp.exp(lse_first - total), jnp.exp(lse_second - total)
    delta = found[4:, :tokens] * shares[0] + found[4:, tokens:] * shares[1]
    return slot_cols, total, delta, shares


def total_body(tokens, table_ref, arrived_ref, out_ref):
    slot_cols, total, delta, _ = found_at_tokens(tokens, table_ref, arrived_ref[...])
    stat = jnp.concatenate([total, delta])
    first, second, third_piece = [member.astype(jnp.float32) for member in pieces_of(stat)]
    spare = jnp.zeros((LANES - 9 * STAT, tokens), jnp.float32)
    table = jnp.concatenate(
        [first] * 3 + [second] * 3 + [third_piece] * 3 + [spare]
    ).astype(jnp.bfloat16)
    third_slots = arrived_ref.shape[0]
    lane_third = (iota((third_slots, LANES), 1) % (3 * STAT)) // STAT
    result = jnp.zeros((third_slots, LANES), jnp.float32)
    for third in range(3):
        codes = slot_cols[4 * third : 4 * third + 4]
        cols = [jnp.where(code >= tokens, code - tokens, code) for code in codes]
        chosen = match_cols(cols, iota((LANES, tokens), 1))
        result = jnp.where(lane_third == third, dot(chosen, table, 1, 1), result)
    owners = third_slots // STAT
    by_owner = result.reshape(owners, STAT, LANES)
    out_ref[:, :STAT, :] = by_owner
    above = jnp.concatenate([by_owner[1:], by_owner[:1]])
    below = jnp.concatenate([by_owner[owners - 1 :], by_owner[: owners - 1]])
    half = table_ref[HALF : HALF + 1, :]
    out_ref[:, STAT:, :] = jnp.where(half[None] == 0, above, below)


def total_stats(table, arrived, tokens):
    owners = arrived.shape[0] // STAT
    return pl.pallas_call(
        functools.partial(total_body, tokens),
        out_shape=jax.ShapeDtypeStruct((owners, 2 * STAT, LANES), jnp.float32),
        compiler_params=params(),
        cost_estimate=cost(2 * 1536 * 1536 * LANES, 1 << 20),
        name="total_stats",
    )(table, arrived)


def prepare_body(tokens, table_ref, arrived_ref, first_ref, second_ref, payload_ref, share_ref):
    @pl.when(pl.program_id(0) == 0)
    def _():
        shares = found_at_tokens(tokens, table_ref, arrived_ref[...])[3]
        spare = jnp.zeros((LANES - STAT, tokens), jnp.float32)
        share_ref[...] = jnp.concatenate([*shares, spare]).T

    back = match_cols(
        table_cols(table_ref, ARRIVAL, SLOT_ROWS), table_row(table_ref, PLACE, PLACE_ROWS)
    )
    rows = [first_ref[:GROUP], second_ref[:GROUP], first_ref[GROUP:], second_ref[GROUP:]]
    payload_ref[...] = dot(back, jnp.concatenate(rows).astype(jnp.bfloat16)).astype(jnp.bfloat16)


def prepare(table, home_stats, outs, tokens):
    slots = SLOT_ROWS * LANES
    rows, width = outs[0].shape
    wide = width // 2
    return pl.pallas_call(
        functools.partial(prepare_body, tokens),
        grid=(2,),
        in_specs=[
            table_spec(),
            pl.BlockSpec(home_stats.shape, lambda i: (0, 0)),
            pl.BlockSpec((rows, wide), lambda i: (0, i)),
            pl.BlockSpec((rows, wide), lambda i: (0, i)),
        ],
        out_specs=[
            pl.BlockSpec((slots, wide), lambda i: (0, i)),
            pl.BlockSpec((tokens, LANES), lambda i: (0, 0)),
        ],
        out_shape=[
            jax.ShapeDtypeStruct((slots, 3 * width), jnp.bfloat16),
            jax.ShapeDtypeStruct((tokens, LANES), jnp.float32),
        ],
        compiler_params=params(),
        cost_estimate=cost(2e9, 1e7),
        name="prepare_outputs",
    )(table, home_stats, *outs)


def backward_tile(query, upstream, keys, values, masked, total_row, delta_row):
    scores = dot(keys, query, 1, 1)
    if masked is not None:
        scores = jnp.where(masked, NEG_SELF, scores)
    probs = jnp.exp(scores - total_row)
    dots = dot(values, upstream, 1, 1)
    slopes = (probs * (dots - delta_row)).astype(jnp.bfloat16)
    return probs.astype(jnp.bfloat16), slopes


def backward_heads(pair, stat, edge_stat, refs, hash_round, shaped):
    heads, tail, tail_cotangent, prior, nexts = refs
    kept = pl.ds(hash_round * GROUP, GROUP)
    own = iota((2 * GROUP, GROUP), 0) == iota((2 * GROUP, GROUP), 1) + GROUP
    width = tail.shape[1] // 2
    for local in range(2):
        head = pair * 2 + local
        columns = pl.ds(head * DH, DH)
        values_at = pl.ds(width + head * DH, DH)
        total_row, delta_row = stat[head : head + 1], stat[head + 4 : head + 5]
        edge_total, edge_delta = edge_stat[head : head + 1], edge_stat[head + 4 : head + 5]
        raw = jnp.concatenate([heads[0][kept, columns], tail[kept, columns]])
        values = jnp.concatenate([heads[1][kept, columns], tail[kept, values_at]])
        upstream = jnp.concatenate([heads[2][kept, columns], tail_cotangent[kept, columns]])
        units, inverse = unit_rows(raw)
        keys = units.astype(jnp.bfloat16)
        prior_keys = unit_rows(prior[kept, columns])[0].astype(jnp.bfloat16)
        keys_first = jnp.concatenate([prior_keys, keys[:GROUP]])
        values_first = jnp.concatenate([prior[kept, values_at], values[:GROUP]])
        probs, slopes = backward_tile(
            raw[:GROUP],
            upstream[:GROUP],
            keys_first,
            values_first,
            own,
            total_row[:, :GROUP],
            delta_row[:, :GROUP],
        )
        query_first = dot(slopes, keys_first, 0, 0)
        unit_first = dot(slopes[GROUP:], raw[:GROUP])
        value_first = dot(probs[GROUP:], upstream[:GROUP])

        probs, slopes = backward_tile(
            raw[GROUP:],
            upstream[GROUP:],
            keys,
            values,
            own,
            total_row[:, GROUP:],
            delta_row[:, GROUP:],
        )
        query_second = dot(slopes, keys, 0, 0)
        unit_both = dot(slopes, raw[GROUP:])
        value_both = dot(probs, upstream[GROUP:])

        next_query = nexts[0][kept, columns]
        next_upstream = nexts[1][kept, columns]
        probs, slopes = backward_tile(
            next_query,
            next_upstream,
            keys[GROUP:],
            values[GROUP:],
            None,
            edge_total,
            edge_delta,
        )
        unit_last = dot(slopes, next_query)
        value_last = dot(probs, next_upstream)

        query_slope = jnp.concatenate([query_first, query_second])
        unit_slope = unit_both + jnp.concatenate([unit_first, unit_last])
        value_slope = value_both + jnp.concatenate([value_first, value_last])
        key_slope = inverse * (
            unit_slope - units * jnp.sum(units * unit_slope, -1, keepdims=True)
        )
        shaped[hash_round, :, local * DH : (local + 1) * DH] = (query_slope + key_slope).astype(
            jnp.bfloat16
        )
        shaped[hash_round, :, (2 + local) * DH : (3 + local) * DH] = value_slope.astype(
            jnp.bfloat16
        )


def backward_body(
    table_ref,
    stats_ref,
    head_query_ref,
    head_value_ref,
    head_cotangent_ref,
    tail_ref,
    tail_cotangent_ref,
    prior_ref,
    next_query_ref,
    next_cotangent_ref,
    _,
    payload_ref,
    stats,
    six,
    double,
    shaped,
    staged,
    load,
    store,
):
    rows = PLACE_ROWS * LANES
    per_round = rows // 2
    sources = [
        stats_ref,
        head_query_ref,
        head_value_ref,
        head_cotangent_ref,
        tail_cotangent_ref,
        next_query_ref,
        next_cotangent_ref,
        tail_ref,
        prior_ref,
    ]
    targets = [stats] + [six.at[i] for i in range(6)] + [double.at[i] for i in range(2)]
    arriving = started(sources, targets, load)
    place_row = table_row(table_ref, PLACE, PLACE_ROWS)
    next_row = table_row(table_ref, NEXT_PLACE, NEXT_ROWS)
    back = [
        match_cols(
            table_cols(table_ref, (FIRST16, LAST16)[each], PART_ROWS),
            place_row[:, each * per_round : (each + 1) * per_round],
        )
        for each in range(2)
    ]
    arriving[0].wait()
    own_stats = stats[:, :STAT, :].reshape(-1, LANES)
    next_stats = stats[:, STAT:, :].reshape(-1, LANES)
    found = gather_stats(place_row, table_cols(table_ref, ARRIVAL3, SLOT_ROWS), own_stats)
    edge = gather_stats(next_row, table_cols(table_ref, NEXT3, SLOT_ROWS), next_stats)
    for copy in arriving[1:]:
        copy.wait()
    refs = (
        (six.at[0], six.at[1], six.at[2]),
        double.at[0],
        six.at[3],
        double.at[1],
        (six.at[4], six.at[5]),
    )
    leaving = []
    width = shaped.shape[2]
    for pair in range(2):
        for hash_round in range(2):
            backward_heads(
                pair,
                found[:, hash_round * per_round : (hash_round + 1) * per_round],
                edge[:, hash_round * GROUP : (hash_round + 1) * GROUP],
                refs,
                hash_round,
                shaped,
            )
        chunks = 2
        for chunk in range(chunks):
            kept = slice(chunk * 1024 // chunks, (chunk + 1) * 1024 // chunks)
            first = dot(back[0][kept], shaped[0]).reshape(-1, 2, STAT, width)
            second = dot(back[1][kept], shaped[1]).reshape(-1, 2, STAT, width)
            whole = jnp.concatenate(
                [first[:, :1], first[:, 1:] + second[:, :1], second[:, 1:]], axis=1
            ).reshape(-1, width)
            count = whole.shape[0]
            at = pl.ds(chunk * count, count)
            staged[pair, at] = whole.astype(jnp.bfloat16)
            leaving += started(
                [staged.at[pair, at]],
                [payload_ref.at[at, pl.ds((pair + 1) * width, width)]],
                store,
                pair * chunks + chunk,
            )
    for copy in leaving:
        copy.wait()


def backward(table, stats, heads, tail, tail_cotangent, prior_tail, nexts, payload):
    slots = SLOT_ROWS * LANES
    rows, width = heads[0].shape
    return pl.pallas_call(
        backward_body,
        in_specs=[table_spec()] + anywhere(10),
        out_specs=anywhere(1)[0],
        out_shape=jax.ShapeDtypeStruct((slots, 3 * width), jnp.bfloat16),
        input_output_aliases={10: 0},
        scratch_shapes=[
            pltpu.VMEM(stats.shape, jnp.float32),
            pltpu.VMEM((6, rows, width), jnp.bfloat16),
            pltpu.VMEM((2, rows, 2 * width), jnp.bfloat16),
            pltpu.VMEM((2, 2 * GROUP, width), jnp.bfloat16),
            pltpu.VMEM((2, slots, width), jnp.bfloat16),
            pltpu.SemaphoreType.DMA((9,)),
            pltpu.SemaphoreType.DMA((4,)),
        ],
        compiler_params=params(),
        cost_estimate=cost(8e9, 1.5e7, 3e6),
        name="backward",
    )(table, stats, *heads, tail, tail_cotangent, prior_tail, *nexts, payload)


def combine_body(
    table_ref, share_ref, arrived_ref, out_ref, first_ref, second_ref, held, staged, load, store
):
    parts, _, wide = held.shape
    tokens = share_ref.shape[0]
    arriving = started(
        [arrived_ref.at[:, pl.ds(i * wide, wide)] for i in range(parts)],
        [held.at[i] for i in range(parts)],
        load,
    )
    token = iota((tokens, 1), 0)
    code = table_row(table_ref, SEND_CODE, SLOT_ROWS)
    by_round = [match(token + tokens * each, code) for each in range(2)]
    chosen = by_round[0] + by_round[1]
    leaving = []
    for part in range(parts):
        arriving[part].wait()
        if part < 2:
            found = 0.0
            for each in range(2):
                at = 4 * each + 2 * part
                share = jnp.concatenate(
                    [
                        jnp.broadcast_to(share_ref[:, at + i : at + i + 1], (tokens, DH))
                        for i in range(2)
                    ],
                    axis=1,
                )
                found = found + share * dot(by_round[each], held[part])
            target = out_ref.at[:, pl.ds(part * wide, wide)]
        else:
            found = dot(chosen, held[part])
            target = (first_ref, second_ref)[part % 2].at[:, pl.ds((part // 2 - 1) * wide, wide)]
        staged[part] = found.astype(jnp.bfloat16)
        leaving += started([staged.at[part]], [target], store, part)
    for copy in leaving:
        copy.wait()


def combine(table, shares, arrived, tokens):
    slots, width = arrived.shape
    wide = width // 6
    return pl.pallas_call(
        combine_body,
        in_specs=[table_spec(), pl.BlockSpec(shares.shape, lambda *_: (0, 0))] + anywhere(1),
        out_specs=anywhere(3),
        out_shape=[jax.ShapeDtypeStruct((tokens, 2 * wide), jnp.bfloat16)] * 3,
        scratch_shapes=[
            pltpu.VMEM((6, slots, wide), jnp.bfloat16),
            pltpu.VMEM((6, tokens, wide), jnp.bfloat16),
            pltpu.SemaphoreType.DMA((6,)),
            pltpu.SemaphoreType.DMA((6,)),
        ],
        compiler_params=params(),
        cost_estimate=cost(2 * slots * tokens * width, 2 * (slots + tokens) * width),
        name="combine_rows",
    )(table, shares, arrived)


def per_device(query_key, value, attended_cotangent, send_rows, arrival_count, receive_slot):
    tokens, row_width = query_key.shape
    rounds = send_rows.shape[0]
    owners = lax.axis_size("seq")
    capacity = send_rows.shape[1] // owners
    per_owner = rounds * capacity
    slots = owners * per_owner

    code = (tokens * jnp.arange(rounds, dtype=jnp.int32))[:, None]
    half = lax.axis_index("head")

    def by_owner(table):
        return table.reshape(rounds, owners, capacity).transpose(1, 0, 2).reshape(owners, per_owner)

    def by_third(codes):
        return codes.reshape(owners, 3, STAT).transpose(1, 0, 2)

    def sent(packed):
        return exchange(packed.reshape(owners, per_owner, -1)).reshape(slots, -1)

    blocks = send_rows.reshape(rounds, owners, capacity)
    send_rows = jnp.where(half == 0, blocks, blocks[:, ::-1]).reshape(rounds, -1)
    send = by_owner(send_rows)
    send_blocks = jnp.pad(send.reshape(-1, LANES), ((0, 4), (0, 0)))
    packed = pack(send_blocks, query_key, value, attended_cotangent)

    within = jnp.arange(capacity, dtype=jnp.int32)

    def arrivals(counts):
        start = jnp.cumsum(counts, axis=1) - counts + code
        codes = jnp.where(within < counts[:, :, None], start[:, :, None] + within, -1)
        return by_owner(codes)

    arrival = arrivals(to_place(arrival_count))
    next_arrival = arrivals(to_place_prior(arrival_count))
    place = to_place(receive_slot) + code
    next_place = to_place_prior(receive_slot[:, :GROUP]) + code
    def half_blocks(codes, first):
        return codes[:, first : first + 2 * STAT]

    members = [
        (ARRIVAL, arrival),
        (ARRIVAL3, by_third(arrival)),
        (NEXT3, by_third(next_arrival)),
        (PLACE, place),
        (NEXT_PLACE, next_place),
        (SEND, send),
        (SEND3, by_third(by_owner(send_rows + code))),
        (HALF, jnp.full((1, LANES), half, jnp.int32)),
        (FIRST16, half_blocks(arrival, 0)),
        (LAST16, half_blocks(arrival, STAT)),
        (SEND_CODE, by_owner(send_rows + code)),
    ]
    rows = [codes.reshape(-1, LANES) for _, codes in members]
    assert [at for at, _ in members] == [sum(map(len, rows[:i])) for i in range(len(rows))]
    table = jnp.concatenate(rows)
    table = jnp.pad(table, ((0, LANES - len(table)), (0, 0)), constant_values=-1)

    arrived, table = lax.optimization_barrier((sent(packed), table))
    tail = sort_tail(table, arrived, 2 * row_width)
    prior_tail = to_next(tail)
    head_query, head_value, head_cotangent, tail_cotangent, out_second, stat_second = forward_own(
        table, arrived, tail
    )
    out_first, stat_first, stats = forward_edge(
        table, head_query, head_value, head_cotangent, prior_tail, stat_second
    )
    next_query = to_prior(head_query)
    next_cotangent = to_prior(head_cotangent)
    home_stats = exchange(stats.reshape(owners, STAT, LANES)).reshape(-1, LANES)
    totals = exchange(total_stats(table, home_stats, tokens))
    payload, shares = prepare(table, home_stats, (out_first, out_second), tokens)
    payload = backward(
        table,
        totals,
        (head_query, head_value, head_cotangent),
        tail,
        tail_cotangent,
        prior_tail,
        (next_query, next_cotangent),
        payload,
    )
    return tuple(combine(table, shares, sent(payload), tokens))


def solution(mesh):
    in_specs = (
        P("seq", "head"),
        P("seq", "head"),
        P("seq", "head"),
        P(None, "seq"),
        P(None, "seq"),
        P(None, "seq"),
    )
    out_specs = (P("seq", "head"), P("seq", "head"), P("seq", "head"))
    return jax.shard_map(
        per_device, mesh=mesh, in_specs=in_specs, out_specs=out_specs, check_vma=False
    )
```

time: 246 us -> 241 us (0.980)
  waiting for transfers between devices: 72.3 us -> 60 us
  Pallas kernels: 58.7 us -> 65.9 us
  blocking collectives: 65 us -> 57.9 us
  starting transfers between devices: 42 us -> 47.6 us
    all_to_all x3, waiting for transfers between devices: 23.2 us -> 14.1 us  [exchange(): return lax.all_to_all(block, 'seq', split_axis=0, concat_axis=0, tiled=True)]
    pallas_call x4 -> x5, Pallas kernels: 35.9 us -> 43.2 us  [the longest x1 16.4 us: backward(): pl.pallas_call(backward_body, in_specs=[table_spec()] + anywhere(10), out...]
    all_to_all x1, blocking collectives: 65 us -> 57.9 us  [exchange(): return lax.all_to_all(block, 'seq', split_axis=0, concat_axis=0, tiled=True)]
    ppermute x7, starting transfers between devices: 17.8 us -> 21.7 us  [routed(): return lax.ppermute(block, ('seq', 'head'), route)]
    ppermute x7, waiting for transfers between devices: 49.1 us -> 45.9 us  [routed(): return lax.ppermute(block, ('seq', 'head'), route)]
  transfers between devices with their start and end apart: 10 -> 10, of which waited for: 6 -> 5; matrix products, arithmetic and copies ran while one was open for 1% -> 2% of each run, Pallas kernels for 6% -> 8%
where the time goes in v4:
time: 241 us
  Pallas kernels  65.9 us (27%)
  waiting for transfers between devices  60 us (25%)
  blocking collectives  57.9 us (24%)
  starting transfers between devices  47.6 us (20%)
  local copies, waits for them, and re-layouts  7.04 us (3%)
    all_to_all x1, blocking collectives, exchange(): return lax.all_to_all(block, 'seq', split_axis=0, concat_axis=0, tiled=True)  57.9 us
    ppermute x7, waiting for transfers between devices, routed(): return lax.ppermute(block, ('seq', 'head'), route)  45.9 us
    all_to_all x3, starting transfers between devices, exchange(): return lax.all_to_all(block, 'seq', split_axis=0, concat_axis=0, tiled=True)  26 us
    ppermute x7, starting transfers between devices, routed(): return lax.ppermute(block, ('seq', 'head'), route)  21.7 us
    pallas_call x1, Pallas kernels, backward(): pl.pallas_call(backward_body, in_specs=[table_spec()] + anywhere(10), out...  16.4 us
    all_to_all x3, waiting for transfers between devices, exchange(): return lax.all_to_all(block, 'seq', split_axis=0, concat_axis=0, tiled=True)  14.1 us
    pallas_call x1, Pallas kernels, forward_own(): pl.pallas_call(own_body, grid=(2, 2), in_specs=[pl.BlockSpec((LANES, LANE...  11.2 us
    pallas_call x1, Pallas kernels, combine(): pl.pallas_call(combine_body, in_specs=[table_spec(), pl.BlockSpec(shares....  8.76 us
  transfers between devices with their start and end apart: 10, of which 5 were waited for; matrix products, arithmetic and copies ran while one was open for 2% of the time, Pallas kernels for 8%

profile of v4, /device:TPU:0, one launch (start us, length us, event | category | flops | bytes accessed | tf_op | source)
XLA Modules:
  0.0 240.6 jit_solution(12729247280077634467)
XLA Ops:
  0.6 0.8 reshape.85
  2.3 5.9 %pack_rows.1 = bf16[1536,1536]{1,0:T(8,128)(2,1)} custom-call(s32[16,128]{1,0:T(8,128)} %pad.8.index_ref, bf16[512,512]{1,0:T(8,128)(2,1)} %refs_0_.1, bf16[512,512]{1,0:T(8,128)(2,1)} %refs_1_.1, bf16[512,512]{1,0:T(8,128)(2,1)} %refs_2_.1), custom_call_target="tpu_custom_call" | custom-call | flops 2415919104 | bytes 6291456 | tf_op jit(solution)/shard_map/pack_rows/pallas_call | solution.py:158
  8.2 11.7 %all-to-all-start = ((bf16[64,24,1536]{2,1,0:T(8,128)(2,1)}), bf16[64,24,1536]{2,1,0:T(8,128)(2,1)}, u32[]{:S(2)}, u32[]{:S(2)}) async-start(bf16[64,24,1536]{2,1,0:T(8,128)(2,1)} %bitcast.35), calls=%async_computation | async-start | bytes 9437184 | tf_op jit(solution)/shard_map/all_to_all | solution.py:64
  20.0 9.2 %collective-permute-start.1 = (s32[2,64]{1,0:T(2,128)S(1)}, s32[2,64]{1,0:T(2,128)S(1)}, u32[]{:S(2)}, u32[]{:S(2)}) collective-permute-start(s32[2,64]{1,0:T(2,128)S(1)} %copy-done.6), channel_id=1, source_target_pairs={{0,126},{1,1},{2,0},{3,127},{4,2},{5,125},{6,4},{7,123},{8,6},{9,1... | collective-permute-start | bytes 1544 | tf_op jit(solution)/shard_map/ppermute | solution.py:44
  30.5 2.8 %collective-permute-start.3 = (s32[2,256]{1,0:T(2,128)S(1)}, s32[2,256]{1,0:T(2,128)S(1)}, u32[]{:S(2)}, u32[]{:S(2)}) collective-permute-start(s32[2,256]{1,0:T(2,128)S(1)} %slice.9), channel_id=1, source_target_pairs={{0,126},{1,1},{2,0},{3,127},{4,2},{5,125},{6,4},{7,123},{8,6},{9,1... | collective-permute-start | bytes 6152 | tf_op jit(solution)/shard_map/ppermute | solution.py:44
  34.0 36.8 %collective-permute-done.1 = s32[2,64]{1,0:T(2,128)S(1)} collective-permute-done((s32[2,64]{1,0:T(2,128)S(1)}, s32[2,64]{1,0:T(2,128)S(1)}, u32[]{:S(2)}, u32[]{:S(2)}) %collective-permute-start.1) | collective-permute-done | bytes 544 | tf_op jit(solution)/shard_map/ppermute | solution.py:44
  74.0 4.6 %all-to-all-done = bf16[64,24,1536]{2,1,0:T(8,128)(2,1)} async-done(((bf16[64,24,1536]{2,1,0:T(8,128)(2,1)}), bf16[64,24,1536]{2,1,0:T(8,128)(2,1)}, u32[]{:S(2)}, u32[]{:S(2)}) %all-to-all-start) | async-done | bytes 4718624 | tf_op jit(solution)/shard_map/all_to_all | solution.py:64
  78.6 6.6 %sort_tail.1.tail_query_ref.tail_value_ref.tail_ref = bf16[512,1024]{1,0:T(8,128)(2,1)} custom-call(s32[128,128]{1,0:T(8,128)} %pad.9.table_ref, bf16[1536,1536]{1,0:T(8,128)(2,1)} %bitcast.2.arrived_ref.arrived_query_ref.arrived_value_ref.arrived_cotangent_ref), custom_call_target="tpu_custom_call" | custom-call | flops 1610612736 | bytes 4194304 | tf_op jit(solution)/shard_map/sort_tail/pallas_call | solution.py:202
  85.4 11.2 %forward_own.1 = (bf16[512,512]{1,0:T(8,128)(2,1)}, bf16[512,512]{1,0:T(8,128)(2,1)}, bf16[512,512]{1,0:T(8,128)(2,1)}, bf16[512,512]{1,0:T(8,128)(2,1)}, f32[512,512]{1,0:T(8,128)}, /*index=5*/f32[512,256]{1,0:T(8,128)}) custom-call(s32[128,128]{1,0:T(8,128)} %pad.9.table_ref, ...), custom_call_target="tpu_custom_call" | custom-call | flops 5000000000 | bytes 10000000 | tf_op jit(solution)/shard_map/forward_own/pallas_call | solution.py:300
  96.7 9.1 %collective-permute-done.4.prior_query_ref.prior_value_ref.prior_ref = bf16[512,1024]{1,0:T(8,128)(2,1)S(1)} collective-permute-done((bf16[512,1024]{1,0:T(8,128)(2,1)}, bf16[512,1024]{1,0:T(8,128)(2,1)S(1)}, u32[]{:S(2)}, u32[]{:S(2)}) %collective-permute-start.4) | collective-permute-done | bytes 1048608 | tf_op jit(solution)/shard_map/ppermute | solution.py:44
  105.7 1.0 copy-done.3
  106.7 8.3 %forward_edge.1 = (f32[512,512]{1,0:T(8,128)}, f32[512,256]{1,0:T(8,128)}, f32[512,128]{1,0:T(8,128)}) custom-call(s32[128,128]{1,0:T(8,128)} %pad.9.table_ref, bf16[512,512]{1,0:T(8,128)(2,1)} %get-tuple-element.17.query_ref.head_query_ref, bf16[512,512]{1,0:T(8,128)(2,1)} %get-tuple-element.18.value_ref.head_value_ref, ...), custom_call_target="tpu_custom_call" | custom-call | flops 2000000000 | bytes 4000000 | tf_op jit(solution)/shard_map/forward_edge/pallas_call | solution.py:379
  115.0 9.6 %all-to-all-start.1 = ((f32[64,8,128]{2,1,0:T(8,128)}), f32[64,8,128]{2,1,0:T(8,128)S(1)}, u32[]{:S(2)}, u32[]{:S(2)}) async-start(f32[64,8,128]{2,1,0:T(8,128)} %bitcast.40), calls=%async_computation.1 | async-start | bytes 524288 | tf_op jit(solution)/shard_map/all_to_all | solution.py:64
  124.7 7.4 %collective-permute-start.5 = (bf16[512,512]{1,0:T(8,128)(2,1)}, bf16[512,512]{1,0:T(8,128)(2,1)S(1)}, u32[]{:S(2)}, u32[]{:S(2)}) collective-permute-start(bf16[512,512]{1,0:T(8,128)(2,1)} %get-tuple-element.17.query_ref.head_query_ref), channel_id=1, source_target_pairs={{0,126},{1,3},{2,0},{3,5},{4,2},{5,7},{6,4},{7,9},{8,6},{9,11},{10... | collective-permute-start | bytes 1572872 | tf_op jit(solution)/shard_map/ppermute | solution.py:44
  132.0 0.9 collective-permute-start.6
  132.9 3.2 %all-to-all-done.1 = f32[64,8,128]{2,1,0:T(8,128)S(1)} async-done(((f32[64,8,128]{2,1,0:T(8,128)}), f32[64,8,128]{2,1,0:T(8,128)S(1)}, u32[]{:S(2)}, u32[]{:S(2)}) %all-to-all-start.1) | async-done | bytes 262176 | tf_op jit(solution)/shard_map/all_to_all | solution.py:64
  136.8 3.2 %total_stats.1 = f32[64,16,128]{2,1,0:T(8,128)} custom-call(s32[128,128]{1,0:T(8,128)} %pad.9.table_ref, f32[512,128]{1,0:T(8,128)} %bitcast.38), custom_call_target="tpu_custom_call" | custom-call | flops 603979776 | bytes 1048576 | tf_op jit(solution)/shard_map/total_stats/pallas_call | solution.py:453
  140.0 4.6 %all-to-all-start.2 = ((f32[64,16,128]{2,1,0:T(8,128)}), f32[64,16,128]{2,1,0:T(8,128)S(1)}, u32[]{:S(2)}, u32[]{:S(2)}) async-start(f32[64,16,128]{2,1,0:T(8,128)} %total_stats.1), calls=%async_computation.2 | async-start | bytes 1048576 | tf_op jit(solution)/shard_map/all_to_all | solution.py:64
  144.7 5.6 %prepare_outputs.1 = (bf16[1536,1536]{1,0:T(8,128)(2,1)}, f32[512,128]{1,0:T(8,128)}) custom-call(s32[128,128]{1,0:T(8,128)} %pad.9.table_ref, f32[512,128]{1,0:T(8,128)} %bitcast.39, f32[512,512]{1,0:T(8,128)} %get-tuple-element.22.first_ref, f32[512,512]{1,0:T(8,128)} %get-tuple-element.23.second_ref), custom_call_target="tpu_custom_call" | custom-call | flops 2000000000 | bytes 10000000 | tf_op jit(solution)/shard_map/prepare_outputs/pallas_call | solution.py:480
  150.2 6.3 %all-to-all-done.2.stats_ref = f32[64,16,128]{2,1,0:T(8,128)S(1)} async-done(((f32[64,16,128]{2,1,0:T(8,128)}), f32[64,16,128]{2,1,0:T(8,128)S(1)}, u32[]{:S(2)}, u32[]{:S(2)}) %all-to-all-start.2) | async-done | bytes 524320 | tf_op jit(solution)/shard_map/all_to_all | solution.py:64
  156.5 0.8 copy-done
  157.4 16.4 %backward.1 = bf16[1536,1536]{1,0:T(8,128)(2,1)} custom-call(s32[128,128]{1,0:T(8,128)} %pad.9.table_ref, f32[64,16,128]{2,1,0:T(8,128)} %copy-done, bf16[512,512]{1,0:T(8,128)(2,1)} %get-tuple-element.17.query_ref.head_query_ref, bf16[512,512]{1,0:T(8,128)(2,1)} %get-tuple-element.18.value_ref.head_value_ref, ...), custom_call_target="tpu_custom_call", output_to_operand_aliasing={{}: (10, {})} | custom-call | flops 8000000000 | bytes 15000000 | tf_op jit(solution)/shard_map/backward/pallas_call | solution.py:681
  173.8 57.9 %all_to_all.20 = bf16[64,24,1536]{2,1,0:T(8,128)(2,1)} all-to-all(bf16[64,24,1536]{2,1,0:T(8,128)(2,1)} %bitcast.36), channel_id=1, replica_groups=mesh['seq'=64,'head'=2] {'seq'}, dimensions={0} | all-to-all | bytes 9437184 | tf_op jit(solution)/shard_map/all_to_all | solution.py:64
  231.7 8.8 %combine_rows.1 = (bf16[512,512]{1,0:T(8,128)(2,1)}, bf16[512,512]{1,0:T(8,128)(2,1)}, bf16[512,512]{1,0:T(8,128)(2,1)}) custom-call(s32[128,128]{1,0:T(8,128)} %pad.9.table_ref, f32[512,128]{1,0:T(8,128)} %get-tuple-element.24.share_ref, bf16[1536,1536]{1,0:T(8,128)(2,1)} %bitcast.37), custom_call_target="tpu_custom_call" | custom-call | flops 2415919104 | bytes 6291456 | tf_op jit(solution)/shard_map/combine_rows/pallas_call | solution.py:744
  (71 shorter events, 6.9 us)
Async XLA Ops:
  8.2 11.8 %copy-start.6 = (s32[2,64]{1,0:T(2,128)S(1)}, s32[2,64]{1,0:T(2,128)}, u32[]{:S(2)}) copy-start(s32[2,64]{1,0:T(2,128)} %param.10) | copy-start | bytes 1540
  8.2 21.6 %copy-start.2 = (s32[2,512]{1,0:T(2,128)S(1)}, s32[2,512]{1,0:T(2,128)}, u32[]{:S(2)}) copy-start(s32[2,512]{1,0:T(2,128)} %param.11) | copy-start | bytes 12292
  8.2 70.4 %all-to-all-start = ((bf16[64,24,1536]{2,1,0:T(8,128)(2,1)}), bf16[64,24,1536]{2,1,0:T(8,128)(2,1)}, u32[]{:S(2)}, u32[]{:S(2)}) async-start(bf16[64,24,1536]{2,1,0:T(8,128)(2,1)} %bitcast.35), calls=%async_computation | async-start | bytes 9437184 | tf_op jit(solution)/shard_map/all_to_all | solution.py:64
  20.0 50.8 %collective-permute-start.1 = (s32[2,64]{1,0:T(2,128)S(1)}, s32[2,64]{1,0:T(2,128)S(1)}, u32[]{:S(2)}, u32[]{:S(2)}) collective-permute-start(s32[2,64]{1,0:T(2,128)S(1)} %copy-done.6), channel_id=1, source_target_pairs={{0,126},{1,1},{2,0},{3,127},{4,2},{5,125},{6,4},{7,123},{8,6},{9,1... | collective-permute-start | bytes 1544 | tf_op jit(solution)/shard_map/ppermute | solution.py:44
  29.2 41.9 %collective-permute-start = (s32[2,64]{1,0:T(2,128)S(1)}, s32[2,64]{1,0:T(2,128)S(1)}, u32[]{:S(2)}, u32[]{:S(2)}) collective-permute-start(s32[2,64]{1,0:T(2,128)S(1)} %copy-done.6), channel_id=1, source_target_pairs={{0,0},{1,127},{2,2},{3,125},{4,4},{5,123},{6,6},{7,121},{8,8},{9,1... | collective-permute-start | bytes 1544 | tf_op jit(solution)/shard_map/ppermute | solution.py:44
  29.8 42.8 %collective-permute-start.2 = (s32[2,512]{1,0:T(2,128)S(1)}, s32[2,512]{1,0:T(2,128)S(1)}, u32[]{:S(2)}, u32[]{:S(2)}) collective-permute-start(s32[2,512]{1,0:T(2,128)S(1)} %copy-done.2), channel_id=1, source_target_pairs={{0,0},{1,127},{2,2},{3,125},{4,4},{5,123},{6,6},{7,121},{8,8},{9,1... | collective-permute-start | bytes 12296 | tf_op jit(solution)/shard_map/ppermute | solution.py:44
  30.5 42.1 %collective-permute-start.3 = (s32[2,256]{1,0:T(2,128)S(1)}, s32[2,256]{1,0:T(2,128)S(1)}, u32[]{:S(2)}, u32[]{:S(2)}) collective-permute-start(s32[2,256]{1,0:T(2,128)S(1)} %slice.9), channel_id=1, source_target_pairs={{0,126},{1,1},{2,0},{3,127},{4,2},{5,125},{6,4},{7,123},{8,6},{9,1... | collective-permute-start | bytes 6152 | tf_op jit(solution)/shard_map/ppermute | solution.py:44
  85.2 20.5 %collective-permute-start.4 = (bf16[512,1024]{1,0:T(8,128)(2,1)}, bf16[512,1024]{1,0:T(8,128)(2,1)S(1)}, u32[]{:S(2)}, u32[]{:S(2)}) collective-permute-start(bf16[512,1024]{1,0:T(8,128)(2,1)} %sort_tail.1.tail_query_ref.tail_value_ref.tail_ref), channel_id=1, source_target_pairs={{0,2},{1,127},{2,4},{3,1},{4,6},{5,3},{6,8},{7,5},{8,10},{9,7},{10... | collective-permute-start | bytes 3145736 | tf_op jit(solution)/shard_map/ppermute | solution.py:44
  105.7 1.0 copy-start.3
  115.0 21.1 %all-to-all-start.1 = ((f32[64,8,128]{2,1,0:T(8,128)}), f32[64,8,128]{2,1,0:T(8,128)S(1)}, u32[]{:S(2)}, u32[]{:S(2)}) async-start(f32[64,8,128]{2,1,0:T(8,128)} %bitcast.40), calls=%async_computation.1 | async-start | bytes 524288 | tf_op jit(solution)/shard_map/all_to_all | solution.py:64
  124.7 25.6 %collective-permute-start.5 = (bf16[512,512]{1,0:T(8,128)(2,1)}, bf16[512,512]{1,0:T(8,128)(2,1)S(1)}, u32[]{:S(2)}, u32[]{:S(2)}) collective-permute-start(bf16[512,512]{1,0:T(8,128)(2,1)} %get-tuple-element.17.query_ref.head_query_ref), channel_id=1, source_target_pairs={{0,126},{1,3},{2,0},{3,5},{4,2},{5,7},{6,4},{7,9},{8,6},{9,11},{10... | collective-permute-start | bytes 1572872 | tf_op jit(solution)/shard_map/ppermute | solution.py:44
  132.0 18.2 %collective-permute-start.6 = (bf16[512,512]{1,0:T(8,128)(2,1)}, bf16[512,512]{1,0:T(8,128)(2,1)S(1)}, u32[]{:S(2)}, u32[]{:S(2)}) collective-permute-start(bf16[512,512]{1,0:T(8,128)(2,1)} %get-tuple-element.19.cotangent_ref.head_cotangent_ref), channel_id=1, source_target_pairs={{0,126},{1,3},{2,0},{3,5},{4,2},{5,7},{6,4},{7,9},{8,6},{9,11},{10... | collective-permute-start | bytes 1572872 | tf_op jit(solution)/shard_map/ppermute | solution.py:44
  136.1 0.7 copy-start.1
  140.0 16.5 %all-to-all-start.2 = ((f32[64,16,128]{2,1,0:T(8,128)}), f32[64,16,128]{2,1,0:T(8,128)S(1)}, u32[]{:S(2)}, u32[]{:S(2)}) async-start(f32[64,16,128]{2,1,0:T(8,128)} %total_stats.1), calls=%async_computation.2 | async-start | bytes 1048576 | tf_op jit(solution)/shard_map/all_to_all | solution.py:64
  150.2 6.3 %copy-start.4 = (bf16[512,512]{1,0:T(8,128)(2,1)}, bf16[512,512]{1,0:T(8,128)(2,1)S(1)}, u32[]{:S(2)}) copy-start(bf16[512,512]{1,0:T(8,128)(2,1)S(1)} %collective-permute-done.5.next_query_ref) | copy-start | bytes 1572868
  150.2 6.3 %copy-start.5 = (bf16[512,512]{1,0:T(8,128)(2,1)}, bf16[512,512]{1,0:T(8,128)(2,1)S(1)}, u32[]{:S(2)}) copy-start(bf16[512,512]{1,0:T(8,128)(2,1)S(1)} %collective-permute-done.6.next_cotangent_ref) | copy-start | bytes 1572868
  156.5 0.8 copy-start

commit v5 on v4

--- a/solution.py
+++ b/solution.py
@@ -123,11 +123,11 @@
 
 
 def pack_body(index_ref, *refs):
-    sources, out_ref, held, staged, load, store = refs[:3], *refs[3:]
+    sources, out_ref, held, staged, chosen, load, store = refs[:3], *refs[3:]
     tokens, width = sources[0].shape
     arriving = started(sources, [held.at[i] for i in range(3)], load)
     turned = index_ref[...].T
-    chosen = match_cols(
+    chosen[...] = match_cols(
         [turned[:, i : i + 1] for i in range(SLOT_ROWS)], iota((LANES, tokens), 1)
     )
     steps = 4
@@ -163,6 +163,7 @@
         scratch_shapes=[
             pltpu.VMEM((3, tokens, width), jnp.bfloat16),
             pltpu.VMEM((slots, total), jnp.bfloat16),
+            pltpu.VMEM((slots, tokens), jnp.bfloat16),
             pltpu.SemaphoreType.DMA((3,)),
             pltpu.SemaphoreType.DMA((4,)),
         ],
@@ -179,18 +180,18 @@
     return cols[first : first + each], cols[second : second + each]
 
 
-def tail_body(table_ref, arrived_ref, tail_ref, held, staged, load, store):
+def tail_body(table_ref, arrived_ref, tail_ref, held, staged, chosen, load, store):
     parts, _, wide = held.shape
     columns = [pl.ds(i * wide, wide) for i in range(parts)]
     arriving = started(
         [arrived_ref.at[:, each] for each in columns], [held.at[i] for i in range(parts)], load
     )
     first, second = place_cols(table_ref, 1)
-    chosen = match_cols(first + second, table_row(table_ref, ARRIVAL, SLOT_ROWS))
+    chosen[...] = match_cols(first + second, table_row(table_ref, ARRIVAL, SLOT_ROWS))
     leaving = []
     for part in range(parts):
         arriving[part].wait()
-        staged[part] = dot(chosen, held[part]).astype(jnp.bfloat16)
+        staged[part] = dot(chosen[...], held[part]).astype(jnp.bfloat16)
         leaving += started([staged.at[part]], [tail_ref.at[:, columns[part]]], store, part)
     for copy in leaving:
         copy.wait()
@@ -207,6 +208,7 @@
         scratch_shapes=[
             pltpu.VMEM((4, slots, wide), jnp.bfloat16),
             pltpu.VMEM((4, 2 * GROUP, wide), jnp.bfloat16),
+            pltpu.VMEM((2 * GROUP, slots), jnp.bfloat16),
             pltpu.SemaphoreType.DMA((4,)),
             pltpu.SemaphoreType.DMA((4,)),
         ],
@@ -494,7 +496,7 @@
             jax.ShapeDtypeStruct((slots, 3 * width), jnp.bfloat16),
             jax.ShapeDtypeStruct((tokens, LANES), jnp.float32),
         ],
-        compiler_params=params(),
+        compiler_params=params(62),
         cost_estimate=cost(2e9, 1e7),
         name="prepare_outputs",
     )(table, home_stats, *outs)
@@ -503,7 +505,14 @@
 def backward_tile(query, upstream, keys, values, masked, total_row, delta_row):
     scores = dot(keys, query, 1, 1)
     if masked is not None:
-        scores = jnp.where(masked, NEG_SELF, scores)
+        low, high = scores[GROUP : GROUP + LANES], scores[GROUP + LANES :]
+        low = jnp.concatenate(
+            [jnp.where(masked, NEG_SELF, low[:, :LANES]), low[:, LANES:]], axis=1
+        )
+        high = jnp.concatenate(
+            [high[:, :LANES], jnp.where(masked, NEG_SELF, high[:, LANES:])], axis=1
+        )
+        scores = jnp.concatenate([scores[:GROUP], low, high])
     probs = jnp.exp(scores - total_row)
     dots = dot(values, upstream, 1, 1)
     slopes = (probs * (dots - delta_row)).astype(jnp.bfloat16)
@@ -513,7 +522,7 @@
 def backward_heads(pair, stat, edge_stat, refs, hash_round, shaped):
     heads, tail, tail_cotangent, prior, nexts = refs
     kept = pl.ds(hash_round * GROUP, GROUP)
-    own = iota((2 * GROUP, GROUP), 0) == iota((2 * GROUP, GROUP), 1) + GROUP
+    own = iota((LANES, LANES), 0) == iota((LANES, LANES), 1)
     width = tail.shape[1] // 2
     for local in range(2):
         head = pair * 2 + local
@@ -538,7 +547,7 @@
             total_row[:, :GROUP],
             delta_row[:, :GROUP],
         )
-        query_first = dot(slopes, keys_first, 0, 0)
+        query_first = dot(keys_first, slopes, 0, 0).T
         unit_first = dot(slopes[GROUP:], raw[:GROUP])
         value_first = dot(probs[GROUP:], upstream[:GROUP])
 
@@ -551,7 +560,7 @@
             total_row[:, GROUP:],
             delta_row[:, GROUP:],
         )
-        query_second = dot(slopes, keys, 0, 0)
+        query_second = dot(keys, slopes, 0, 0).T
         unit_both = dot(slopes, raw[GROUP:])
         value_both = dot(probs, upstream[GROUP:])
 
@@ -693,29 +702,32 @@
             pltpu.SemaphoreType.DMA((9,)),
             pltpu.SemaphoreType.DMA((4,)),
         ],
-        compiler_params=params(),
+        compiler_params=params(62),
         cost_estimate=cost(8e9, 1.5e7, 3e6),
         name="backward",
     )(table, stats, *heads, tail, tail_cotangent, prior_tail, *nexts, payload)
 
 
 def combine_body(
-    table_ref, share_ref, arrived_ref, out_ref, first_ref, second_ref, held, staged, load, store
+    table_ref,
+    share_ref,
+    arrived_ref,
+    out_ref,
+    first_ref,
+    second_ref,
+    staged,
+    chosen,
+    store,
 ):
-    parts, _, wide = held.shape
-    tokens = share_ref.shape[0]
-    arriving = started(
-        [arrived_ref.at[:, pl.ds(i * wide, wide)] for i in range(parts)],
-        [held.at[i] for i in range(parts)],
-        load,
-    )
+    parts, tokens, wide = staged.shape
     token = iota((tokens, 1), 0)
     code = table_row(table_ref, SEND_CODE, SLOT_ROWS)
-    by_round = [match(token + tokens * each, code) for each in range(2)]
-    chosen = by_round[0] + by_round[1]
+    chosen[0] = match(token, code)
+    chosen[1] = match(token + tokens, code)
+    chosen[2] = match(token, table_row(table_ref, SEND, SLOT_ROWS))
     leaving = []
     for part in range(parts):
-        arriving[part].wait()
+        arrived = arrived_ref[:, part * wide : (part + 1) * wide]
         if part < 2:
             found = 0.0
             for each in range(2):
@@ -727,10 +739,10 @@
                     ],
                     axis=1,
                 )
-                found = found + share * dot(by_round[each], held[part])
+                found = found + share * dot(chosen[each], arrived)
             target = out_ref.at[:, pl.ds(part * wide, wide)]
         else:
-            found = dot(chosen, held[part])
+            found = dot(chosen[2], arrived)
             target = (first_ref, second_ref)[part % 2].at[:, pl.ds((part // 2 - 1) * wide, wide)]
         staged[part] = found.astype(jnp.bfloat16)
         leaving += started([staged.at[part]], [target], store, part)
@@ -743,16 +755,16 @@
     wide = width // 6
     return pl.pallas_call(
         combine_body,
-        in_specs=[table_spec(), pl.BlockSpec(shares.shape, lambda *_: (0, 0))] + anywhere(1),
+        in_specs=[table_spec(), pl.BlockSpec(shares.shape, lambda *_: (0, 0))]
+        + [pl.BlockSpec(memory_space=pltpu.VMEM)],
         out_specs=anywhere(3),
         out_shape=[jax.ShapeDtypeStruct((tokens, 2 * wide), jnp.bfloat16)] * 3,
         scratch_shapes=[
-            pltpu.VMEM((6, slots, wide), jnp.bfloat16),
             pltpu.VMEM((6, tokens, wide), jnp.bfloat16),
+            pltpu.VMEM((3, tokens, slots), jnp.bfloat16),
             pltpu.SemaphoreType.DMA((6,)),
-            pltpu.SemaphoreType.DMA((6,)),
-        ],
-        compiler_params=params(),
+        ],
+        compiler_params=params(40),
         cost_estimate=cost(2 * slots * tokens * width, 2 * (slots + tokens) * width),
         name="combine_rows",
     )(table, shares, arrived)
@@ -791,10 +803,15 @@
         codes = jnp.where(within < counts[:, :, None], start[:, :, None] + within, -1)
         return by_owner(codes)
 
-    arrival = arrivals(to_place(arrival_count))
-    next_arrival = arrivals(to_place_prior(arrival_count))
-    place = to_place(receive_slot) + code
-    next_place = to_place_prior(receive_slot[:, :GROUP]) + code
+    tables = jnp.concatenate([arrival_count, receive_slot], axis=1)
+    packed, mine, following = lax.optimization_barrier(
+        (packed, to_place(tables), to_place_prior(tables[:, : owners + GROUP]))
+    )
+    arrival = arrivals(mine[:, :owners])
+    next_arrival = arrivals(following[:, :owners])
+    place = mine[:, owners:] + code
+    next_place = following[:, owners:] + code
+
     def half_blocks(codes, first):
         return codes[:, first : first + 2 * STAT]
 

time: 241 us -> 245 us (1.017)
  waiting for transfers between devices: 60 us -> 70.9 us
  starting transfers between devices: 47.6 us -> 39.1 us
  Pallas kernels: 65.9 us -> 60.2 us
  blocking collectives: 57.9 us -> 63.6 us
    all_to_all x3, waiting for transfers between devices: 14.1 us -> 63.1 us  [exchange(): return lax.all_to_all(block, 'seq', split_axis=0, concat_axis=0, tiled=True)]
    ppermute x7 -> x5, waiting for transfers between devices: 45.9 us -> 7.8 us  [routed(): return lax.ppermute(block, ('seq', 'head'), route)]
    all_to_all x3, starting transfers between devices: 26 us -> 18.1 us  [exchange(): return lax.all_to_all(block, 'seq', split_axis=0, concat_axis=0, tiled=True)]
    all_to_all x1, blocking collectives: 57.9 us -> 63.6 us  [exchange(): return lax.all_to_all(block, 'seq', split_axis=0, concat_axis=0, tiled=True)]
    pallas_call x1, Pallas kernels: 8.76 us -> 4.3 us  [combine(): pl.pallas_call(combine_body, in_specs=[table_spec(), pl.BlockSpec(shares....]
    ppermute x7 -> x5, starting transfers between devices: 21.7 us -> 21 us  [routed(): return lax.ppermute(block, ('seq', 'head'), route)]
  transfers between devices with their start and end apart: 10 -> 8, of which waited for: 5 -> 4; matrix products, arithmetic and copies ran while one was open for 2% -> 3% of each run, Pallas kernels for 8% -> 11%
where the time goes in v5:
time: 245 us; the launch traced here: 244 us
  waiting for transfers between devices  70.9 us (29%)
  blocking collectives  63.6 us (26%)
  Pallas kernels  60.2 us (25%)
  starting transfers between devices  39.1 us (16%)
  local copies, waits for them, and re-layouts  7.05 us (3%)
  other arithmetic  2.48 us (1%)
    all_to_all x1, blocking collectives, exchange(): return lax.all_to_all(block, 'seq', split_axis=0, concat_axis=0, tiled=True)  63.6 us
    all_to_all x3, waiting for transfers between devices, exchange(): return lax.all_to_all(block, 'seq', split_axis=0, concat_axis=0, tiled=True)  63.1 us
    ppermute x5, starting transfers between devices, routed(): return lax.ppermute(block, ('seq', 'head'), route)  21 us
    all_to_all x3, starting transfers between devices, exchange(): return lax.all_to_all(block, 'seq', split_axis=0, concat_axis=0, tiled=True)  18.1 us
    pallas_call x1, Pallas kernels, backward(): pl.pallas_call(backward_body, in_specs=[table_spec()] + anywhere(10), out...  15.1 us
    pallas_call x1, Pallas kernels, forward_own(): pl.pallas_call(own_body, grid=(2, 2), in_specs=[pl.BlockSpec((LANES, LANE...  11.2 us
    pallas_call x1, Pallas kernels, forward_edge(): pl.pallas_call(edge_body, grid=(2, 2), in_specs=[pl.BlockSpec((LANES, LAN...  8.34 us
    ppermute x5, waiting for transfers between devices, routed(): return lax.ppermute(block, ('seq', 'head'), route)  7.8 us
  transfers between devices with their start and end apart: 8, of which 4 were waited for; matrix products, arithmetic and copies ran while one was open for 3% of the time, Pallas kernels for 11%

profile of v5, /device:TPU:0, one launch (start us, length us, event | category | flops | bytes accessed | tf_op | source)
XLA Modules:
  0.0 244.5 jit_solution(10799118972714042415)
XLA Ops:
  0.6 0.8 pad_add_fusion
  2.8 10.7 %collective-permute-start.1 = (s32[2,320]{1,0:T(2,128)S(1)}, s32[2,320]{1,0:T(2,128)S(1)}, u32[]{:S(2)}, u32[]{:S(2)}) collective-permute-start(s32[2,320]{1,0:T(2,128)S(1)} %fusion.1), channel_id=1, source_target_pairs={{0,126},{1,1},{2,0},{3,127},{4,2},{5,125},{6,4},{7,123},{8,6},{9,1... | collective-permute-start | bytes 7688 | tf_op jit(solution)/shard_map/ppermute | solution.py:44
  13.5 0.8 reshape.85
  15.2 5.8 %pack_rows.1 = bf16[1536,1536]{1,0:T(8,128)(2,1)} custom-call(s32[16,128]{1,0:T(8,128)} %pad.8.index_ref, bf16[512,512]{1,0:T(8,128)(2,1)} %refs_0_.1, bf16[512,512]{1,0:T(8,128)(2,1)} %refs_1_.1, bf16[512,512]{1,0:T(8,128)(2,1)} %refs_2_.1), custom_call_target="tpu_custom_call" | custom-call | flops 2415919104 | bytes 6291456 | tf_op jit(solution)/shard_map/pack_rows/pallas_call | solution.py:158
  21.1 5.7 %all-to-all-start = ((bf16[64,24,1536]{2,1,0:T(8,128)(2,1)}), bf16[64,24,1536]{2,1,0:T(8,128)(2,1)}, u32[]{:S(2)}, u32[]{:S(2)}) async-start(bf16[64,24,1536]{2,1,0:T(8,128)(2,1)} %bitcast.38), calls=%async_computation | async-start | bytes 9437184 | tf_op jit(solution)/shard_map/all_to_all | solution.py:64
  30.7 51.7 %all-to-all-done = bf16[64,24,1536]{2,1,0:T(8,128)(2,1)} async-done(((bf16[64,24,1536]{2,1,0:T(8,128)(2,1)}), bf16[64,24,1536]{2,1,0:T(8,128)(2,1)}, u32[]{:S(2)}, u32[]{:S(2)}) %all-to-all-start) | async-done | bytes 4718624 | tf_op jit(solution)/shard_map/all_to_all | solution.py:64
  82.4 6.6 %sort_tail.1.tail_query_ref.tail_value_ref.tail_ref = bf16[512,1024]{1,0:T(8,128)(2,1)} custom-call(s32[128,128]{1,0:T(8,128)} %pad.9.table_ref, bf16[1536,1536]{1,0:T(8,128)(2,1)} %bitcast.2.arrived_ref.arrived_query_ref.arrived_value_ref.arrived_cotangent_ref), custom_call_target="tpu_custom_call" | custom-call | flops 1610612736 | bytes 4194304 | tf_op jit(solution)/shard_map/sort_tail/pallas_call | solution.py:203
  89.1 1.5 collective-permute-start.2
  90.5 11.2 %forward_own.1 = (bf16[512,512]{1,0:T(8,128)(2,1)}, bf16[512,512]{1,0:T(8,128)(2,1)}, bf16[512,512]{1,0:T(8,128)(2,1)}, bf16[512,512]{1,0:T(8,128)(2,1)}, f32[512,512]{1,0:T(8,128)}, /*index=5*/f32[512,256]{1,0:T(8,128)}) custom-call(s32[128,128]{1,0:T(8,128)} %pad.9.table_ref, ...), custom_call_target="tpu_custom_call" | custom-call | flops 5000000000 | bytes 10000000 | tf_op jit(solution)/shard_map/forward_own/pallas_call | solution.py:302
  101.8 7.8 %collective-permute-done.2.prior_query_ref.prior_value_ref.prior_ref = bf16[512,1024]{1,0:T(8,128)(2,1)S(1)} collective-permute-done((bf16[512,1024]{1,0:T(8,128)(2,1)}, bf16[512,1024]{1,0:T(8,128)(2,1)S(1)}, u32[]{:S(2)}, u32[]{:S(2)}) %collective-permute-start.2) | collective-permute-done | bytes 1048608 | tf_op jit(solution)/shard_map/ppermute | solution.py:44
  109.6 1.0 copy-done.4
  110.6 8.3 %forward_edge.1 = (f32[512,512]{1,0:T(8,128)}, f32[512,256]{1,0:T(8,128)}, f32[512,128]{1,0:T(8,128)}) custom-call(s32[128,128]{1,0:T(8,128)} %pad.9.table_ref, bf16[512,512]{1,0:T(8,128)(2,1)} %get-tuple-element.23.query_ref.head_query_ref, bf16[512,512]{1,0:T(8,128)(2,1)} %get-tuple-element.24.value_ref.head_value_ref, ...), custom_call_target="tpu_custom_call" | custom-call | flops 2000000000 | bytes 4000000 | tf_op jit(solution)/shard_map/forward_edge/pallas_call | solution.py:381
  118.9 7.5 %all-to-all-start.1 = ((f32[64,8,128]{2,1,0:T(8,128)}), f32[64,8,128]{2,1,0:T(8,128)S(1)}, u32[]{:S(2)}, u32[]{:S(2)}) async-start(f32[64,8,128]{2,1,0:T(8,128)} %bitcast.42), calls=%async_computation.1 | async-start | bytes 524288 | tf_op jit(solution)/shard_map/all_to_all | solution.py:64
  126.4 7.4 %collective-permute-start.3 = (bf16[512,512]{1,0:T(8,128)(2,1)}, bf16[512,512]{1,0:T(8,128)(2,1)S(1)}, u32[]{:S(2)}, u32[]{:S(2)}) collective-permute-start(bf16[512,512]{1,0:T(8,128)(2,1)} %get-tuple-element.23.query_ref.head_query_ref), channel_id=1, source_target_pairs={{0,126},{1,3},{2,0},{3,5},{4,2},{5,7},{6,4},{7,9},{8,6},{9,11},{10... | collective-permute-start | bytes 1572872 | tf_op jit(solution)/shard_map/ppermute | solution.py:44
  133.8 0.9 collective-permute-start.4
  134.6 2.4 all-to-all-done.1
  137.8 3.2 %total_stats.1 = f32[64,16,128]{2,1,0:T(8,128)} custom-call(s32[128,128]{1,0:T(8,128)} %pad.9.table_ref, f32[512,128]{1,0:T(8,128)} %bitcast.40), custom_call_target="tpu_custom_call" | custom-call | flops 603979776 | bytes 1048576 | tf_op jit(solution)/shard_map/total_stats/pallas_call | solution.py:455
  141.0 4.9 %all-to-all-start.2 = ((f32[64,16,128]{2,1,0:T(8,128)}), f32[64,16,128]{2,1,0:T(8,128)S(1)}, u32[]{:S(2)}, u32[]{:S(2)}) async-start(f32[64,16,128]{2,1,0:T(8,128)} %total_stats.1), calls=%async_computation.2 | async-start | bytes 1048576 | tf_op jit(solution)/shard_map/all_to_all | solution.py:64
  145.9 5.6 %prepare_outputs.1 = (bf16[1536,1536]{1,0:T(8,128)(2,1)}, f32[512,128]{1,0:T(8,128)}) custom-call(s32[128,128]{1,0:T(8,128)} %pad.9.table_ref, f32[512,128]{1,0:T(8,128)} %bitcast.41, f32[512,512]{1,0:T(8,128)} %get-tuple-element.28.first_ref, f32[512,512]{1,0:T(8,128)} %get-tuple-element.29.second_ref), custom_call_target="tpu_custom_call" | custom-call | flops 2000000000 | bytes 10000000 | tf_op jit(solution)/shard_map/prepare_outputs/pallas_call | solution.py:482
  151.5 8.9 %all-to-all-done.2.stats_ref = f32[64,16,128]{2,1,0:T(8,128)S(1)} async-done(((f32[64,16,128]{2,1,0:T(8,128)}), f32[64,16,128]{2,1,0:T(8,128)S(1)}, u32[]{:S(2)}, u32[]{:S(2)}) %all-to-all-start.2) | async-done | bytes 524320 | tf_op jit(solution)/shard_map/all_to_all | solution.py:64
  160.4 0.8 copy-done.2
  161.3 15.1 %backward.1 = bf16[1536,1536]{1,0:T(8,128)(2,1)} custom-call(s32[128,128]{1,0:T(8,128)} %pad.9.table_ref, f32[64,16,128]{2,1,0:T(8,128)} %copy-done.2, bf16[512,512]{1,0:T(8,128)(2,1)} %get-tuple-element.23.query_ref.head_query_ref, bf16[512,512]{1,0:T(8,128)(2,1)} %get-tuple-element.24.value_ref.head_value_ref, ...), custom_call_target="tpu_custom_call", output_to_operand_aliasing={{}: (10, {})} | custom-call | flops 8000000000 | bytes 15000000 | tf_op jit(solution)/shard_map/backward/pallas_call | solution.py:690
  176.4 63.6 %all_to_all.20 = bf16[64,24,1536]{2,1,0:T(8,128)(2,1)S(1)} all-to-all(bf16[64,24,1536]{2,1,0:T(8,128)(2,1)} %bitcast.39), channel_id=1, replica_groups=mesh['seq'=64,'head'=2] {'seq'}, dimensions={0} | all-to-all | bytes 9437184 | tf_op jit(solution)/shard_map/all_to_all | solution.py:64
  240.0 4.3 %combine_rows.1 = (bf16[512,512]{1,0:T(8,128)(2,1)}, bf16[512,512]{1,0:T(8,128)(2,1)}, bf16[512,512]{1,0:T(8,128)(2,1)}) custom-call(s32[128,128]{1,0:T(8,128)S(1)} %copy-done, f32[512,128]{1,0:T(8,128)S(1)} %copy-done.1, bf16[1536,1536]{1,0:T(8,128)(2,1)S(1)} %bitcast.37), custom_call_target="tpu_custom_call" | custom-call | flops 2415919104 | bytes 6291456 | tf_op jit(solution)/shard_map/combine_rows/pallas_call | solution.py:756
  (70 shorter events, 6.8 us)
Async XLA Ops:
  1.4 19.7 %collective-permute-start = (s32[2,576]{1,0:T(2,128)S(1)}, s32[2,576]{1,0:T(2,128)S(1)}, u32[]{:S(2)}, u32[]{:S(2)}) collective-permute-start(s32[2,576]{1,0:T(2,128)S(1)} %pad_add_fusion), channel_id=1, source_target_pairs={{0,0},{1,127},{2,2},{3,125},{4,4},{5,123},{6,6},{7,121},{8,8},{9,1... | collective-permute-start | bytes 13832 | tf_op jit(solution)/shard_map/ppermute | solution.py:44
  2.8 18.2 %collective-permute-start.1 = (s32[2,320]{1,0:T(2,128)S(1)}, s32[2,320]{1,0:T(2,128)S(1)}, u32[]{:S(2)}, u32[]{:S(2)}) collective-permute-start(s32[2,320]{1,0:T(2,128)S(1)} %fusion.1), channel_id=1, source_target_pairs={{0,126},{1,1},{2,0},{3,127},{4,2},{5,125},{6,4},{7,123},{8,6},{9,1... | collective-permute-start | bytes 7688 | tf_op jit(solution)/shard_map/ppermute | solution.py:44
  21.1 61.3 %all-to-all-start = ((bf16[64,24,1536]{2,1,0:T(8,128)(2,1)}), bf16[64,24,1536]{2,1,0:T(8,128)(2,1)}, u32[]{:S(2)}, u32[]{:S(2)}) async-start(bf16[64,24,1536]{2,1,0:T(8,128)(2,1)} %bitcast.38), calls=%async_computation | async-start | bytes 9437184 | tf_op jit(solution)/shard_map/all_to_all | solution.py:64
  89.1 20.5 %collective-permute-start.2 = (bf16[512,1024]{1,0:T(8,128)(2,1)}, bf16[512,1024]{1,0:T(8,128)(2,1)S(1)}, u32[]{:S(2)}, u32[]{:S(2)}) collective-permute-start(bf16[512,1024]{1,0:T(8,128)(2,1)} %sort_tail.1.tail_query_ref.tail_value_ref.tail_ref), channel_id=1, source_target_pairs={{0,2},{1,127},{2,4},{3,1},{4,6},{5,3},{6,8},{7,5},{8,10},{9,7},{10... | collective-permute-start | bytes 3145736 | tf_op jit(solution)/shard_map/ppermute | solution.py:44
  109.6 1.0 copy-start.4
  118.9 18.2 %all-to-all-start.1 = ((f32[64,8,128]{2,1,0:T(8,128)}), f32[64,8,128]{2,1,0:T(8,128)S(1)}, u32[]{:S(2)}, u32[]{:S(2)}) async-start(f32[64,8,128]{2,1,0:T(8,128)} %bitcast.42), calls=%async_computation.1 | async-start | bytes 524288 | tf_op jit(solution)/shard_map/all_to_all | solution.py:64
  126.4 25.1 %collective-permute-start.3 = (bf16[512,512]{1,0:T(8,128)(2,1)}, bf16[512,512]{1,0:T(8,128)(2,1)S(1)}, u32[]{:S(2)}, u32[]{:S(2)}) collective-permute-start(bf16[512,512]{1,0:T(8,128)(2,1)} %get-tuple-element.23.query_ref.head_query_ref), channel_id=1, source_target_pairs={{0,126},{1,3},{2,0},{3,5},{4,2},{5,7},{6,4},{7,9},{8,6},{9,11},{10... | collective-permute-start | bytes 1572872 | tf_op jit(solution)/shard_map/ppermute | solution.py:44
  133.8 17.7 %collective-permute-start.4 = (bf16[512,512]{1,0:T(8,128)(2,1)}, bf16[512,512]{1,0:T(8,128)(2,1)S(1)}, u32[]{:S(2)}, u32[]{:S(2)}) collective-permute-start(bf16[512,512]{1,0:T(8,128)(2,1)} %get-tuple-element.25.cotangent_ref.head_cotangent_ref), channel_id=1, source_target_pairs={{0,126},{1,3},{2,0},{3,5},{4,2},{5,7},{6,4},{7,9},{8,6},{9,11},{10... | collective-permute-start | bytes 1572872 | tf_op jit(solution)/shard_map/ppermute | solution.py:44
  137.1 0.7 copy-start.3
  141.0 19.4 %all-to-all-start.2 = ((f32[64,16,128]{2,1,0:T(8,128)}), f32[64,16,128]{2,1,0:T(8,128)S(1)}, u32[]{:S(2)}, u32[]{:S(2)}) async-start(f32[64,16,128]{2,1,0:T(8,128)} %total_stats.1), calls=%async_computation.2 | async-start | bytes 1048576 | tf_op jit(solution)/shard_map/all_to_all | solution.py:64
  151.5 8.9 %copy-start.5 = (bf16[512,512]{1,0:T(8,128)(2,1)}, bf16[512,512]{1,0:T(8,128)(2,1)S(1)}, u32[]{:S(2)}) copy-start(bf16[512,512]{1,0:T(8,128)(2,1)S(1)} %collective-permute-done.3.next_query_ref) | copy-start | bytes 1572868
  151.5 8.9 %copy-start.6 = (bf16[512,512]{1,0:T(8,128)(2,1)}, bf16[512,512]{1,0:T(8,128)(2,1)S(1)}, u32[]{:S(2)}) copy-start(bf16[512,512]{1,0:T(8,128)(2,1)S(1)} %collective-permute-done.4.next_cotangent_ref) | copy-start | bytes 1572868
  160.4 0.8 copy-start.2
  176.4 63.6 %copy-start = (s32[128,128]{1,0:T(8,128)S(1)}, s32[128,128]{1,0:T(8,128)}, u32[]{:S(2)}) copy-start(s32[128,128]{1,0:T(8,128)} %pad.9.table_ref) | copy-start | bytes 196612
  176.4 63.6 %copy-start.1 = (f32[512,128]{1,0:T(8,128)S(1)}, f32[512,128]{1,0:T(8,128)}, u32[]{:S(2)}) copy-start(f32[512,128]{1,0:T(8,128)} %get-tuple-element.30.share_ref) | copy-start | bytes 786436

commit v6 on v5

--- a/solution.py
+++ b/solution.py
@@ -68,9 +68,9 @@
     return jnp.where(left == right, 1.0, 0.0).astype(jnp.bfloat16)
 
 
-ARRIVAL, ARRIVAL3, NEXT3, PLACE, NEXT_PLACE, SEND, SEND3, HALF = 0, 12, 24, 36, 44, 48, 60, 72
-FIRST16, LAST16, SEND_CODE = 73, 81, 89
-SLOT_ROWS, PLACE_ROWS, NEXT_ROWS, PART_ROWS = 12, 8, 4, 8
+ARRIVAL3, PLACE, ARRIVAL, SEND, SEND3, HALF, FIRST16, LAST16, SEND_CODE = 0, 12, 20, 32, 44, 56, 57, 65, 73
+SLOT_ROWS, PLACE_ROWS, PART_ROWS = 12, 8, 8
+SHARED_ROWS = 24
 
 
 def table_row(table_ref, start, count):
@@ -181,18 +181,20 @@
 
 
 def tail_body(table_ref, arrived_ref, tail_ref, held, staged, chosen, load, store):
-    parts, _, wide = held.shape
-    columns = [pl.ds(i * wide, wide) for i in range(parts)]
-    arriving = started(
-        [arrived_ref.at[:, each] for each in columns], [held.at[i] for i in range(parts)], load
-    )
+    width = held.shape[1]
+    arriving = started([arrived_ref.at[:, pl.ds(0, width)]], [held], load)
     first, second = place_cols(table_ref, 1)
-    chosen[...] = match_cols(first + second, table_row(table_ref, ARRIVAL, SLOT_ROWS))
+    row = table_row(table_ref, ARRIVAL, SLOT_ROWS)
+    for i, col in enumerate(first + second):
+        chosen[i * LANES : (i + 1) * LANES] = match(col, row)
+    arriving[0].wait()
     leaving = []
-    for part in range(parts):
-        arriving[part].wait()
-        staged[part] = dot(chosen[...], held[part]).astype(jnp.bfloat16)
-        leaving += started([staged.at[part]], [tail_ref.at[:, columns[part]]], store, part)
+    for i in range(2):
+        staged[i * GROUP : (i + 1) * GROUP] = dot(
+            chosen[i * GROUP : (i + 1) * GROUP], held[...]
+        ).astype(jnp.bfloat16)
+        at = pl.ds(i * GROUP, GROUP)
+        leaving += started([staged.at[at]], [tail_ref.at[at]], store, i)
     for copy in leaving:
         copy.wait()
 
@@ -206,8 +208,8 @@
         out_specs=anywhere(1)[0],
         out_shape=jax.ShapeDtypeStruct((2 * GROUP, width), jnp.bfloat16),
         scratch_shapes=[
-            pltpu.VMEM((4, slots, wide), jnp.bfloat16),
-            pltpu.VMEM((4, 2 * GROUP, wide), jnp.bfloat16),
+            pltpu.VMEM((slots, width), jnp.bfloat16),
+            pltpu.VMEM((2 * GROUP, width), jnp.bfloat16),
             pltpu.VMEM((2 * GROUP, slots), jnp.bfloat16),
             pltpu.SemaphoreType.DMA((4,)),
             pltpu.SemaphoreType.DMA((4,)),
@@ -236,7 +238,7 @@
         columns = slice(local * DH, (local + 1) * DH)
         keys = unit_rows(raw[:, columns])[0].astype(jnp.bfloat16)
         partial, lse = forward_tile(query[:, columns], keys, values[:, columns])
-        out_ref[:, columns] = partial
+        out_ref[:, columns] = partial.astype(jnp.bfloat16)
         delta = jnp.sum(partial * cotangent[:, columns].astype(jnp.float32), -1, keepdims=True)
         head = pair * 2 + local
         stat = jnp.where(lane == head, lse, jnp.where(lane == head + 4, delta, stat))
@@ -308,7 +310,7 @@
         out_specs=[group_spec()] * 5 + [stat_spec()],
         out_shape=[array] * 4
         + [
-            jax.ShapeDtypeStruct((rows, width // 3), jnp.float32),
+            jax.ShapeDtypeStruct((rows, width // 3), jnp.bfloat16),
             jax.ShapeDtypeStruct((rows, 2 * LANES), jnp.float32),
         ],
         scratch_shapes=[pltpu.VMEM((2, 2 * GROUP, slots), jnp.bfloat16)],
@@ -323,56 +325,69 @@
     query_ref,
     value_ref,
     cotangent_ref,
-    prior_query_ref,
-    prior_value_ref,
+    prior_ref,
     second_stat_ref,
     out_ref,
-    stat_ref,
     stats_ref,
+    three,
+    prior,
+    second_stat,
+    staged,
     both,
+    load,
+    store,
 ):
-    pair = pl.program_id(0)
-    hash_round = pl.program_id(1)
-    stat = forward_pair(
-        pair,
-        query_ref[...],
-        jnp.concatenate([prior_query_ref[...], query_ref[...]]),
-        jnp.concatenate([prior_value_ref[...], value_ref[...]]),
-        cotangent_ref[...],
-        out_ref,
-    )
-    stat_ref[...] = stat
-
-    @pl.when(pair == 0)
-    def _():
-        both[hash_round, :GROUP] = stat
-        both[hash_round, GROUP:] = second_stat_ref[...]
-
-    @pl.when(pair == 1)
-    def _():
-        both[hash_round, :GROUP] += stat
-        both[hash_round, GROUP:] += second_stat_ref[...]
-
-    @pl.when((pair == 1) & (hash_round == 1))
-    def _():
-        rows = 4 * GROUP
-        piece = iota((rows, LANES), 1) // (PIECES * STAT)
-        first, second, third = pieces_of(both[...].reshape(rows, LANES))
-        nothing = jnp.zeros((rows, LANES), jnp.bfloat16)
-        stats = jnp.where(
-            piece == 0,
-            first,
-            jnp.where(piece == 1, second, jnp.where(piece == 2, third, nothing)),
-        )
-        place_row = table_row(table_ref, PLACE, PLACE_ROWS)
-        third_slots = stats_ref.shape[0]
-        arrival_cols = table_cols(table_ref, ARRIVAL3, SLOT_ROWS)
-        lane_third = (iota((third_slots, LANES), 1) % (3 * STAT)) // STAT
-        result = jnp.zeros((third_slots, LANES), jnp.float32)
-        for third in range(3):
-            back = match_cols(arrival_cols[4 * third : 4 * third + 4], place_row)
-            result = jnp.where(lane_third == third, dot(back, stats), result)
-        stats_ref[...] = result
+    arriving = started(
+        [query_ref, prior_ref, value_ref, cotangent_ref, second_stat_ref],
+        [three.at[0], prior, three.at[1], three.at[2], second_stat],
+        load,
+    )
+    place_row = table_row(table_ref, PLACE, PLACE_ROWS)
+    arrival_cols = table_cols(table_ref, ARRIVAL3, SLOT_ROWS)
+    for copy in arriving:
+        copy.wait()
+    width = staged.shape[1]
+    leaving = []
+    for hash_round in range(2):
+        kept = slice(hash_round * GROUP, (hash_round + 1) * GROUP)
+        at = pl.ds(hash_round * GROUP, GROUP)
+        stat = 0.0
+        second = 0.0
+        for pair in range(2):
+            columns = slice(pair * 2 * DH, (pair + 1) * 2 * DH)
+            values_at = slice(width + pair * 2 * DH, width + (pair + 1) * 2 * DH)
+            query = three[0, kept, columns]
+            stat = stat + forward_pair(
+                pair,
+                query,
+                jnp.concatenate([prior[kept, columns], query]),
+                jnp.concatenate([prior[kept, values_at], three[1, kept, columns]]),
+                three[2, kept, columns],
+                staged.at[at, pl.ds(pair * 2 * DH, 2 * DH)],
+            )
+            second = second + second_stat[kept, pair * LANES : (pair + 1) * LANES]
+        leaving += started([staged.at[at]], [out_ref.at[at]], store, hash_round)
+        both[2 * hash_round * GROUP : (2 * hash_round + 1) * GROUP] = stat
+        both[(2 * hash_round + 1) * GROUP : (2 * hash_round + 2) * GROUP] = second
+    rows = 4 * GROUP
+    piece = iota((rows, LANES), 1) // (PIECES * STAT)
+    first, second, third = pieces_of(both[...])
+    nothing = jnp.zeros((rows, LANES), jnp.bfloat16)
+    stats = jnp.where(
+        piece == 0,
+        first,
+        jnp.where(piece == 1, second, jnp.where(piece == 2, third, nothing)),
+    )
+    third_slots = stats_ref.shape[0]
+    lane_third = (iota((third_slots, LANES), 1) % (3 * STAT)) // STAT
+    result = jnp.zeros((third_slots, LANES), jnp.float32)
+    for third in range(3):
+        span = slice((0, 0, rows // 2)[third], (rows // 2, rows, rows)[third])
+        back = match_cols(arrival_cols[4 * third : 4 * third + 4], place_row[:, span])
+        result = jnp.where(lane_third == third, dot(back, stats[span]), result)
+    stats_ref[...] = result
+    for copy in leaving:
+        copy.wait()
 
 
 def forward_edge(table, query, value, cotangent, prior_tail, second_stat):
@@ -380,38 +395,40 @@
     third_slots = SLOT_ROWS * LANES // 3
     return pl.pallas_call(
         edge_body,
-        grid=(2, 2),
-        in_specs=[pl.BlockSpec((LANES, LANES), lambda p, r: (0, 0))]
-        + [group_spec()] * 4
-        + [group_spec(2), stat_spec()],
-        out_specs=[
-            group_spec(),
-            stat_spec(),
-            pl.BlockSpec((third_slots, LANES), lambda p, r: (0, 0)),
-        ],
+        in_specs=[table_spec()] + anywhere(5),
+        out_specs=anywhere(1) + [pl.BlockSpec(memory_space=pltpu.VMEM)],
         out_shape=[
-            jax.ShapeDtypeStruct((rows, width), jnp.float32),
-            jax.ShapeDtypeStruct((rows, 2 * LANES), jnp.float32),
+            jax.ShapeDtypeStruct((rows, width), jnp.bfloat16),
             jax.ShapeDtypeStruct((third_slots, LANES), jnp.float32),
         ],
-        scratch_shapes=[pltpu.VMEM((2, 2 * GROUP, LANES), jnp.float32)],
-        compiler_params=params(),
+        scratch_shapes=[
+            pltpu.VMEM((3, rows, width), jnp.bfloat16),
+            pltpu.VMEM((rows, 2 * width), jnp.bfloat16),
+            pltpu.VMEM((rows, 2 * LANES), jnp.float32),
+            pltpu.VMEM((rows, width), jnp.bfloat16),
+            pltpu.VMEM((2 * rows, LANES), jnp.float32),
+            pltpu.SemaphoreType.DMA((5,)),
+            pltpu.SemaphoreType.DMA((2,)),
+        ],
+        compiler_params=params(62),
         cost_estimate=cost(2e9, 4e6, 8 * GROUP * 512),
         name="forward_edge",
-    )(table, query, value, cotangent, prior_tail, prior_tail, second_stat)
+    )(table, query, value, cotangent, prior_tail, second_stat)
 
 
 def gather_stats(codes_row, slot_cols, stats):
     narrow = stats.astype(jnp.bfloat16)
-    total = None
+    half = codes_row.shape[1] // 2
+    sums = [0.0, 0.0]
     for third in range(3):
-        chosen = match_cols(slot_cols[4 * third : 4 * third + 4], codes_row)
-        found = dot(narrow, chosen, 0, 0)
-        for piece in range(PIECES):
-            at = piece * PIECES * STAT + third * STAT
-            part = found[at : at + STAT]
-            total = part if total is None else total + part
-    return total
+        for each in ((0,), (0, 1), (1,))[third]:
+            codes = codes_row[:, each * half : (each + 1) * half]
+            chosen = match_cols(slot_cols[4 * third : 4 * third + 4], codes)
+            found = dot(narrow, chosen, 0, 0)
+            for piece in range(PIECES):
+                at = piece * PIECES * STAT + third * STAT
+                sums[each] = sums[each] + found[at : at + STAT]
+    return jnp.concatenate(sums, axis=1)
 
 
 def found_at_tokens(tokens, table_ref, stats):
@@ -455,7 +472,7 @@
     return pl.pallas_call(
         functools.partial(total_body, tokens),
         out_shape=jax.ShapeDtypeStruct((owners, 2 * STAT, LANES), jnp.float32),
-        compiler_params=params(),
+        compiler_params=params(24),
         cost_estimate=cost(2 * 1536 * 1536 * LANES, 1 << 20),
         name="total_stats",
     )(table, arrived)
@@ -472,7 +489,7 @@
         table_cols(table_ref, ARRIVAL, SLOT_ROWS), table_row(table_ref, PLACE, PLACE_ROWS)
     )
     rows = [first_ref[:GROUP], second_ref[:GROUP], first_ref[GROUP:], second_ref[GROUP:]]
-    payload_ref[...] = dot(back, jnp.concatenate(rows).astype(jnp.bfloat16)).astype(jnp.bfloat16)
+    payload_ref[...] = dot(back, jnp.concatenate(rows)).astype(jnp.bfloat16)
 
 
 def prepare(table, home_stats, outs, tokens):
@@ -594,6 +611,7 @@
 
 def backward_body(
     table_ref,
+    next_table_ref,
     stats_ref,
     head_query_ref,
     head_value_ref,
@@ -629,7 +647,10 @@
     targets = [stats] + [six.at[i] for i in range(6)] + [double.at[i] for i in range(2)]
     arriving = started(sources, targets, load)
     place_row = table_row(table_ref, PLACE, PLACE_ROWS)
-    next_row = table_row(table_ref, NEXT_PLACE, NEXT_ROWS)
+    next_places = table_row(next_table_ref, PLACE, PLACE_ROWS)
+    next_row = jnp.concatenate(
+        [next_places[:, each * per_round : each * per_round + GROUP] for each in range(2)], axis=1
+    )
     back = [
         match_cols(
             table_cols(table_ref, (FIRST16, LAST16)[each], PART_ROWS),
@@ -641,7 +662,7 @@
     own_stats = stats[:, :STAT, :].reshape(-1, LANES)
     next_stats = stats[:, STAT:, :].reshape(-1, LANES)
     found = gather_stats(place_row, table_cols(table_ref, ARRIVAL3, SLOT_ROWS), own_stats)
-    edge = gather_stats(next_row, table_cols(table_ref, NEXT3, SLOT_ROWS), next_stats)
+    edge = gather_stats(next_row, table_cols(next_table_ref, ARRIVAL3, SLOT_ROWS), next_stats)
     for copy in arriving[1:]:
         copy.wait()
     refs = (
@@ -684,15 +705,15 @@
         copy.wait()
 
 
-def backward(table, stats, heads, tail, tail_cotangent, prior_tail, nexts, payload):
+def backward(table, next_table, stats, heads, tail, tail_cotangent, prior_tail, nexts, payload):
     slots = SLOT_ROWS * LANES
     rows, width = heads[0].shape
     return pl.pallas_call(
         backward_body,
-        in_specs=[table_spec()] + anywhere(10),
+        in_specs=[table_spec(), pl.BlockSpec(next_table.shape, lambda *_: (0, 0))] + anywhere(10),
         out_specs=anywhere(1)[0],
         out_shape=jax.ShapeDtypeStruct((slots, 3 * width), jnp.bfloat16),
-        input_output_aliases={10: 0},
+        input_output_aliases={11: 0},
         scratch_shapes=[
             pltpu.VMEM(stats.shape, jnp.float32),
             pltpu.VMEM((6, rows, width), jnp.bfloat16),
@@ -705,7 +726,7 @@
         compiler_params=params(62),
         cost_estimate=cost(8e9, 1.5e7, 3e6),
         name="backward",
-    )(table, stats, *heads, tail, tail_cotangent, prior_tail, *nexts, payload)
+    )(table, next_table, stats, *heads, tail, tail_cotangent, prior_tail, *nexts, payload)
 
 
 def combine_body(
@@ -725,27 +746,41 @@
     chosen[0] = match(token, code)
     chosen[1] = match(token + tokens, code)
     chosen[2] = match(token, table_row(table_ref, SEND, SLOT_ROWS))
+    width = parts * wide // 3
     leaving = []
-    for part in range(parts):
-        arrived = arrived_ref[:, part * wide : (part + 1) * wide]
-        if part < 2:
-            found = 0.0
-            for each in range(2):
-                at = 4 * each + 2 * part
-                share = jnp.concatenate(
-                    [
-                        jnp.broadcast_to(share_ref[:, at + i : at + i + 1], (tokens, DH))
-                        for i in range(2)
-                    ],
-                    axis=1,
-                )
-                found = found + share * dot(chosen[each], arrived)
-            target = out_ref.at[:, pl.ds(part * wide, wide)]
-        else:
-            found = dot(chosen[2], arrived)
-            target = (first_ref, second_ref)[part % 2].at[:, pl.ds((part // 2 - 1) * wide, wide)]
-        staged[part] = found.astype(jnp.bfloat16)
-        leaving += started([staged.at[part]], [target], store, part)
+    for half in range(2):
+        kept = slice(half * tokens // 2, (half + 1) * tokens // 2)
+        at = pl.ds(half * tokens // 2, tokens // 2)
+        slopes = dot(chosen[2, kept], arrived_ref[:, width:]).astype(jnp.bfloat16)
+        for place in range(4):
+            staged[2 + place, kept] = slopes[:, place * wide : (place + 1) * wide]
+            leaving += started(
+                [staged.at[2 + place, at]],
+                [(first_ref, second_ref)[place % 2].at[at, pl.ds((place // 2) * wide, wide)]],
+                store,
+                half * parts + 2 + place,
+            )
+        found = 0.0
+        for each in range(2):
+            share = jnp.concatenate(
+                [
+                    jnp.broadcast_to(
+                        share_ref[kept, 4 * each + head : 4 * each + head + 1], (tokens // 2, DH)
+                    )
+                    for head in range(4)
+                ],
+                axis=1,
+            )
+            found = found + share * dot(chosen[each, kept], arrived_ref[:, :width])
+        found = found.astype(jnp.bfloat16)
+        for place in range(2):
+            staged[place, kept] = found[:, place * wide : (place + 1) * wide]
+            leaving += started(
+                [staged.at[place, at]],
+                [out_ref.at[at, pl.ds(place * wide, wide)]],
+                store,
+                half * parts + place,
+            )
     for copy in leaving:
         copy.wait()
 
@@ -762,7 +797,7 @@
         scratch_shapes=[
             pltpu.VMEM((6, tokens, wide), jnp.bfloat16),
             pltpu.VMEM((3, tokens, slots), jnp.bfloat16),
-            pltpu.SemaphoreType.DMA((6,)),
+            pltpu.SemaphoreType.DMA((12,)),
         ],
         compiler_params=params(40),
         cost_estimate=cost(2 * slots * tokens * width, 2 * (slots + tokens) * width),
@@ -803,24 +838,17 @@
         codes = jnp.where(within < counts[:, :, None], start[:, :, None] + within, -1)
         return by_owner(codes)
 
-    tables = jnp.concatenate([arrival_count, receive_slot], axis=1)
-    packed, mine, following = lax.optimization_barrier(
-        (packed, to_place(tables), to_place_prior(tables[:, : owners + GROUP]))
-    )
-    arrival = arrivals(mine[:, :owners])
-    next_arrival = arrivals(following[:, :owners])
-    place = mine[:, owners:] + code
-    next_place = following[:, owners:] + code
+    tables = to_place(jnp.concatenate([arrival_count, receive_slot], axis=1))
+    arrival = arrivals(tables[:, :owners])
+    place = tables[:, owners:] + code
 
     def half_blocks(codes, first):
         return codes[:, first : first + 2 * STAT]
 
     members = [
+        (ARRIVAL3, by_third(arrival)),
+        (PLACE, place),
         (ARRIVAL, arrival),
-        (ARRIVAL3, by_third(arrival)),
-        (NEXT3, by_third(next_arrival)),
-        (PLACE, place),
-        (NEXT_PLACE, next_place),
         (SEND, send),
         (SEND3, by_third(by_owner(send_rows + code))),
         (HALF, jnp.full((1, LANES), half, jnp.int32)),
@@ -839,9 +867,11 @@
     head_query, head_value, head_cotangent, tail_cotangent, out_second, stat_second = forward_own(
         table, arrived, tail
     )
-    out_first, stat_first, stats = forward_edge(
+    out_first, stats = forward_edge(
         table, head_query, head_value, head_cotangent, prior_tail, stat_second
     )
+    shared, stats = lax.optimization_barrier((table[:SHARED_ROWS], stats))
+    next_table = to_prior(shared)
     next_query = to_prior(head_query)
     next_cotangent = to_prior(head_cotangent)
     home_stats = exchange(stats.reshape(owners, STAT, LANES)).reshape(-1, LANES)
@@ -849,6 +879,7 @@
     payload, shares = prepare(table, home_stats, (out_first, out_second), tokens)
     payload = backward(
         table,
+        next_table,
         totals,
         (head_query, head_value, head_cotangent),
         tail,

time: 245 us -> 230 us (0.939)
  blocking collectives: 63.6 us -> 58 us
  waiting for transfers between devices: 70.9 us -> 66.2 us
  Pallas kernels: 60.2 us -> 56.9 us
    all_to_all x1, blocking collectives: 63.6 us -> 58 us  [exchange(): return lax.all_to_all(block, 'seq', split_axis=0, concat_axis=0, tiled=True)]
    all_to_all x3, waiting for transfers between devices: 63.1 us -> 57.8 us  [exchange(): return lax.all_to_all(block, 'seq', split_axis=0, concat_axis=0, tiled=True)]
    ppermute x5, starting transfers between devices: 21 us -> 16.6 us  [routed(): return lax.ppermute(block, ('seq', 'head'), route)]
    all_to_all x3, starting transfers between devices: 18.1 us -> 22.3 us  [exchange(): return lax.all_to_all(block, 'seq', split_axis=0, concat_axis=0, tiled=True)]
  transfers between devices with their start and end apart: 8 -> 8, of which waited for: 4 -> 3; matrix products, arithmetic and copies ran while one was open for 3% -> 2% of each run, Pallas kernels for 11% -> 8%
where the time goes in v6:
time: 230 us; the launch traced here: 229 us
  waiting for transfers between devices  66.2 us (29%)
  blocking collectives  58 us (25%)
  Pallas kernels  56.9 us (25%)
  starting transfers between devices  38.9 us (17%)
  local copies, waits for them, and re-layouts  7.18 us (3%)
    all_to_all x1, blocking collectives, exchange(): return lax.all_to_all(block, 'seq', split_axis=0, concat_axis=0, tiled=True)  58 us
    all_to_all x3, waiting for transfers between devices, exchange(): return lax.all_to_all(block, 'seq', split_axis=0, concat_axis=0, tiled=True)  57.8 us
    all_to_all x3, starting transfers between devices, exchange(): return lax.all_to_all(block, 'seq', split_axis=0, concat_axis=0, tiled=True)  22.3 us
    ppermute x5, starting transfers between devices, routed(): return lax.ppermute(block, ('seq', 'head'), route)  16.6 us
    pallas_call x1, Pallas kernels, backward(): pl.pallas_call(backward_body, in_specs=[table_spec(), pl.BlockSpec(next_t...  15.1 us
    pallas_call x1, Pallas kernels, forward_own(): pl.pallas_call(own_body, grid=(2, 2), in_specs=[pl.BlockSpec((LANES, LANE...  11.2 us
    ppermute x5, waiting for transfers between devices, routed(): return lax.ppermute(block, ('seq', 'head'), route)  8.45 us
    pallas_call x1, Pallas kernels, forward_edge(): pl.pallas_call(edge_body, in_specs=[table_spec()] + anywhere(5), out_spec...  7.85 us
  transfers between devices with their start and end apart: 8, of which 3 were waited for; matrix products, arithmetic and copies ran while one was open for 2% of the time, Pallas kernels for 8%

profile of v6, /device:TPU:0, one launch (start us, length us, event | category | flops | bytes accessed | tf_op | source)
XLA Modules:
  0.0 229.1 jit_solution(18002429679035866775)
XLA Ops:
  0.6 0.8 reshape.73
  2.3 5.9 %pack_rows.1 = bf16[1536,1536]{1,0:T(8,128)(2,1)} custom-call(s32[16,128]{1,0:T(8,128)} %pad.8.index_ref, bf16[512,512]{1,0:T(8,128)(2,1)} %refs_0_.1, bf16[512,512]{1,0:T(8,128)(2,1)} %refs_1_.1, bf16[512,512]{1,0:T(8,128)(2,1)} %refs_2_.1), custom_call_target="tpu_custom_call" | custom-call | flops 2415919104 | bytes 6291456 | tf_op jit(solution)/shard_map/pack_rows/pallas_call | solution.py:158
  8.2 11.7 %all-to-all-start = ((bf16[64,24,1536]{2,1,0:T(8,128)(2,1)}), bf16[64,24,1536]{2,1,0:T(8,128)(2,1)}, u32[]{:S(2)}, u32[]{:S(2)}) async-start(bf16[64,24,1536]{2,1,0:T(8,128)(2,1)} %bitcast.30), calls=%async_computation | async-start | bytes 9437184 | tf_op jit(solution)/shard_map/all_to_all | solution.py:64
  20.1 0.7 collective-permute-start
  23.5 0.6 pad.9.table_ref
  24.1 54.5 %all-to-all-done = bf16[64,24,1536]{2,1,0:T(8,128)(2,1)} async-done(((bf16[64,24,1536]{2,1,0:T(8,128)(2,1)}), bf16[64,24,1536]{2,1,0:T(8,128)(2,1)}, u32[]{:S(2)}, u32[]{:S(2)}) %all-to-all-start) | async-done | bytes 4718624 | tf_op jit(solution)/shard_map/all_to_all | solution.py:64
  78.6 5.4 %sort_tail.1.tail_query_ref.tail_value_ref.tail_ref = bf16[512,1024]{1,0:T(8,128)(2,1)} custom-call(s32[128,128]{1,0:T(8,128)} %pad.9.table_ref, bf16[1536,1536]{1,0:T(8,128)(2,1)} %bitcast.2.arrived_ref.arrived_query_ref.arrived_value_ref.arrived_cotangent_ref), custom_call_target="tpu_custom_call" | custom-call | flops 1610612736 | bytes 4194304 | tf_op jit(solution)/shard_map/sort_tail/pallas_call | solution.py:205
  84.4 0.7 slice.19
  85.1 11.2 %forward_own.1 = (bf16[512,512]{1,0:T(8,128)(2,1)}, bf16[512,512]{1,0:T(8,128)(2,1)}, bf16[512,512]{1,0:T(8,128)(2,1)}, bf16[512,512]{1,0:T(8,128)(2,1)}, bf16[512,512]{1,0:T(8,128)(2,1)}, /*index=5*/f32[512,256]{1,0:T(8,128)}) custom-call(s32[128,128]{1,0:T(8,128)} %pad.9.table_ref, ...), custom_call_target="tpu_custom_call" | custom-call | flops 5000000000 | bytes 10000000 | tf_op jit(solution)/shard_map/forward_own/pallas_call | solution.py:304
  96.3 8.4 %collective-permute-done.1.prior_ref = bf16[512,1024]{1,0:T(8,128)(2,1)S(1)} collective-permute-done((bf16[512,1024]{1,0:T(8,128)(2,1)}, bf16[512,1024]{1,0:T(8,128)(2,1)S(1)}, u32[]{:S(2)}, u32[]{:S(2)}) %collective-permute-start.1) | collective-permute-done | bytes 1048608 | tf_op jit(solution)/shard_map/ppermute | solution.py:44
  104.7 1.0 copy-done.7
  105.7 7.9 %forward_edge.1 = (bf16[512,512]{1,0:T(8,128)(2,1)}, f32[512,128]{1,0:T(8,128)}) custom-call(s32[128,128]{1,0:T(8,128)} %pad.9.table_ref, bf16[512,512]{1,0:T(8,128)(2,1)} %get-tuple-element.19.query_ref.head_query_ref, bf16[512,512]{1,0:T(8,128)(2,1)} %get-tuple-element.20.value_ref.head_value_ref, ...), custom_call_target="tpu_custom_call" | custom-call | flops 2000000000 | bytes 4000000 | tf_op jit(solution)/shard_map/forward_edge/pallas_call | solution.py:396
  113.5 5.9 %all-to-all-start.1 = ((f32[64,8,128]{2,1,0:T(8,128)}), f32[64,8,128]{2,1,0:T(8,128)S(1)}, u32[]{:S(2)}, u32[]{:S(2)}) async-start(f32[64,8,128]{2,1,0:T(8,128)} %bitcast.32), calls=%async_computation.1 | async-start | bytes 524288 | tf_op jit(solution)/shard_map/all_to_all | solution.py:64
  119.4 7.4 %collective-permute-start.3 = (bf16[512,512]{1,0:T(8,128)(2,1)}, bf16[512,512]{1,0:T(8,128)(2,1)S(1)}, u32[]{:S(2)}, u32[]{:S(2)}) collective-permute-start(bf16[512,512]{1,0:T(8,128)(2,1)} %get-tuple-element.19.query_ref.head_query_ref), channel_id=1, source_target_pairs={{0,126},{1,3},{2,0},{3,5},{4,2},{5,7},{6,4},{7,9},{8,6},{9,11},{10... | collective-permute-start | bytes 1572872 | tf_op jit(solution)/shard_map/ppermute | solution.py:44
  126.8 0.9 collective-permute-start.4
  127.7 3.3 %all-to-all-done.1 = f32[64,8,128]{2,1,0:T(8,128)S(1)} async-done(((f32[64,8,128]{2,1,0:T(8,128)}), f32[64,8,128]{2,1,0:T(8,128)S(1)}, u32[]{:S(2)}, u32[]{:S(2)}) %all-to-all-start.1) | async-done | bytes 262176 | tf_op jit(solution)/shard_map/all_to_all | solution.py:64
  131.0 2.1 total_stats.1
  133.1 4.6 %all-to-all-start.2 = ((f32[64,16,128]{2,1,0:T(8,128)}), f32[64,16,128]{2,1,0:T(8,128)S(1)}, u32[]{:S(2)}, u32[]{:S(2)}) async-start(f32[64,16,128]{2,1,0:T(8,128)} %total_stats.1), calls=%async_computation.2 | async-start | bytes 1048576 | tf_op jit(solution)/shard_map/all_to_all | solution.py:64
  137.7 7.4 %collective-permute-start.2 = (s32[24,128]{1,0:T(8,128)S(1)}, s32[24,128]{1,0:T(8,128)S(1)}, u32[]{:S(2)}, u32[]{:S(2)}) collective-permute-start(s32[24,128]{1,0:T(8,128)S(1)} %slice.19), channel_id=1, source_target_pairs={{0,126},{1,3},{2,0},{3,5},{4,2},{5,7},{6,4},{7,9},{8,6},{9,11},{10... | collective-permute-start | bytes 36872 | tf_op jit(solution)/shard_map/ppermute | solution.py:44
  145.1 5.1 %prepare_outputs.1 = (bf16[1536,1536]{1,0:T(8,128)(2,1)}, f32[512,128]{1,0:T(8,128)}) custom-call(s32[128,128]{1,0:T(8,128)} %pad.9.table_ref, f32[512,128]{1,0:T(8,128)} %bitcast.29, bf16[512,512]{1,0:T(8,128)(2,1)} %get-tuple-element.25.first_ref, bf16[512,512]{1,0:T(8,128)(2,1)} %get-tuple-element.26.second_ref), custom_call_target="tpu_custom_call" | custom-call | flops 2000000000 | bytes 10000000 | tf_op jit(solution)/shard_map/prepare_outputs/pallas_call | solution.py:499
  150.3 0.7 copy-done.8
  151.5 15.1 %backward.1 = bf16[1536,1536]{1,0:T(8,128)(2,1)} custom-call(s32[128,128]{1,0:T(8,128)} %pad.9.table_ref, s32[24,128]{1,0:T(8,128)} %copy-done.10, f32[64,16,128]{2,1,0:T(8,128)} %copy-done.4, bf16[512,512]{1,0:T(8,128)(2,1)} %get-tuple-element.19.query_ref.head_query_ref, ...), custom_call_target="tpu_custom_call", output_to_operand_aliasing={{}: (11, {})} | custom-call | flops 8000000000 | bytes 15000000 | tf_op jit(solution)/shard_map/backward/pallas_call | solution.py:711
  166.6 58.0 %all_to_all.20 = bf16[64,24,1536]{2,1,0:T(8,128)(2,1)S(1)} all-to-all(bf16[64,24,1536]{2,1,0:T(8,128)(2,1)} %bitcast.31), channel_id=1, replica_groups=mesh['seq'=64,'head'=2] {'seq'}, dimensions={0} | all-to-all | bytes 9437184 | tf_op jit(solution)/shard_map/all_to_all | solution.py:64
  224.6 4.3 %combine_rows.1 = (bf16[512,512]{1,0:T(8,128)(2,1)}, bf16[512,512]{1,0:T(8,128)(2,1)}, bf16[512,512]{1,0:T(8,128)(2,1)}) custom-call(s32[128,128]{1,0:T(8,128)S(1)} %copy-done.2, f32[512,128]{1,0:T(8,128)S(1)} %copy-done.3, bf16[1536,1536]{1,0:T(8,128)(2,1)S(1)} %bitcast.27), custom_call_target="tpu_custom_call" | custom-call | flops 2415919104 | bytes 6291456 | tf_op jit(solution)/shard_map/combine_rows/pallas_call | solution.py:791
  (68 shorter events, 4.4 us)
Async XLA Ops:
  8.2 11.8 %copy-start.5 = (s32[2,512]{1,0:T(2,128)S(1)}, s32[2,512]{1,0:T(2,128)}, u32[]{:S(2)}) copy-start(s32[2,512]{1,0:T(2,128)} %param.11) | copy-start | bytes 12292
  8.2 11.8 %copy-start.6 = (s32[2,64]{1,0:T(2,128)S(1)}, s32[2,64]{1,0:T(2,128)}, u32[]{:S(2)}) copy-start(s32[2,64]{1,0:T(2,128)} %param.10) | copy-start | bytes 1540
  8.2 70.4 %all-to-all-start = ((bf16[64,24,1536]{2,1,0:T(8,128)(2,1)}), bf16[64,24,1536]{2,1,0:T(8,128)(2,1)}, u32[]{:S(2)}, u32[]{:S(2)}) async-start(bf16[64,24,1536]{2,1,0:T(8,128)(2,1)} %bitcast.30), calls=%async_computation | async-start | bytes 9437184 | tf_op jit(solution)/shard_map/all_to_all | solution.py:64
  20.1 1.3 collective-permute-start
  84.0 20.7 %collective-permute-start.1 = (bf16[512,1024]{1,0:T(8,128)(2,1)}, bf16[512,1024]{1,0:T(8,128)(2,1)S(1)}, u32[]{:S(2)}, u32[]{:S(2)}) collective-permute-start(bf16[512,1024]{1,0:T(8,128)(2,1)} %sort_tail.1.tail_query_ref.tail_value_ref.tail_ref), channel_id=1, source_target_pairs={{0,2},{1,127},{2,4},{3,1},{4,6},{5,3},{6,8},{7,5},{8,10},{9,7},{10... | collective-permute-start | bytes 3145736 | tf_op jit(solution)/shard_map/ppermute | solution.py:44
  96.2 34.7 %copy-start.1 = (s32[128,128]{1,0:T(8,128)S(1)}, s32[128,128]{1,0:T(8,128)}, u32[]{:S(2)}) copy-start(s32[128,128]{1,0:T(8,128)} %pad.9.table_ref) | copy-start | bytes 196612
  104.7 1.0 copy-start.7
  113.5 17.4 %all-to-all-start.1 = ((f32[64,8,128]{2,1,0:T(8,128)}), f32[64,8,128]{2,1,0:T(8,128)S(1)}, u32[]{:S(2)}, u32[]{:S(2)}) async-start(f32[64,8,128]{2,1,0:T(8,128)} %bitcast.32), calls=%async_computation.1 | async-start | bytes 524288 | tf_op jit(solution)/shard_map/all_to_all | solution.py:64
  119.4 30.8 %collective-permute-start.3 = (bf16[512,512]{1,0:T(8,128)(2,1)}, bf16[512,512]{1,0:T(8,128)(2,1)S(1)}, u32[]{:S(2)}, u32[]{:S(2)}) collective-permute-start(bf16[512,512]{1,0:T(8,128)(2,1)} %get-tuple-element.19.query_ref.head_query_ref), channel_id=1, source_target_pairs={{0,126},{1,3},{2,0},{3,5},{4,2},{5,7},{6,4},{7,9},{8,6},{9,11},{10... | collective-permute-start | bytes 1572872 | tf_op jit(solution)/shard_map/ppermute | solution.py:44
  126.8 23.4 %collective-permute-start.4 = (bf16[512,512]{1,0:T(8,128)(2,1)}, bf16[512,512]{1,0:T(8,128)(2,1)S(1)}, u32[]{:S(2)}, u32[]{:S(2)}) collective-permute-start(bf16[512,512]{1,0:T(8,128)(2,1)} %get-tuple-element.21.cotangent_ref.head_cotangent_ref), channel_id=1, source_target_pairs={{0,126},{1,3},{2,0},{3,5},{4,2},{5,7},{6,4},{7,9},{8,6},{9,11},{10... | collective-permute-start | bytes 1572872 | tf_op jit(solution)/shard_map/ppermute | solution.py:44
  131.0 14.1 %copy-start = (f32[64,8,128]{2,1,0:T(8,128)}, f32[64,8,128]{2,1,0:T(8,128)S(1)}, u32[]{:S(2)}) copy-start(f32[64,8,128]{2,1,0:T(8,128)S(1)} %all-to-all-done.1) | copy-start | bytes 786436
  133.1 17.2 %all-to-all-start.2 = ((f32[64,16,128]{2,1,0:T(8,128)}), f32[64,16,128]{2,1,0:T(8,128)S(1)}, u32[]{:S(2)}, u32[]{:S(2)}) async-start(f32[64,16,128]{2,1,0:T(8,128)} %total_stats.1), calls=%async_computation.2 | async-start | bytes 1048576 | tf_op jit(solution)/shard_map/all_to_all | solution.py:64
  137.7 12.6 %collective-permute-start.2 = (s32[24,128]{1,0:T(8,128)S(1)}, s32[24,128]{1,0:T(8,128)S(1)}, u32[]{:S(2)}, u32[]{:S(2)}) collective-permute-start(s32[24,128]{1,0:T(8,128)S(1)} %slice.19), channel_id=1, source_target_pairs={{0,126},{1,3},{2,0},{3,5},{4,2},{5,7},{6,4},{7,9},{8,6},{9,11},{10... | collective-permute-start | bytes 36872 | tf_op jit(solution)/shard_map/ppermute | solution.py:44
  150.2 0.8 copy-start.8
  150.3 1.1 copy-start.9
  150.3 1.0 copy-start.10
  150.3 1.2 copy-start.4
  166.6 58.0 %copy-start.2 = (s32[128,128]{1,0:T(8,128)S(1)}, s32[128,128]{1,0:T(8,128)}, u32[]{:S(2)}) copy-start(s32[128,128]{1,0:T(8,128)} %pad.9.table_ref) | copy-start | bytes 196612
  166.6 58.0 %copy-start.3 = (f32[512,128]{1,0:T(8,128)S(1)}, f32[512,128]{1,0:T(8,128)}, u32[]{:S(2)}) copy-start(f32[512,128]{1,0:T(8,128)} %get-tuple-element.27.share_ref) | copy-start | bytes 786436

commit v7 on v6

--- a/solution.py
+++ b/solution.py
@@ -337,22 +337,27 @@
     load,
     store,
 ):
-    arriving = started(
-        [query_ref, prior_ref, value_ref, cotangent_ref, second_stat_ref],
-        [three.at[0], prior, three.at[1], three.at[2], second_stat],
-        load,
-    )
+    each = [pl.ds(hash_round * GROUP, GROUP) for hash_round in range(2)]
+    arriving = [
+        started(
+            [source.at[at] for source in (query_ref, prior_ref, value_ref, cotangent_ref)],
+            [three.at[0, at], prior.at[at], three.at[1, at], three.at[2, at]],
+            load,
+            4 * hash_round,
+        )
+        for hash_round, at in enumerate(each)
+    ]
+    arriving[1] += started([second_stat_ref], [second_stat], load, 8)
     place_row = table_row(table_ref, PLACE, PLACE_ROWS)
     arrival_cols = table_cols(table_ref, ARRIVAL3, SLOT_ROWS)
-    for copy in arriving:
-        copy.wait()
     width = staged.shape[1]
     leaving = []
     for hash_round in range(2):
         kept = slice(hash_round * GROUP, (hash_round + 1) * GROUP)
-        at = pl.ds(hash_round * GROUP, GROUP)
+        at = each[hash_round]
+        for copy in arriving[hash_round]:
+            copy.wait()
         stat = 0.0
-        second = 0.0
         for pair in range(2):
             columns = slice(pair * 2 * DH, (pair + 1) * 2 * DH)
             values_at = slice(width + pair * 2 * DH, width + (pair + 1) * 2 * DH)
@@ -365,10 +370,13 @@
                 three[2, kept, columns],
                 staged.at[at, pl.ds(pair * 2 * DH, 2 * DH)],
             )
-            second = second + second_stat[kept, pair * LANES : (pair + 1) * LANES]
         leaving += started([staged.at[at]], [out_ref.at[at]], store, hash_round)
         both[2 * hash_round * GROUP : (2 * hash_round + 1) * GROUP] = stat
-        both[(2 * hash_round + 1) * GROUP : (2 * hash_round + 2) * GROUP] = second
+    for hash_round in range(2):
+        kept = slice(hash_round * GROUP, (hash_round + 1) * GROUP)
+        both[(2 * hash_round + 1) * GROUP : (2 * hash_round + 2) * GROUP] = (
+            second_stat[kept, :LANES] + second_stat[kept, LANES:]
+        )
     rows = 4 * GROUP
     piece = iota((rows, LANES), 1) // (PIECES * STAT)
     first, second, third = pieces_of(both[...])
@@ -407,10 +415,10 @@
             pltpu.VMEM((rows, 2 * LANES), jnp.float32),
             pltpu.VMEM((rows, width), jnp.bfloat16),
             pltpu.VMEM((2 * rows, LANES), jnp.float32),
-            pltpu.SemaphoreType.DMA((5,)),
+            pltpu.SemaphoreType.DMA((9,)),
             pltpu.SemaphoreType.DMA((2,)),
         ],
-        compiler_params=params(62),
+        compiler_params=params(59),
         cost_estimate=cost(2e9, 4e6, 8 * GROUP * 512),
         name="forward_edge",
     )(table, query, value, cotangent, prior_tail, second_stat)
@@ -723,7 +731,7 @@
             pltpu.SemaphoreType.DMA((9,)),
             pltpu.SemaphoreType.DMA((4,)),
         ],
-        compiler_params=params(62),
+        compiler_params=params(57),
         cost_estimate=cost(8e9, 1.5e7, 3e6),
         name="backward",
     )(table, next_table, stats, *heads, tail, tail_cotangent, prior_tail, *nexts, payload)
@@ -839,6 +847,7 @@
         return by_owner(codes)
 
     tables = to_place(jnp.concatenate([arrival_count, receive_slot], axis=1))
+    packed, tables = lax.optimization_barrier((packed, tables))
     arrival = arrivals(tables[:, :owners])
     place = tables[:, owners:] + code
 

time: 230 us -> 237 us (1.030)
  blocking collectives: 58 us -> 63.2 us
  starting transfers between devices: 38.9 us -> 42.4 us
    all_to_all x1, blocking collectives: 58 us -> 63.2 us  [exchange(): return lax.all_to_all(block, 'seq', split_axis=0, concat_axis=0, tiled=True)]
  transfers between devices with their start and end apart: 8 -> 8, of which waited for: 3 -> 4; matrix products, arithmetic and copies ran while one was open for 2% -> 2% of each run, Pallas kernels for 8% -> 10%
where the time goes in v7:
time: 237 us; the launch traced here: 236 us
  waiting for transfers between devices  64.5 us (27%)
  blocking collectives  63.2 us (27%)
  Pallas kernels  56.6 us (24%)
  starting transfers between devices  42.4 us (18%)
  local copies, waits for them, and re-layouts  6.84 us (3%)
    all_to_all x1, blocking collectives, exchange(): return lax.all_to_all(block, 'seq', split_axis=0, concat_axis=0, tiled=True)  63.2 us
    all_to_all x3, waiting for transfers between devices, exchange(): return lax.all_to_all(block, 'seq', split_axis=0, concat_axis=0, tiled=True)  57.4 us
    all_to_all x3, starting transfers between devices, exchange(): return lax.all_to_all(block, 'seq', split_axis=0, concat_axis=0, tiled=True)  24.3 us
    ppermute x5, starting transfers between devices, routed(): return lax.ppermute(block, ('seq', 'head'), route)  18.1 us
    pallas_call x1, Pallas kernels, backward(): pl.pallas_call(backward_body, in_specs=[table_spec(), pl.BlockSpec(next_t...  15.1 us
    pallas_call x1, Pallas kernels, forward_own(): pl.pallas_call(own_body, grid=(2, 2), in_specs=[pl.BlockSpec((LANES, LANE...  11.2 us
    pallas_call x1, Pallas kernels, forward_edge(): pl.pallas_call(edge_body, in_specs=[table_spec()] + anywhere(5), out_spec...  7.63 us
    ppermute x5, waiting for transfers between devices, routed(): return lax.ppermute(block, ('seq', 'head'), route)  7.02 us
  transfers between devices with their start and end apart: 8, of which 4 were waited for; matrix products, arithmetic and copies ran while one was open for 2% of the time, Pallas kernels for 10%

profile of v7, /device:TPU:0, one launch (start us, length us, event | category | flops | bytes accessed | tf_op | source)
XLA Modules:
  0.0 235.9 jit_solution(12570572745211818236)
XLA Ops:
  0.6 0.8 pad_add_fusion
  2.1 0.8 reshape.73
  3.8 5.8 %pack_rows.1 = bf16[1536,1536]{1,0:T(8,128)(2,1)} custom-call(s32[16,128]{1,0:T(8,128)} %pad.8.index_ref, bf16[512,512]{1,0:T(8,128)(2,1)} %refs_0_.1, bf16[512,512]{1,0:T(8,128)(2,1)} %refs_1_.1, bf16[512,512]{1,0:T(8,128)(2,1)} %refs_2_.1), custom_call_target="tpu_custom_call" | custom-call | flops 2415919104 | bytes 6291456 | tf_op jit(solution)/shard_map/pack_rows/pallas_call | solution.py:158
  9.6 11.7 %all-to-all-start = ((bf16[64,24,1536]{2,1,0:T(8,128)(2,1)}), bf16[64,24,1536]{2,1,0:T(8,128)(2,1)}, u32[]{:S(2)}, u32[]{:S(2)}) async-start(bf16[64,24,1536]{2,1,0:T(8,128)(2,1)} %bitcast.30), calls=%async_computation | async-start | bytes 9437184 | tf_op jit(solution)/shard_map/all_to_all | solution.py:64
  24.7 53.0 %all-to-all-done = bf16[64,24,1536]{2,1,0:T(8,128)(2,1)} async-done(((bf16[64,24,1536]{2,1,0:T(8,128)(2,1)}), bf16[64,24,1536]{2,1,0:T(8,128)(2,1)}, u32[]{:S(2)}, u32[]{:S(2)}) %all-to-all-start) | async-done | bytes 4718624 | tf_op jit(solution)/shard_map/all_to_all | solution.py:64
  77.7 5.4 %sort_tail.1.tail_query_ref.tail_value_ref.tail_ref = bf16[512,1024]{1,0:T(8,128)(2,1)} custom-call(s32[128,128]{1,0:T(8,128)} %pad.9.table_ref, bf16[1536,1536]{1,0:T(8,128)(2,1)} %bitcast.2.arrived_ref.arrived_query_ref.arrived_value_ref.arrived_cotangent_ref), custom_call_target="tpu_custom_call" | custom-call | flops 1610612736 | bytes 4194304 | tf_op jit(solution)/shard_map/sort_tail/pallas_call | solution.py:205
  83.1 1.8 collective-permute-start.1
  85.6 11.2 %forward_own.1 = (bf16[512,512]{1,0:T(8,128)(2,1)}, bf16[512,512]{1,0:T(8,128)(2,1)}, bf16[512,512]{1,0:T(8,128)(2,1)}, bf16[512,512]{1,0:T(8,128)(2,1)}, bf16[512,512]{1,0:T(8,128)(2,1)}, /*index=5*/f32[512,256]{1,0:T(8,128)}) custom-call(s32[128,128]{1,0:T(8,128)} %pad.9.table_ref, ...), custom_call_target="tpu_custom_call" | custom-call | flops 5000000000 | bytes 10000000 | tf_op jit(solution)/shard_map/forward_own/pallas_call | solution.py:304
  96.8 7.0 %collective-permute-done.1.prior_ref = bf16[512,1024]{1,0:T(8,128)(2,1)S(1)} collective-permute-done((bf16[512,1024]{1,0:T(8,128)(2,1)}, bf16[512,1024]{1,0:T(8,128)(2,1)S(1)}, u32[]{:S(2)}, u32[]{:S(2)}) %collective-permute-start.1) | collective-permute-done | bytes 1048608 | tf_op jit(solution)/shard_map/ppermute | solution.py:44
  103.8 1.0 copy-done.5
  104.8 7.6 %forward_edge.1 = (bf16[512,512]{1,0:T(8,128)(2,1)}, f32[512,128]{1,0:T(8,128)}) custom-call(s32[128,128]{1,0:T(8,128)} %pad.9.table_ref, bf16[512,512]{1,0:T(8,128)(2,1)} %get-tuple-element.23.query_ref.head_query_ref, bf16[512,512]{1,0:T(8,128)(2,1)} %get-tuple-element.24.value_ref.head_value_ref, ...), custom_call_target="tpu_custom_call" | custom-call | flops 2000000000 | bytes 4000000 | tf_op jit(solution)/shard_map/forward_edge/pallas_call | solution.py:404
  112.4 7.6 %all-to-all-start.1 = ((f32[64,8,128]{2,1,0:T(8,128)}), f32[64,8,128]{2,1,0:T(8,128)S(1)}, u32[]{:S(2)}, u32[]{:S(2)}) async-start(f32[64,8,128]{2,1,0:T(8,128)} %bitcast.32), calls=%async_computation.1 | async-start | bytes 524288 | tf_op jit(solution)/shard_map/all_to_all | solution.py:64
  120.0 7.4 %collective-permute-start.3 = (bf16[512,512]{1,0:T(8,128)(2,1)}, bf16[512,512]{1,0:T(8,128)(2,1)S(1)}, u32[]{:S(2)}, u32[]{:S(2)}) collective-permute-start(bf16[512,512]{1,0:T(8,128)(2,1)} %get-tuple-element.23.query_ref.head_query_ref), channel_id=1, source_target_pairs={{0,126},{1,3},{2,0},{3,5},{4,2},{5,7},{6,4},{7,9},{8,6},{9,11},{10... | collective-permute-start | bytes 1572872 | tf_op jit(solution)/shard_map/ppermute | solution.py:44
  127.4 0.9 collective-permute-start.4
  128.2 2.5 %all-to-all-done.1 = f32[64,8,128]{2,1,0:T(8,128)S(1)} async-done(((f32[64,8,128]{2,1,0:T(8,128)}), f32[64,8,128]{2,1,0:T(8,128)S(1)}, u32[]{:S(2)}, u32[]{:S(2)}) %all-to-all-start.1) | async-done | bytes 262176 | tf_op jit(solution)/shard_map/all_to_all | solution.py:64
  130.8 2.1 total_stats.1
  132.9 5.0 %all-to-all-start.2 = ((f32[64,16,128]{2,1,0:T(8,128)}), f32[64,16,128]{2,1,0:T(8,128)S(1)}, u32[]{:S(2)}, u32[]{:S(2)}) async-start(f32[64,16,128]{2,1,0:T(8,128)} %total_stats.1), calls=%async_computation.2 | async-start | bytes 1048576 | tf_op jit(solution)/shard_map/all_to_all | solution.py:64
  137.9 7.4 %collective-permute-start.2 = (s32[24,128]{1,0:T(8,128)S(1)}, s32[24,128]{1,0:T(8,128)S(1)}, u32[]{:S(2)}, u32[]{:S(2)}) collective-permute-start(s32[24,128]{1,0:T(8,128)S(1)} %slice.19), channel_id=1, source_target_pairs={{0,126},{1,3},{2,0},{3,5},{4,2},{5,7},{6,4},{7,9},{8,6},{9,11},{10... | collective-permute-start | bytes 36872 | tf_op jit(solution)/shard_map/ppermute | solution.py:44
  145.3 5.1 %prepare_outputs.1 = (bf16[1536,1536]{1,0:T(8,128)(2,1)}, f32[512,128]{1,0:T(8,128)}) custom-call(s32[128,128]{1,0:T(8,128)} %pad.9.table_ref, f32[512,128]{1,0:T(8,128)} %bitcast.29, bf16[512,512]{1,0:T(8,128)(2,1)} %get-tuple-element.29.first_ref, bf16[512,512]{1,0:T(8,128)(2,1)} %get-tuple-element.30.second_ref), custom_call_target="tpu_custom_call" | custom-call | flops 2000000000 | bytes 10000000 | tf_op jit(solution)/shard_map/prepare_outputs/pallas_call | solution.py:507
  150.4 1.9 all-to-all-done.2.stats_ref
  152.3 0.8 copy-done.4
  153.2 15.1 %backward.1 = bf16[1536,1536]{1,0:T(8,128)(2,1)} custom-call(s32[128,128]{1,0:T(8,128)} %pad.9.table_ref, s32[24,128]{1,0:T(8,128)} %copy-done.8, f32[64,16,128]{2,1,0:T(8,128)} %copy-done.4, bf16[512,512]{1,0:T(8,128)(2,1)} %get-tuple-element.23.query_ref.head_query_ref, ...), custom_call_target="tpu_custom_call", output_to_operand_aliasing={{}: (11, {})} | custom-call | flops 8000000000 | bytes 15000000 | tf_op jit(solution)/shard_map/backward/pallas_call | solution.py:719
  168.3 63.2 %all_to_all.20 = bf16[64,24,1536]{2,1,0:T(8,128)(2,1)S(1)} all-to-all(bf16[64,24,1536]{2,1,0:T(8,128)(2,1)} %bitcast.31), channel_id=1, replica_groups=mesh['seq'=64,'head'=2] {'seq'}, dimensions={0} | all-to-all | bytes 9437184 | tf_op jit(solution)/shard_map/all_to_all | solution.py:64
  231.5 4.3 %combine_rows.1 = (bf16[512,512]{1,0:T(8,128)(2,1)}, bf16[512,512]{1,0:T(8,128)(2,1)}, bf16[512,512]{1,0:T(8,128)(2,1)}) custom-call(s32[128,128]{1,0:T(8,128)S(1)} %copy-done.2, f32[512,128]{1,0:T(8,128)S(1)} %copy-done.3, bf16[1536,1536]{1,0:T(8,128)(2,1)S(1)} %bitcast.27), custom_call_target="tpu_custom_call" | custom-call | flops 2415919104 | bytes 6291456 | tf_op jit(solution)/shard_map/combine_rows/pallas_call | solution.py:799
  (64 shorter events, 5.5 us)
Async XLA Ops:
  1.4 8.2 %collective-permute-start = (s32[2,576]{1,0:T(2,128)S(1)}, s32[2,576]{1,0:T(2,128)S(1)}, u32[]{:S(2)}, u32[]{:S(2)}) collective-permute-start(s32[2,576]{1,0:T(2,128)S(1)} %pad_add_fusion), channel_id=1, source_target_pairs={{0,0},{1,127},{2,2},{3,125},{4,4},{5,123},{6,6},{7,121},{8,8},{9,1... | collective-permute-start | bytes 13832 | tf_op jit(solution)/shard_map/ppermute | solution.py:44
  9.6 68.1 %all-to-all-start = ((bf16[64,24,1536]{2,1,0:T(8,128)(2,1)}), bf16[64,24,1536]{2,1,0:T(8,128)(2,1)}, u32[]{:S(2)}, u32[]{:S(2)}) async-start(bf16[64,24,1536]{2,1,0:T(8,128)(2,1)} %bitcast.30), calls=%async_computation | async-start | bytes 9437184 | tf_op jit(solution)/shard_map/all_to_all | solution.py:64
  83.1 20.7 %collective-permute-start.1 = (bf16[512,1024]{1,0:T(8,128)(2,1)}, bf16[512,1024]{1,0:T(8,128)(2,1)S(1)}, u32[]{:S(2)}, u32[]{:S(2)}) collective-permute-start(bf16[512,1024]{1,0:T(8,128)(2,1)} %sort_tail.1.tail_query_ref.tail_value_ref.tail_ref), channel_id=1, source_target_pairs={{0,2},{1,127},{2,4},{3,1},{4,6},{5,3},{6,8},{7,5},{8,10},{9,7},{10... | collective-permute-start | bytes 3145736 | tf_op jit(solution)/shard_map/ppermute | solution.py:44
  96.8 34.0 %copy-start.1 = (s32[128,128]{1,0:T(8,128)S(1)}, s32[128,128]{1,0:T(8,128)}, u32[]{:S(2)}) copy-start(s32[128,128]{1,0:T(8,128)} %pad.9.table_ref) | copy-start | bytes 196612
  103.8 1.0 copy-start.5
  112.4 18.4 %all-to-all-start.1 = ((f32[64,8,128]{2,1,0:T(8,128)}), f32[64,8,128]{2,1,0:T(8,128)S(1)}, u32[]{:S(2)}, u32[]{:S(2)}) async-start(f32[64,8,128]{2,1,0:T(8,128)} %bitcast.32), calls=%async_computation.1 | async-start | bytes 524288 | tf_op jit(solution)/shard_map/all_to_all | solution.py:64
  120.0 30.3 %collective-permute-start.3 = (bf16[512,512]{1,0:T(8,128)(2,1)}, bf16[512,512]{1,0:T(8,128)(2,1)S(1)}, u32[]{:S(2)}, u32[]{:S(2)}) collective-permute-start(bf16[512,512]{1,0:T(8,128)(2,1)} %get-tuple-element.23.query_ref.head_query_ref), channel_id=1, source_target_pairs={{0,126},{1,3},{2,0},{3,5},{4,2},{5,7},{6,4},{7,9},{8,6},{9,11},{10... | collective-permute-start | bytes 1572872 | tf_op jit(solution)/shard_map/ppermute | solution.py:44
  127.4 23.0 %collective-permute-start.4 = (bf16[512,512]{1,0:T(8,128)(2,1)}, bf16[512,512]{1,0:T(8,128)(2,1)S(1)}, u32[]{:S(2)}, u32[]{:S(2)}) collective-permute-start(bf16[512,512]{1,0:T(8,128)(2,1)} %get-tuple-element.25.cotangent_ref.head_cotangent_ref), channel_id=1, source_target_pairs={{0,126},{1,3},{2,0},{3,5},{4,2},{5,7},{6,4},{7,9},{8,6},{9,11},{10... | collective-permute-start | bytes 1572872 | tf_op jit(solution)/shard_map/ppermute | solution.py:44
  130.8 14.5 %copy-start = (f32[64,8,128]{2,1,0:T(8,128)}, f32[64,8,128]{2,1,0:T(8,128)S(1)}, u32[]{:S(2)}) copy-start(f32[64,8,128]{2,1,0:T(8,128)S(1)} %all-to-all-done.1) | copy-start | bytes 786436
  132.9 19.4 %all-to-all-start.2 = ((f32[64,16,128]{2,1,0:T(8,128)}), f32[64,16,128]{2,1,0:T(8,128)S(1)}, u32[]{:S(2)}, u32[]{:S(2)}) async-start(f32[64,16,128]{2,1,0:T(8,128)} %total_stats.1), calls=%async_computation.2 | async-start | bytes 1048576 | tf_op jit(solution)/shard_map/all_to_all | solution.py:64
  137.9 12.5 %collective-permute-start.2 = (s32[24,128]{1,0:T(8,128)S(1)}, s32[24,128]{1,0:T(8,128)S(1)}, u32[]{:S(2)}, u32[]{:S(2)}) collective-permute-start(s32[24,128]{1,0:T(8,128)S(1)} %slice.19), channel_id=1, source_target_pairs={{0,126},{1,3},{2,0},{3,5},{4,2},{5,7},{6,4},{7,9},{8,6},{9,11},{10... | collective-permute-start | bytes 36872 | tf_op jit(solution)/shard_map/ppermute | solution.py:44
  150.3 2.0 copy-start.6
  150.4 1.9 copy-start.7
  150.4 1.9 copy-start.8
  152.3 0.9 copy-start.4
  168.3 63.2 %copy-start.2 = (s32[128,128]{1,0:T(8,128)S(1)}, s32[128,128]{1,0:T(8,128)}, u32[]{:S(2)}) copy-start(s32[128,128]{1,0:T(8,128)} %pad.9.table_ref) | copy-start | bytes 196612
  168.3 63.2 %copy-start.3 = (f32[512,128]{1,0:T(8,128)S(1)}, f32[512,128]{1,0:T(8,128)}, u32[]{:S(2)}) copy-start(f32[512,128]{1,0:T(8,128)} %get-tuple-element.31.share_ref) | copy-start | bytes 786436

commit v8 on v7

--- a/solution.py
+++ b/solution.py
@@ -530,14 +530,19 @@
 def backward_tile(query, upstream, keys, values, masked, total_row, delta_row):
     scores = dot(keys, query, 1, 1)
     if masked is not None:
-        low, high = scores[GROUP : GROUP + LANES], scores[GROUP + LANES :]
+        low, high = scores[:LANES], scores[LANES:]
         low = jnp.concatenate(
             [jnp.where(masked, NEG_SELF, low[:, :LANES]), low[:, LANES:]], axis=1
         )
         high = jnp.concatenate(
-            [high[:, :LANES], jnp.where(masked, NEG_SELF, high[:, LANES:])], axis=1
-        )
-        scores = jnp.concatenate([scores[:GROUP], low, high])
+            [
+                high[:, :LANES],
+                jnp.where(masked, NEG_SELF, high[:, LANES : 2 * LANES]),
+                high[:, 2 * LANES :],
+            ],
+            axis=1,
+        )
+        scores = jnp.concatenate([low, high])
     probs = jnp.exp(scores - total_row)
     dots = dot(values, upstream, 1, 1)
     slopes = (probs * (dots - delta_row)).astype(jnp.bfloat16)
@@ -561,51 +566,49 @@
         units, inverse = unit_rows(raw)
         keys = units.astype(jnp.bfloat16)
         prior_keys = unit_rows(prior[kept, columns])[0].astype(jnp.bfloat16)
-        keys_first = jnp.concatenate([prior_keys, keys[:GROUP]])
-        values_first = jnp.concatenate([prior[kept, values_at], values[:GROUP]])
-        probs, slopes = backward_tile(
+        _, prior_slopes = backward_tile(
             raw[:GROUP],
             upstream[:GROUP],
-            keys_first,
-            values_first,
-            own,
+            prior_keys,
+            prior[kept, values_at],
+            None,
             total_row[:, :GROUP],
             delta_row[:, :GROUP],
         )
-        query_first = dot(keys_first, slopes, 0, 0).T
-        unit_first = dot(slopes[GROUP:], raw[:GROUP])
-        value_first = dot(probs[GROUP:], upstream[:GROUP])
-
-        probs, slopes = backward_tile(
-            raw[GROUP:],
-            upstream[GROUP:],
-            keys,
-            values,
-            own,
-            total_row[:, GROUP:],
-            delta_row[:, GROUP:],
-        )
-        query_second = dot(keys, slopes, 0, 0).T
-        unit_both = dot(slopes, raw[GROUP:])
-        value_both = dot(probs, upstream[GROUP:])
-
-        next_query = nexts[0][kept, columns]
-        next_upstream = nexts[1][kept, columns]
-        probs, slopes = backward_tile(
-            next_query,
-            next_upstream,
+        first_probs, first_slopes = backward_tile(
+            raw, upstream, keys[:GROUP], values[:GROUP], own, total_row, delta_row
+        )
+        second_raw = jnp.concatenate([raw[GROUP:], nexts[0][kept, columns]])
+        second_upstream = jnp.concatenate([upstream[GROUP:], nexts[1][kept, columns]])
+        second_probs, second_slopes = backward_tile(
+            second_raw,
+            second_upstream,
             keys[GROUP:],
             values[GROUP:],
-            None,
-            edge_total,
-            edge_delta,
-        )
-        unit_last = dot(slopes, next_query)
-        value_last = dot(probs, next_upstream)
-
-        query_slope = jnp.concatenate([query_first, query_second])
-        unit_slope = unit_both + jnp.concatenate([unit_first, unit_last])
-        value_slope = value_both + jnp.concatenate([value_first, value_last])
+            own,
+            jnp.concatenate([total_row[:, GROUP:], edge_total], axis=1),
+            jnp.concatenate([delta_row[:, GROUP:], edge_delta], axis=1),
+        )
+        query_slope = jnp.concatenate(
+            [
+                dot(
+                    jnp.concatenate([prior_keys, keys[:GROUP]]),
+                    jnp.concatenate([prior_slopes, first_slopes[:, :GROUP]]),
+                    0,
+                    0,
+                ).T,
+                dot(
+                    keys,
+                    jnp.concatenate([first_slopes[:, GROUP:], second_slopes[:, :GROUP]]),
+                    0,
+                    0,
+                ).T,
+            ]
+        )
+        unit_slope = jnp.concatenate([dot(first_slopes, raw), dot(second_slopes, second_raw)])
+        value_slope = jnp.concatenate(
+            [dot(first_probs, upstream), dot(second_probs, second_upstream)]
+        )
         key_slope = inverse * (
             unit_slope - units * jnp.sum(units * unit_slope, -1, keepdims=True)
         )
@@ -847,7 +850,6 @@
         return by_owner(codes)
 
     tables = to_place(jnp.concatenate([arrival_count, receive_slot], axis=1))
-    packed, tables = lax.optimization_barrier((packed, tables))
     arrival = arrivals(tables[:, :owners])
     place = tables[:, owners:] + code
 

time: 237 us -> 228 us (0.962)
  blocking collectives: 63.2 us -> 57.9 us
  starting transfers between devices: 42.4 us -> 39.1 us
    all_to_all x1, blocking collectives: 63.2 us -> 57.9 us  [exchange(): return lax.all_to_all(block, 'seq', split_axis=0, concat_axis=0, tiled=True)]
  transfers between devices with their start and end apart: 8 -> 8, of which waited for: 4 -> 3; matrix products, arithmetic and copies ran while one was open for 2% -> 2% of each run, Pallas kernels for 10% -> 8%
where the time goes in v8:
time: 228 us; the launch traced here: 227 us
  waiting for transfers between devices  66.2 us (29%)
  blocking collectives  57.9 us (25%)
  Pallas kernels  54.4 us (24%)
  starting transfers between devices  39.1 us (17%)
  local copies, waits for them, and re-layouts  7.18 us (3%)
    all_to_all x1, blocking collectives, exchange(): return lax.all_to_all(block, 'seq', split_axis=0, concat_axis=0, tiled=True)  57.9 us
    all_to_all x3, waiting for transfers between devices, exchange(): return lax.all_to_all(block, 'seq', split_axis=0, concat_axis=0, tiled=True)  57.8 us
    all_to_all x3, starting transfers between devices, exchange(): return lax.all_to_all(block, 'seq', split_axis=0, concat_axis=0, tiled=True)  22.3 us
    ppermute x5, starting transfers between devices, routed(): return lax.ppermute(block, ('seq', 'head'), route)  16.8 us
    pallas_call x1, Pallas kernels, backward(): pl.pallas_call(backward_body, in_specs=[table_spec(), pl.BlockSpec(next_t...  12.8 us
    pallas_call x1, Pallas kernels, forward_own(): pl.pallas_call(own_body, grid=(2, 2), in_specs=[pl.BlockSpec((LANES, LANE...  11.2 us
    ppermute x5, waiting for transfers between devices, routed(): return lax.ppermute(block, ('seq', 'head'), route)  8.45 us
    pallas_call x1, Pallas kernels, forward_edge(): pl.pallas_call(edge_body, in_specs=[table_spec()] + anywhere(5), out_spec...  7.64 us
  transfers between devices with their start and end apart: 8, of which 3 were waited for; matrix products, arithmetic and copies ran while one was open for 2% of the time, Pallas kernels for 8%

profile of v8, /device:TPU:0, one launch (start us, length us, event | category | flops | bytes accessed | tf_op | source)
XLA Modules:
  0.0 226.7 jit_solution(10276387133479477659)
XLA Ops:
  0.6 0.8 reshape.73
  2.3 5.9 %pack_rows.1 = bf16[1536,1536]{1,0:T(8,128)(2,1)} custom-call(s32[16,128]{1,0:T(8,128)} %pad.8.index_ref, bf16[512,512]{1,0:T(8,128)(2,1)} %refs_0_.1, bf16[512,512]{1,0:T(8,128)(2,1)} %refs_1_.1, bf16[512,512]{1,0:T(8,128)(2,1)} %refs_2_.1), custom_call_target="tpu_custom_call" | custom-call | flops 2415919104 | bytes 6291456 | tf_op jit(solution)/shard_map/pack_rows/pallas_call | solution.py:158
  8.2 11.7 %all-to-all-start = ((bf16[64,24,1536]{2,1,0:T(8,128)(2,1)}), bf16[64,24,1536]{2,1,0:T(8,128)(2,1)}, u32[]{:S(2)}, u32[]{:S(2)}) async-start(bf16[64,24,1536]{2,1,0:T(8,128)(2,1)} %bitcast.30), calls=%async_computation | async-start | bytes 9437184 | tf_op jit(solution)/shard_map/all_to_all | solution.py:64
  20.1 0.7 collective-permute-start
  23.5 0.6 pad.9.table_ref
  24.1 54.5 %all-to-all-done = bf16[64,24,1536]{2,1,0:T(8,128)(2,1)} async-done(((bf16[64,24,1536]{2,1,0:T(8,128)(2,1)}), bf16[64,24,1536]{2,1,0:T(8,128)(2,1)}, u32[]{:S(2)}, u32[]{:S(2)}) %all-to-all-start) | async-done | bytes 4718624 | tf_op jit(solution)/shard_map/all_to_all | solution.py:64
  78.6 5.4 %sort_tail.1.tail_query_ref.tail_value_ref.tail_ref = bf16[512,1024]{1,0:T(8,128)(2,1)} custom-call(s32[128,128]{1,0:T(8,128)} %pad.9.table_ref, bf16[1536,1536]{1,0:T(8,128)(2,1)} %bitcast.2.arrived_ref.arrived_query_ref.arrived_value_ref.arrived_cotangent_ref), custom_call_target="tpu_custom_call" | custom-call | flops 1610612736 | bytes 4194304 | tf_op jit(solution)/shard_map/sort_tail/pallas_call | solution.py:205
  84.4 0.7 slice.19
  85.1 11.2 %forward_own.1 = (bf16[512,512]{1,0:T(8,128)(2,1)}, bf16[512,512]{1,0:T(8,128)(2,1)}, bf16[512,512]{1,0:T(8,128)(2,1)}, bf16[512,512]{1,0:T(8,128)(2,1)}, bf16[512,512]{1,0:T(8,128)(2,1)}, /*index=5*/f32[512,256]{1,0:T(8,128)}) custom-call(s32[128,128]{1,0:T(8,128)} %pad.9.table_ref, ...), custom_call_target="tpu_custom_call" | custom-call | flops 5000000000 | bytes 10000000 | tf_op jit(solution)/shard_map/forward_own/pallas_call | solution.py:304
  96.3 8.4 %collective-permute-done.1.prior_ref = bf16[512,1024]{1,0:T(8,128)(2,1)S(1)} collective-permute-done((bf16[512,1024]{1,0:T(8,128)(2,1)}, bf16[512,1024]{1,0:T(8,128)(2,1)S(1)}, u32[]{:S(2)}, u32[]{:S(2)}) %collective-permute-start.1) | collective-permute-done | bytes 1048608 | tf_op jit(solution)/shard_map/ppermute | solution.py:44
  104.7 1.0 copy-done.7
  105.7 7.6 %forward_edge.1 = (bf16[512,512]{1,0:T(8,128)(2,1)}, f32[512,128]{1,0:T(8,128)}) custom-call(s32[128,128]{1,0:T(8,128)} %pad.9.table_ref, bf16[512,512]{1,0:T(8,128)(2,1)} %get-tuple-element.19.query_ref.head_query_ref, bf16[512,512]{1,0:T(8,128)(2,1)} %get-tuple-element.20.value_ref.head_value_ref, ...), custom_call_target="tpu_custom_call" | custom-call | flops 2000000000 | bytes 4000000 | tf_op jit(solution)/shard_map/forward_edge/pallas_call | solution.py:404
  113.3 5.9 %all-to-all-start.1 = ((f32[64,8,128]{2,1,0:T(8,128)}), f32[64,8,128]{2,1,0:T(8,128)S(1)}, u32[]{:S(2)}, u32[]{:S(2)}) async-start(f32[64,8,128]{2,1,0:T(8,128)} %bitcast.32), calls=%async_computation.1 | async-start | bytes 524288 | tf_op jit(solution)/shard_map/all_to_all | solution.py:64
  119.2 7.4 %collective-permute-start.3 = (bf16[512,512]{1,0:T(8,128)(2,1)}, bf16[512,512]{1,0:T(8,128)(2,1)S(1)}, u32[]{:S(2)}, u32[]{:S(2)}) collective-permute-start(bf16[512,512]{1,0:T(8,128)(2,1)} %get-tuple-element.19.query_ref.head_query_ref), channel_id=1, source_target_pairs={{0,126},{1,3},{2,0},{3,5},{4,2},{5,7},{6,4},{7,9},{8,6},{9,11},{10... | collective-permute-start | bytes 1572872 | tf_op jit(solution)/shard_map/ppermute | solution.py:44
  126.6 0.9 collective-permute-start.4
  127.5 3.3 %all-to-all-done.1 = f32[64,8,128]{2,1,0:T(8,128)S(1)} async-done(((f32[64,8,128]{2,1,0:T(8,128)}), f32[64,8,128]{2,1,0:T(8,128)S(1)}, u32[]{:S(2)}, u32[]{:S(2)}) %all-to-all-start.1) | async-done | bytes 262176 | tf_op jit(solution)/shard_map/all_to_all | solution.py:64
  130.8 2.1 total_stats.1
  132.9 4.6 %all-to-all-start.2 = ((f32[64,16,128]{2,1,0:T(8,128)}), f32[64,16,128]{2,1,0:T(8,128)S(1)}, u32[]{:S(2)}, u32[]{:S(2)}) async-start(f32[64,16,128]{2,1,0:T(8,128)} %total_stats.1), calls=%async_computation.2 | async-start | bytes 1048576 | tf_op jit(solution)/shard_map/all_to_all | solution.py:64
  137.5 7.6 %collective-permute-start.2 = (s32[24,128]{1,0:T(8,128)S(1)}, s32[24,128]{1,0:T(8,128)S(1)}, u32[]{:S(2)}, u32[]{:S(2)}) collective-permute-start(s32[24,128]{1,0:T(8,128)S(1)} %slice.19), channel_id=1, source_target_pairs={{0,126},{1,3},{2,0},{3,5},{4,2},{5,7},{6,4},{7,9},{8,6},{9,11},{10... | collective-permute-start | bytes 36872 | tf_op jit(solution)/shard_map/ppermute | solution.py:44
  145.1 5.1 %prepare_outputs.1 = (bf16[1536,1536]{1,0:T(8,128)(2,1)}, f32[512,128]{1,0:T(8,128)}) custom-call(s32[128,128]{1,0:T(8,128)} %pad.9.table_ref, f32[512,128]{1,0:T(8,128)} %bitcast.29, bf16[512,512]{1,0:T(8,128)(2,1)} %get-tuple-element.25.first_ref, bf16[512,512]{1,0:T(8,128)(2,1)} %get-tuple-element.26.second_ref), custom_call_target="tpu_custom_call" | custom-call | flops 2000000000 | bytes 10000000 | tf_op jit(solution)/shard_map/prepare_outputs/pallas_call | solution.py:507
  150.3 0.7 copy-done.8
  151.5 12.8 %backward.1 = bf16[1536,1536]{1,0:T(8,128)(2,1)} custom-call(s32[128,128]{1,0:T(8,128)} %pad.9.table_ref, s32[24,128]{1,0:T(8,128)} %copy-done.10, f32[64,16,128]{2,1,0:T(8,128)} %copy-done.4, bf16[512,512]{1,0:T(8,128)(2,1)} %get-tuple-element.19.query_ref.head_query_ref, ...), custom_call_target="tpu_custom_call", output_to_operand_aliasing={{}: (11, {})} | custom-call | flops 8000000000 | bytes 15000000 | tf_op jit(solution)/shard_map/backward/pallas_call | solution.py:722
  164.4 57.9 %all_to_all.20 = bf16[64,24,1536]{2,1,0:T(8,128)(2,1)S(1)} all-to-all(bf16[64,24,1536]{2,1,0:T(8,128)(2,1)} %bitcast.31), channel_id=1, replica_groups=mesh['seq'=64,'head'=2] {'seq'}, dimensions={0} | all-to-all | bytes 9437184 | tf_op jit(solution)/shard_map/all_to_all | solution.py:64
  222.3 4.3 %combine_rows.1 = (bf16[512,512]{1,0:T(8,128)(2,1)}, bf16[512,512]{1,0:T(8,128)(2,1)}, bf16[512,512]{1,0:T(8,128)(2,1)}) custom-call(s32[128,128]{1,0:T(8,128)S(1)} %copy-done.2, f32[512,128]{1,0:T(8,128)S(1)} %copy-done.3, bf16[1536,1536]{1,0:T(8,128)(2,1)S(1)} %bitcast.27), custom_call_target="tpu_custom_call" | custom-call | flops 2415919104 | bytes 6291456 | tf_op jit(solution)/shard_map/combine_rows/pallas_call | solution.py:802
  (68 shorter events, 4.4 us)
Async XLA Ops:
  8.2 11.8 %copy-start.5 = (s32[2,512]{1,0:T(2,128)S(1)}, s32[2,512]{1,0:T(2,128)}, u32[]{:S(2)}) copy-start(s32[2,512]{1,0:T(2,128)} %param.11) | copy-start | bytes 12292
  8.2 11.8 %copy-start.6 = (s32[2,64]{1,0:T(2,128)S(1)}, s32[2,64]{1,0:T(2,128)}, u32[]{:S(2)}) copy-start(s32[2,64]{1,0:T(2,128)} %param.10) | copy-start | bytes 1540
  8.2 70.4 %all-to-all-start = ((bf16[64,24,1536]{2,1,0:T(8,128)(2,1)}), bf16[64,24,1536]{2,1,0:T(8,128)(2,1)}, u32[]{:S(2)}, u32[]{:S(2)}) async-start(bf16[64,24,1536]{2,1,0:T(8,128)(2,1)} %bitcast.30), calls=%async_computation | async-start | bytes 9437184 | tf_op jit(solution)/shard_map/all_to_all | solution.py:64
  20.1 1.3 collective-permute-start
  84.0 20.7 %collective-permute-start.1 = (bf16[512,1024]{1,0:T(8,128)(2,1)}, bf16[512,1024]{1,0:T(8,128)(2,1)S(1)}, u32[]{:S(2)}, u32[]{:S(2)}) collective-permute-start(bf16[512,1024]{1,0:T(8,128)(2,1)} %sort_tail.1.tail_query_ref.tail_value_ref.tail_ref), channel_id=1, source_target_pairs={{0,2},{1,127},{2,4},{3,1},{4,6},{5,3},{6,8},{7,5},{8,10},{9,7},{10... | collective-permute-start | bytes 3145736 | tf_op jit(solution)/shard_map/ppermute | solution.py:44
  96.2 34.5 %copy-start.1 = (s32[128,128]{1,0:T(8,128)S(1)}, s32[128,128]{1,0:T(8,128)}, u32[]{:S(2)}) copy-start(s32[128,128]{1,0:T(8,128)} %pad.9.table_ref) | copy-start | bytes 196612
  104.7 1.0 copy-start.7
  113.3 17.4 %all-to-all-start.1 = ((f32[64,8,128]{2,1,0:T(8,128)}), f32[64,8,128]{2,1,0:T(8,128)S(1)}, u32[]{:S(2)}, u32[]{:S(2)}) async-start(f32[64,8,128]{2,1,0:T(8,128)} %bitcast.32), calls=%async_computation.1 | async-start | bytes 524288 | tf_op jit(solution)/shard_map/all_to_all | solution.py:64
  119.2 31.0 %collective-permute-start.3 = (bf16[512,512]{1,0:T(8,128)(2,1)}, bf16[512,512]{1,0:T(8,128)(2,1)S(1)}, u32[]{:S(2)}, u32[]{:S(2)}) collective-permute-start(bf16[512,512]{1,0:T(8,128)(2,1)} %get-tuple-element.19.query_ref.head_query_ref), channel_id=1, source_target_pairs={{0,126},{1,3},{2,0},{3,5},{4,2},{5,7},{6,4},{7,9},{8,6},{9,11},{10... | collective-permute-start | bytes 1572872 | tf_op jit(solution)/shard_map/ppermute | solution.py:44
  126.6 23.7 %collective-permute-start.4 = (bf16[512,512]{1,0:T(8,128)(2,1)}, bf16[512,512]{1,0:T(8,128)(2,1)S(1)}, u32[]{:S(2)}, u32[]{:S(2)}) collective-permute-start(bf16[512,512]{1,0:T(8,128)(2,1)} %get-tuple-element.21.cotangent_ref.head_cotangent_ref), channel_id=1, source_target_pairs={{0,126},{1,3},{2,0},{3,5},{4,2},{5,7},{6,4},{7,9},{8,6},{9,11},{10... | collective-permute-start | bytes 1572872 | tf_op jit(solution)/shard_map/ppermute | solution.py:44
  130.8 14.4 %copy-start = (f32[64,8,128]{2,1,0:T(8,128)}, f32[64,8,128]{2,1,0:T(8,128)S(1)}, u32[]{:S(2)}) copy-start(f32[64,8,128]{2,1,0:T(8,128)S(1)} %all-to-all-done.1) | copy-start | bytes 786436
  132.9 17.4 %all-to-all-start.2 = ((f32[64,16,128]{2,1,0:T(8,128)}), f32[64,16,128]{2,1,0:T(8,128)S(1)}, u32[]{:S(2)}, u32[]{:S(2)}) async-start(f32[64,16,128]{2,1,0:T(8,128)} %total_stats.1), calls=%async_computation.2 | async-start | bytes 1048576 | tf_op jit(solution)/shard_map/all_to_all | solution.py:64
  137.5 12.8 %collective-permute-start.2 = (s32[24,128]{1,0:T(8,128)S(1)}, s32[24,128]{1,0:T(8,128)S(1)}, u32[]{:S(2)}, u32[]{:S(2)}) collective-permute-start(s32[24,128]{1,0:T(8,128)S(1)} %slice.19), channel_id=1, source_target_pairs={{0,126},{1,3},{2,0},{3,5},{4,2},{5,7},{6,4},{7,9},{8,6},{9,11},{10... | collective-permute-start | bytes 36872 | tf_op jit(solution)/shard_map/ppermute | solution.py:44
  150.3 0.8 copy-start.8
  150.3 1.1 copy-start.9
  150.3 1.0 copy-start.10
  150.3 1.2 copy-start.4
  164.3 57.9 %copy-start.2 = (s32[128,128]{1,0:T(8,128)S(1)}, s32[128,128]{1,0:T(8,128)}, u32[]{:S(2)}) copy-start(s32[128,128]{1,0:T(8,128)} %pad.9.table_ref) | copy-start | bytes 196612
  164.3 57.9 %copy-start.3 = (f32[512,128]{1,0:T(8,128)S(1)}, f32[512,128]{1,0:T(8,128)}, u32[]{:S(2)}) copy-start(f32[512,128]{1,0:T(8,128)} %get-tuple-element.27.share_ref) | copy-start | bytes 786436

commit v9 on v8

--- a/solution.py
+++ b/solution.py
@@ -126,7 +126,8 @@
     sources, out_ref, held, staged, chosen, load, store = refs[:3], *refs[3:]
     tokens, width = sources[0].shape
     arriving = started(sources, [held.at[i] for i in range(3)], load)
-    turned = index_ref[...].T
+    spare = jnp.zeros((LANES - SLOT_ROWS, LANES), jnp.int32)
+    turned = jnp.concatenate([index_ref[...], spare]).T
     chosen[...] = match_cols(
         [turned[:, i : i + 1] for i in range(SLOT_ROWS)], iota((LANES, tokens), 1)
     )
@@ -645,7 +646,6 @@
     rows = PLACE_ROWS * LANES
     per_round = rows // 2
     sources = [
-        stats_ref,
         head_query_ref,
         head_value_ref,
         head_cotangent_ref,
@@ -655,8 +655,19 @@
         tail_ref,
         prior_ref,
     ]
-    targets = [stats] + [six.at[i] for i in range(6)] + [double.at[i] for i in range(2)]
-    arriving = started(sources, targets, load)
+    targets = [six.at[i] for i in range(6)] + [double.at[i] for i in range(2)]
+    (stats_copy,) = started([stats_ref], [stats], load)
+    arriving = []
+    for each in range(2):
+        at = pl.ds(each * GROUP, GROUP)
+        arriving.append(
+            started(
+                [source.at[at] for source in sources],
+                [target.at[at] for target in targets],
+                load,
+                1 + each * len(sources),
+            )
+        )
     place_row = table_row(table_ref, PLACE, PLACE_ROWS)
     next_places = table_row(next_table_ref, PLACE, PLACE_ROWS)
     next_row = jnp.concatenate(
@@ -669,13 +680,11 @@
         )
         for each in range(2)
     ]
-    arriving[0].wait()
+    stats_copy.wait()
     own_stats = stats[:, :STAT, :].reshape(-1, LANES)
     next_stats = stats[:, STAT:, :].reshape(-1, LANES)
     found = gather_stats(place_row, table_cols(table_ref, ARRIVAL3, SLOT_ROWS), own_stats)
     edge = gather_stats(next_row, table_cols(next_table_ref, ARRIVAL3, SLOT_ROWS), next_stats)
-    for copy in arriving[1:]:
-        copy.wait()
     refs = (
         (six.at[0], six.at[1], six.at[2]),
         double.at[0],
@@ -687,6 +696,9 @@
     width = shaped.shape[2]
     for pair in range(2):
         for hash_round in range(2):
+            if pair == 0:
+                for copy in arriving[hash_round]:
+                    copy.wait()
             backward_heads(
                 pair,
                 found[:, hash_round * per_round : (hash_round + 1) * per_round],
@@ -731,7 +743,7 @@
             pltpu.VMEM((2, rows, 2 * width), jnp.bfloat16),
             pltpu.VMEM((2, 2 * GROUP, width), jnp.bfloat16),
             pltpu.VMEM((2, slots, width), jnp.bfloat16),
-            pltpu.SemaphoreType.DMA((9,)),
+            pltpu.SemaphoreType.DMA((17,)),
             pltpu.SemaphoreType.DMA((4,)),
         ],
         compiler_params=params(57),
@@ -839,7 +851,7 @@
     blocks = send_rows.reshape(rounds, owners, capacity)
     send_rows = jnp.where(half == 0, blocks, blocks[:, ::-1]).reshape(rounds, -1)
     send = by_owner(send_rows)
-    send_blocks = jnp.pad(send.reshape(-1, LANES), ((0, 4), (0, 0)))
+    send_blocks = send.reshape(-1, LANES)
     packed = pack(send_blocks, query_key, value, attended_cotangent)
 
     within = jnp.arange(capacity, dtype=jnp.int32)

time: 228 us -> 227 us (level)
  no operation moved by 1% of the time
where the time goes in v9:
time: 227 us
  waiting for transfers between devices  66.2 us (29%)
  blocking collectives  58 us (26%)
  Pallas kernels  54 us (24%)
  starting transfers between devices  39.2 us (17%)
  local copies, waits for them, and re-layouts  7.19 us (3%)
    all_to_all x1, blocking collectives, exchange(): return lax.all_to_all(block, 'seq', split_axis=0, concat_axis=0, tiled=True)  58 us
    all_to_all x3, waiting for transfers between devices, exchange(): return lax.all_to_all(block, 'seq', split_axis=0, concat_axis=0, tiled=True)  57.8 us
    all_to_all x3, starting transfers between devices, exchange(): return lax.all_to_all(block, 'seq', split_axis=0, concat_axis=0, tiled=True)  22.4 us
    ppermute x5, starting transfers between devices, routed(): return lax.ppermute(block, ('seq', 'head'), route)  16.8 us
    pallas_call x1, Pallas kernels, backward(): pl.pallas_call(backward_body, in_specs=[table_spec(), pl.BlockSpec(next_t...  12.4 us
    pallas_call x1, Pallas kernels, forward_own(): pl.pallas_call(own_body, grid=(2, 2), in_specs=[pl.BlockSpec((LANES, LANE...  11.2 us
    ppermute x5, waiting for transfers between devices, routed(): return lax.ppermute(block, ('seq', 'head'), route)  8.46 us
    pallas_call x1, Pallas kernels, forward_edge(): pl.pallas_call(edge_body, in_specs=[table_spec()] + anywhere(5), out_spec...  7.66 us
  transfers between devices with their start and end apart: 8, of which 3 were waited for; matrix products, arithmetic and copies ran while one was open for 2% of the time, Pallas kernels for 8%

profile of v9, /device:TPU:0, one launch (start us, length us, event | category | flops | bytes accessed | tf_op | source)
XLA Modules:
  0.0 226.6 jit_solution(5706798371694398997)
XLA Ops:
  0.6 0.8 reshape.73
  1.6 0.7 reshape_reshape.12.index_ref
  2.3 5.9 %pack_rows.1 = bf16[1536,1536]{1,0:T(8,128)(2,1)} custom-call(s32[12,128]{1,0:T(8,128)} %reshape_reshape.12.index_ref, bf16[512,512]{1,0:T(8,128)(2,1)} %refs_0_.1, bf16[512,512]{1,0:T(8,128)(2,1)} %refs_1_.1, bf16[512,512]{1,0:T(8,128)(2,1)} %refs_2_.1), custom_call_target="tpu_custom_call" | custom-call | flops 2415919104 | bytes 6291456 | tf_op jit(solution)/shard_map/pack_rows/pallas_call | solution.py:159
  8.2 11.9 %all-to-all-start = ((bf16[64,24,1536]{2,1,0:T(8,128)(2,1)}), bf16[64,24,1536]{2,1,0:T(8,128)(2,1)}, u32[]{:S(2)}, u32[]{:S(2)}) async-start(bf16[64,24,1536]{2,1,0:T(8,128)(2,1)} %bitcast.30), calls=%async_computation | async-start | bytes 9437184 | tf_op jit(solution)/shard_map/all_to_all | solution.py:64
  20.2 0.7 collective-permute-start
  24.3 54.5 %all-to-all-done = bf16[64,24,1536]{2,1,0:T(8,128)(2,1)} async-done(((bf16[64,24,1536]{2,1,0:T(8,128)(2,1)}), bf16[64,24,1536]{2,1,0:T(8,128)(2,1)}, u32[]{:S(2)}, u32[]{:S(2)}) %all-to-all-start) | async-done | bytes 4718624 | tf_op jit(solution)/shard_map/all_to_all | solution.py:64
  78.8 5.4 %sort_tail.1.tail_query_ref.tail_value_ref.tail_ref = bf16[512,1024]{1,0:T(8,128)(2,1)} custom-call(s32[128,128]{1,0:T(8,128)} %pad.4.table_ref, bf16[1536,1536]{1,0:T(8,128)(2,1)} %bitcast.2.arrived_ref.arrived_query_ref.arrived_value_ref.arrived_cotangent_ref), custom_call_target="tpu_custom_call" | custom-call | flops 1610612736 | bytes 4194304 | tf_op jit(solution)/shard_map/sort_tail/pallas_call | solution.py:206
  84.5 0.7 slice.19
  85.2 11.2 %forward_own.1 = (bf16[512,512]{1,0:T(8,128)(2,1)}, bf16[512,512]{1,0:T(8,128)(2,1)}, bf16[512,512]{1,0:T(8,128)(2,1)}, bf16[512,512]{1,0:T(8,128)(2,1)}, bf16[512,512]{1,0:T(8,128)(2,1)}, /*index=5*/f32[512,256]{1,0:T(8,128)}) custom-call(s32[128,128]{1,0:T(8,128)} %pad.4.table_ref, ...), custom_call_target="tpu_custom_call" | custom-call | flops 5000000000 | bytes 10000000 | tf_op jit(solution)/shard_map/forward_own/pallas_call | solution.py:305
  96.4 8.4 %collective-permute-done.1.prior_ref = bf16[512,1024]{1,0:T(8,128)(2,1)S(1)} collective-permute-done((bf16[512,1024]{1,0:T(8,128)(2,1)}, bf16[512,1024]{1,0:T(8,128)(2,1)S(1)}, u32[]{:S(2)}, u32[]{:S(2)}) %collective-permute-start.1) | collective-permute-done | bytes 1048608 | tf_op jit(solution)/shard_map/ppermute | solution.py:44
  104.8 1.0 copy-done.8
  105.8 7.7 %forward_edge.1 = (bf16[512,512]{1,0:T(8,128)(2,1)}, f32[512,128]{1,0:T(8,128)}) custom-call(s32[128,128]{1,0:T(8,128)} %pad.4.table_ref, bf16[512,512]{1,0:T(8,128)(2,1)} %get-tuple-element.19.query_ref.head_query_ref, bf16[512,512]{1,0:T(8,128)(2,1)} %get-tuple-element.20.value_ref.head_value_ref, ...), custom_call_target="tpu_custom_call" | custom-call | flops 2000000000 | bytes 4000000 | tf_op jit(solution)/shard_map/forward_edge/pallas_call | solution.py:405
  113.5 5.9 %all-to-all-start.1 = ((f32[64,8,128]{2,1,0:T(8,128)}), f32[64,8,128]{2,1,0:T(8,128)S(1)}, u32[]{:S(2)}, u32[]{:S(2)}) async-start(f32[64,8,128]{2,1,0:T(8,128)} %bitcast.32), calls=%async_computation.1 | async-start | bytes 524288 | tf_op jit(solution)/shard_map/all_to_all | solution.py:64
  119.4 7.4 %collective-permute-start.3 = (bf16[512,512]{1,0:T(8,128)(2,1)}, bf16[512,512]{1,0:T(8,128)(2,1)S(1)}, u32[]{:S(2)}, u32[]{:S(2)}) collective-permute-start(bf16[512,512]{1,0:T(8,128)(2,1)} %get-tuple-element.19.query_ref.head_query_ref), channel_id=1, source_target_pairs={{0,126},{1,3},{2,0},{3,5},{4,2},{5,7},{6,4},{7,9},{8,6},{9,11},{10... | collective-permute-start | bytes 1572872 | tf_op jit(solution)/shard_map/ppermute | solution.py:44
  126.8 0.9 collective-permute-start.4
  127.6 3.3 %all-to-all-done.1 = f32[64,8,128]{2,1,0:T(8,128)S(1)} async-done(((f32[64,8,128]{2,1,0:T(8,128)}), f32[64,8,128]{2,1,0:T(8,128)S(1)}, u32[]{:S(2)}, u32[]{:S(2)}) %all-to-all-start.1) | async-done | bytes 262176 | tf_op jit(solution)/shard_map/all_to_all | solution.py:64
  130.9 2.1 total_stats.1
  133.0 4.6 %all-to-all-start.2 = ((f32[64,16,128]{2,1,0:T(8,128)}), f32[64,16,128]{2,1,0:T(8,128)S(1)}, u32[]{:S(2)}, u32[]{:S(2)}) async-start(f32[64,16,128]{2,1,0:T(8,128)} %total_stats.1), calls=%async_computation.2 | async-start | bytes 1048576 | tf_op jit(solution)/shard_map/all_to_all | solution.py:64
  137.7 7.6 %collective-permute-start.2 = (s32[24,128]{1,0:T(8,128)S(1)}, s32[24,128]{1,0:T(8,128)S(1)}, u32[]{:S(2)}, u32[]{:S(2)}) collective-permute-start(s32[24,128]{1,0:T(8,128)S(1)} %slice.19), channel_id=1, source_target_pairs={{0,126},{1,3},{2,0},{3,5},{4,2},{5,7},{6,4},{7,9},{8,6},{9,11},{10... | collective-permute-start | bytes 36872 | tf_op jit(solution)/shard_map/ppermute | solution.py:44
  145.3 5.1 %prepare_outputs.1 = (bf16[1536,1536]{1,0:T(8,128)(2,1)}, f32[512,128]{1,0:T(8,128)}) custom-call(s32[128,128]{1,0:T(8,128)} %pad.4.table_ref, f32[512,128]{1,0:T(8,128)} %bitcast.29, bf16[512,512]{1,0:T(8,128)(2,1)} %get-tuple-element.25.first_ref, bf16[512,512]{1,0:T(8,128)(2,1)} %get-tuple-element.26.second_ref), custom_call_target="tpu_custom_call" | custom-call | flops 2000000000 | bytes 10000000 | tf_op jit(solution)/shard_map/prepare_outputs/pallas_call | solution.py:508
  150.4 0.7 copy-done.9
  151.6 12.4 %backward.1 = bf16[1536,1536]{1,0:T(8,128)(2,1)} custom-call(s32[128,128]{1,0:T(8,128)} %pad.4.table_ref, s32[24,128]{1,0:T(8,128)} %copy-done.11, f32[64,16,128]{2,1,0:T(8,128)} %copy-done.4, bf16[512,512]{1,0:T(8,128)(2,1)} %get-tuple-element.19.query_ref.head_query_ref, ...), custom_call_target="tpu_custom_call", output_to_operand_aliasing={{}: (11, {})} | custom-call | flops 8000000000 | bytes 15000000 | tf_op jit(solution)/shard_map/backward/pallas_call | solution.py:734
  164.0 58.0 %all_to_all.20 = bf16[64,24,1536]{2,1,0:T(8,128)(2,1)S(1)} all-to-all(bf16[64,24,1536]{2,1,0:T(8,128)(2,1)} %bitcast.31), channel_id=1, replica_groups=mesh['seq'=64,'head'=2] {'seq'}, dimensions={0} | all-to-all | bytes 9437184 | tf_op jit(solution)/shard_map/all_to_all | solution.py:64
  222.1 4.3 %combine_rows.1 = (bf16[512,512]{1,0:T(8,128)(2,1)}, bf16[512,512]{1,0:T(8,128)(2,1)}, bf16[512,512]{1,0:T(8,128)(2,1)}) custom-call(s32[128,128]{1,0:T(8,128)S(1)} %copy-done.2, f32[512,128]{1,0:T(8,128)S(1)} %copy-done.3, bf16[1536,1536]{1,0:T(8,128)(2,1)S(1)} %bitcast.27), custom_call_target="tpu_custom_call" | custom-call | flops 2415919104 | bytes 6291456 | tf_op jit(solution)/shard_map/combine_rows/pallas_call | solution.py:814
  (69 shorter events, 4.3 us)
Async XLA Ops:
  8.2 11.9 %copy-start.6 = (s32[2,512]{1,0:T(2,128)S(1)}, s32[2,512]{1,0:T(2,128)}, u32[]{:S(2)}) copy-start(s32[2,512]{1,0:T(2,128)} %param.11) | copy-start | bytes 12292
  8.2 11.9 %copy-start.7 = (s32[2,64]{1,0:T(2,128)S(1)}, s32[2,64]{1,0:T(2,128)}, u32[]{:S(2)}) copy-start(s32[2,64]{1,0:T(2,128)} %param.10) | copy-start | bytes 1540
  8.2 14.7 %copy-start.5 = (s32[12,128]{1,0:T(8,128)S(1)}, s32[12,128]{1,0:T(8,128)}, u32[]{:S(2)}) copy-start(s32[12,128]{1,0:T(8,128)} %reshape_reshape.12.index_ref) | copy-start | bytes 18436
  8.2 70.5 %all-to-all-start = ((bf16[64,24,1536]{2,1,0:T(8,128)(2,1)}), bf16[64,24,1536]{2,1,0:T(8,128)(2,1)}, u32[]{:S(2)}, u32[]{:S(2)}) async-start(bf16[64,24,1536]{2,1,0:T(8,128)(2,1)} %bitcast.30), calls=%async_computation | async-start | bytes 9437184 | tf_op jit(solution)/shard_map/all_to_all | solution.py:64
  20.2 1.3 collective-permute-start
  84.2 20.7 %collective-permute-start.1 = (bf16[512,1024]{1,0:T(8,128)(2,1)}, bf16[512,1024]{1,0:T(8,128)(2,1)S(1)}, u32[]{:S(2)}, u32[]{:S(2)}) collective-permute-start(bf16[512,1024]{1,0:T(8,128)(2,1)} %sort_tail.1.tail_query_ref.tail_value_ref.tail_ref), channel_id=1, source_target_pairs={{0,2},{1,127},{2,4},{3,1},{4,6},{5,3},{6,8},{7,5},{8,10},{9,7},{10... | collective-permute-start | bytes 3145736 | tf_op jit(solution)/shard_map/ppermute | solution.py:44
  96.4 34.5 %copy-start.1 = (s32[128,128]{1,0:T(8,128)S(1)}, s32[128,128]{1,0:T(8,128)}, u32[]{:S(2)}) copy-start(s32[128,128]{1,0:T(8,128)} %pad.4.table_ref) | copy-start | bytes 196612
  104.8 1.0 copy-start.8
  113.5 17.4 %all-to-all-start.1 = ((f32[64,8,128]{2,1,0:T(8,128)}), f32[64,8,128]{2,1,0:T(8,128)S(1)}, u32[]{:S(2)}, u32[]{:S(2)}) async-start(f32[64,8,128]{2,1,0:T(8,128)} %bitcast.32), calls=%async_computation.1 | async-start | bytes 524288 | tf_op jit(solution)/shard_map/all_to_all | solution.py:64
  119.4 31.0 %collective-permute-start.3 = (bf16[512,512]{1,0:T(8,128)(2,1)}, bf16[512,512]{1,0:T(8,128)(2,1)S(1)}, u32[]{:S(2)}, u32[]{:S(2)}) collective-permute-start(bf16[512,512]{1,0:T(8,128)(2,1)} %get-tuple-element.19.query_ref.head_query_ref), channel_id=1, source_target_pairs={{0,126},{1,3},{2,0},{3,5},{4,2},{5,7},{6,4},{7,9},{8,6},{9,11},{10... | collective-permute-start | bytes 1572872 | tf_op jit(solution)/shard_map/ppermute | solution.py:44
  126.8 23.6 %collective-permute-start.4 = (bf16[512,512]{1,0:T(8,128)(2,1)}, bf16[512,512]{1,0:T(8,128)(2,1)S(1)}, u32[]{:S(2)}, u32[]{:S(2)}) collective-permute-start(bf16[512,512]{1,0:T(8,128)(2,1)} %get-tuple-element.21.cotangent_ref.head_cotangent_ref), channel_id=1, source_target_pairs={{0,126},{1,3},{2,0},{3,5},{4,2},{5,7},{6,4},{7,9},{8,6},{9,11},{10... | collective-permute-start | bytes 1572872 | tf_op jit(solution)/shard_map/ppermute | solution.py:44
  130.9 14.3 %copy-start = (f32[64,8,128]{2,1,0:T(8,128)}, f32[64,8,128]{2,1,0:T(8,128)S(1)}, u32[]{:S(2)}) copy-start(f32[64,8,128]{2,1,0:T(8,128)S(1)} %all-to-all-done.1) | copy-start | bytes 786436
  133.0 17.4 %all-to-all-start.2 = ((f32[64,16,128]{2,1,0:T(8,128)}), f32[64,16,128]{2,1,0:T(8,128)S(1)}, u32[]{:S(2)}, u32[]{:S(2)}) async-start(f32[64,16,128]{2,1,0:T(8,128)} %total_stats.1), calls=%async_computation.2 | async-start | bytes 1048576 | tf_op jit(solution)/shard_map/all_to_all | solution.py:64
  137.7 12.7 %collective-permute-start.2 = (s32[24,128]{1,0:T(8,128)S(1)}, s32[24,128]{1,0:T(8,128)S(1)}, u32[]{:S(2)}, u32[]{:S(2)}) collective-permute-start(s32[24,128]{1,0:T(8,128)S(1)} %slice.19), channel_id=1, source_target_pairs={{0,126},{1,3},{2,0},{3,5},{4,2},{5,7},{6,4},{7,9},{8,6},{9,11},{10... | collective-permute-start | bytes 36872 | tf_op jit(solution)/shard_map/ppermute | solution.py:44
  150.3 0.8 copy-start.9
  150.4 1.1 copy-start.10
  150.4 1.0 copy-start.11
  150.4 1.2 copy-start.4
  164.0 58.1 %copy-start.2 = (s32[128,128]{1,0:T(8,128)S(1)}, s32[128,128]{1,0:T(8,128)}, u32[]{:S(2)}) copy-start(s32[128,128]{1,0:T(8,128)} %pad.4.table_ref) | copy-start | bytes 196612
  164.0 58.1 %copy-start.3 = (f32[512,128]{1,0:T(8,128)S(1)}, f32[512,128]{1,0:T(8,128)}, u32[]{:S(2)}) copy-start(f32[512,128]{1,0:T(8,128)} %get-tuple-element.27.share_ref) | copy-start | bytes 786436

commit v10 on v9

--- a/solution.py
+++ b/solution.py
@@ -895,9 +895,12 @@
     )
     shared, stats = lax.optimization_barrier((table[:SHARED_ROWS], stats))
     next_table = to_prior(shared)
-    next_query = to_prior(head_query)
-    next_cotangent = to_prior(head_cotangent)
     home_stats = exchange(stats.reshape(owners, STAT, LANES)).reshape(-1, LANES)
+    home_stats, for_query, for_cotangent = lax.optimization_barrier(
+        (home_stats, head_query, head_cotangent)
+    )
+    next_query = to_prior(for_query)
+    next_cotangent = to_prior(for_cotangent)
     totals = exchange(total_stats(table, home_stats, tokens))
     payload, shares = prepare(table, home_stats, (out_first, out_second), tokens)
     payload = backward(

time: 227 us -> 237 us (1.044)
  blocking collectives: 58 us -> 82.3 us
  starting transfers between devices: 39.2 us -> 28.2 us
  waiting for transfers between devices: 66.2 us -> 63 us
    all_to_all x1 -> x2, blocking collectives: 58 us -> 82.3 us  [exchange(): return lax.all_to_all(block, 'seq', split_axis=0, concat_axis=0, tiled=True)]
    ppermute x5, starting transfers between devices: 16.8 us -> 11.1 us  [routed(): return lax.ppermute(block, ('seq', 'head'), route)]
    all_to_all x3 -> x2, starting transfers between devices: 22.4 us -> 17.1 us  [exchange(): return lax.all_to_all(block, 'seq', split_axis=0, concat_axis=0, tiled=True)]
    all_to_all x3 -> x2, waiting for transfers between devices: 57.8 us -> 54.5 us  [exchange(): return lax.all_to_all(block, 'seq', split_axis=0, concat_axis=0, tiled=True)]
  transfers between devices with their start and end apart: 8 -> 7, of which waited for: 3 -> 2; matrix products, arithmetic and copies ran while one was open for 2% -> 2% of each run, Pallas kernels for 8% -> 8%
where the time goes in v10:
time: 237 us
  blocking collectives  82.3 us (35%)
  waiting for transfers between devices  63 us (27%)
  Pallas kernels  54 us (23%)
  starting transfers between devices  28.2 us (12%)
  local copies, waits for them, and re-layouts  7.22 us (3%)
    all_to_all x2, blocking collectives, exchange(): return lax.all_to_all(block, 'seq', split_axis=0, concat_axis=0, tiled=True)  82.3 us
    all_to_all x2, waiting for transfers between devices, exchange(): return lax.all_to_all(block, 'seq', split_axis=0, concat_axis=0, tiled=True)  54.5 us
    all_to_all x2, starting transfers between devices, exchange(): return lax.all_to_all(block, 'seq', split_axis=0, concat_axis=0, tiled=True)  17.1 us
    pallas_call x1, Pallas kernels, backward(): pl.pallas_call(backward_body, in_specs=[table_spec(), pl.BlockSpec(next_t...  12.5 us
    pallas_call x1, Pallas kernels, forward_own(): pl.pallas_call(own_body, grid=(2, 2), in_specs=[pl.BlockSpec((LANES, LANE...  11.2 us
    ppermute x5, starting transfers between devices, routed(): return lax.ppermute(block, ('seq', 'head'), route)  11.1 us
    ppermute x5, waiting for transfers between devices, routed(): return lax.ppermute(block, ('seq', 'head'), route)  8.46 us
    pallas_call x1, Pallas kernels, forward_edge(): pl.pallas_call(edge_body, in_specs=[table_spec()] + anywhere(5), out_spec...  7.63 us
  transfers between devices with their start and end apart: 7, of which 2 were waited for; matrix products, arithmetic and copies ran while one was open for 2% of the time, Pallas kernels for 8%

profile of v10, /device:TPU:0, one launch (start us, length us, event | category | flops | bytes accessed | tf_op | source)
XLA Modules:
  0.0 236.6 jit_solution(3601703037913784978)
XLA Ops:
  0.6 0.8 reshape.73
  1.6 0.7 reshape_reshape.12.index_ref
  2.3 5.8 %pack_rows.1 = bf16[1536,1536]{1,0:T(8,128)(2,1)} custom-call(s32[12,128]{1,0:T(8,128)} %reshape_reshape.12.index_ref, bf16[512,512]{1,0:T(8,128)(2,1)} %refs_0_.1, bf16[512,512]{1,0:T(8,128)(2,1)} %refs_1_.1, bf16[512,512]{1,0:T(8,128)(2,1)} %refs_2_.1), custom_call_target="tpu_custom_call" | custom-call | flops 2415919104 | bytes 6291456 | tf_op jit(solution)/shard_map/pack_rows/pallas_call | solution.py:159
  8.2 11.9 %all-to-all-start = ((bf16[64,24,1536]{2,1,0:T(8,128)(2,1)}), bf16[64,24,1536]{2,1,0:T(8,128)(2,1)}, u32[]{:S(2)}, u32[]{:S(2)}) async-start(bf16[64,24,1536]{2,1,0:T(8,128)(2,1)} %bitcast.30), calls=%async_computation | async-start | bytes 9437184 | tf_op jit(solution)/shard_map/all_to_all | solution.py:64
  20.2 0.7 collective-permute-start
  23.0 0.6 concatenate.7
  23.6 0.6 pad.4.table_ref
  24.2 54.5 %all-to-all-done = bf16[64,24,1536]{2,1,0:T(8,128)(2,1)} async-done(((bf16[64,24,1536]{2,1,0:T(8,128)(2,1)}), bf16[64,24,1536]{2,1,0:T(8,128)(2,1)}, u32[]{:S(2)}, u32[]{:S(2)}) %all-to-all-start) | async-done | bytes 4718624 | tf_op jit(solution)/shard_map/all_to_all | solution.py:64
  78.7 5.4 %sort_tail.1.tail_query_ref.tail_value_ref.tail_ref = bf16[512,1024]{1,0:T(8,128)(2,1)} custom-call(s32[128,128]{1,0:T(8,128)} %pad.4.table_ref, bf16[1536,1536]{1,0:T(8,128)(2,1)} %bitcast.2.arrived_ref.arrived_query_ref.arrived_value_ref.arrived_cotangent_ref), custom_call_target="tpu_custom_call" | custom-call | flops 1610612736 | bytes 4194304 | tf_op jit(solution)/shard_map/sort_tail/pallas_call | solution.py:206
  84.5 0.7 slice.19
  85.2 11.2 %forward_own.1 = (bf16[512,512]{1,0:T(8,128)(2,1)}, bf16[512,512]{1,0:T(8,128)(2,1)}, bf16[512,512]{1,0:T(8,128)(2,1)}, bf16[512,512]{1,0:T(8,128)(2,1)}, bf16[512,512]{1,0:T(8,128)(2,1)}, /*index=5*/f32[512,256]{1,0:T(8,128)}) custom-call(s32[128,128]{1,0:T(8,128)} %pad.4.table_ref, ...), custom_call_target="tpu_custom_call" | custom-call | flops 5000000000 | bytes 10000000 | tf_op jit(solution)/shard_map/forward_own/pallas_call | solution.py:305
  96.4 8.4 %collective-permute-done.1.prior_ref = bf16[512,1024]{1,0:T(8,128)(2,1)S(1)} collective-permute-done((bf16[512,1024]{1,0:T(8,128)(2,1)}, bf16[512,1024]{1,0:T(8,128)(2,1)S(1)}, u32[]{:S(2)}, u32[]{:S(2)}) %collective-permute-start.1) | collective-permute-done | bytes 1048608 | tf_op jit(solution)/shard_map/ppermute | solution.py:44
  104.8 1.0 copy-done.8
  105.8 7.6 %forward_edge.1 = (bf16[512,512]{1,0:T(8,128)(2,1)}, f32[512,128]{1,0:T(8,128)}) custom-call(s32[128,128]{1,0:T(8,128)} %pad.4.table_ref, bf16[512,512]{1,0:T(8,128)(2,1)} %get-tuple-element.34.query_ref.head_query_ref, bf16[512,512]{1,0:T(8,128)(2,1)} %get-tuple-element.23.value_ref.head_value_ref, ...), custom_call_target="tpu_custom_call" | custom-call | flops 2000000000 | bytes 4000000 | tf_op jit(solution)/shard_map/forward_edge/pallas_call | solution.py:405
  113.4 16.4 %all_to_all.20 = f32[64,8,128]{2,1,0:T(8,128)S(1)} all-to-all(f32[64,8,128]{2,1,0:T(8,128)} %bitcast.32), channel_id=1, replica_groups=mesh['seq'=64,'head'=2] {'seq'}, dimensions={0} | all-to-all | bytes 524288 | tf_op jit(solution)/shard_map/all_to_all | solution.py:64
  129.9 2.2 collective-permute-start.3
  132.4 2.1 total_stats.1
  134.5 5.3 %all-to-all-start.2 = ((f32[64,16,128]{2,1,0:T(8,128)}), f32[64,16,128]{2,1,0:T(8,128)S(1)}, u32[]{:S(2)}, u32[]{:S(2)}) async-start(f32[64,16,128]{2,1,0:T(8,128)} %total_stats.1), calls=%async_computation.2 | async-start | bytes 1048576 | tf_op jit(solution)/shard_map/all_to_all | solution.py:64
  139.7 7.6 %collective-permute-start.2 = (s32[24,128]{1,0:T(8,128)S(1)}, s32[24,128]{1,0:T(8,128)S(1)}, u32[]{:S(2)}, u32[]{:S(2)}) collective-permute-start(s32[24,128]{1,0:T(8,128)S(1)} %slice.19), channel_id=1, source_target_pairs={{0,126},{1,3},{2,0},{3,5},{4,2},{5,7},{6,4},{7,9},{8,6},{9,11},{10... | collective-permute-start | bytes 36872 | tf_op jit(solution)/shard_map/ppermute | solution.py:44
  147.4 5.1 %prepare_outputs.1 = (bf16[1536,1536]{1,0:T(8,128)(2,1)}, f32[512,128]{1,0:T(8,128)}) custom-call(s32[128,128]{1,0:T(8,128)} %pad.4.table_ref, f32[512,128]{1,0:T(8,128)} %bitcast.29, bf16[512,512]{1,0:T(8,128)(2,1)} %get-tuple-element.29.first_ref, bf16[512,512]{1,0:T(8,128)(2,1)} %get-tuple-element.30.second_ref), custom_call_target="tpu_custom_call" | custom-call | flops 2000000000 | bytes 10000000 | tf_op jit(solution)/shard_map/prepare_outputs/pallas_call | solution.py:508
  152.5 0.5 copy-done.11
  153.7 12.5 %backward.1 = bf16[1536,1536]{1,0:T(8,128)(2,1)} custom-call(s32[128,128]{1,0:T(8,128)} %pad.4.table_ref, s32[24,128]{1,0:T(8,128)} %copy-done.11, f32[64,16,128]{2,1,0:T(8,128)} %copy-done.4, bf16[512,512]{1,0:T(8,128)(2,1)} %get-tuple-element.34.query_ref.head_query_ref, ...), custom_call_target="tpu_custom_call", output_to_operand_aliasing={{}: (11, {})} | custom-call | flops 8000000000 | bytes 15000000 | tf_op jit(solution)/shard_map/backward/pallas_call | solution.py:734
  166.3 65.8 %all_to_all.21 = bf16[64,24,1536]{2,1,0:T(8,128)(2,1)S(1)} all-to-all(bf16[64,24,1536]{2,1,0:T(8,128)(2,1)} %bitcast.31), channel_id=1, replica_groups=mesh['seq'=64,'head'=2] {'seq'}, dimensions={0} | all-to-all | bytes 9437184 | tf_op jit(solution)/shard_map/all_to_all | solution.py:64
  232.1 4.3 %combine_rows.1 = (bf16[512,512]{1,0:T(8,128)(2,1)}, bf16[512,512]{1,0:T(8,128)(2,1)}, bf16[512,512]{1,0:T(8,128)(2,1)}) custom-call(s32[128,128]{1,0:T(8,128)S(1)} %copy-done.2, f32[512,128]{1,0:T(8,128)S(1)} %copy-done.3, bf16[1536,1536]{1,0:T(8,128)(2,1)S(1)} %bitcast.27), custom_call_target="tpu_custom_call" | custom-call | flops 2415919104 | bytes 6291456 | tf_op jit(solution)/shard_map/combine_rows/pallas_call | solution.py:814
  (68 shorter events, 3.5 us)
Async XLA Ops:
  8.2 11.9 %copy-start.6 = (s32[2,512]{1,0:T(2,128)S(1)}, s32[2,512]{1,0:T(2,128)}, u32[]{:S(2)}) copy-start(s32[2,512]{1,0:T(2,128)} %param.11) | copy-start | bytes 12292
  8.2 11.9 %copy-start.7 = (s32[2,64]{1,0:T(2,128)S(1)}, s32[2,64]{1,0:T(2,128)}, u32[]{:S(2)}) copy-start(s32[2,64]{1,0:T(2,128)} %param.10) | copy-start | bytes 1540
  8.2 14.7 %copy-start.5 = (s32[12,128]{1,0:T(8,128)S(1)}, s32[12,128]{1,0:T(8,128)}, u32[]{:S(2)}) copy-start(s32[12,128]{1,0:T(8,128)} %reshape_reshape.12.index_ref) | copy-start | bytes 18436
  8.2 70.5 %all-to-all-start = ((bf16[64,24,1536]{2,1,0:T(8,128)(2,1)}), bf16[64,24,1536]{2,1,0:T(8,128)(2,1)}, u32[]{:S(2)}, u32[]{:S(2)}) async-start(bf16[64,24,1536]{2,1,0:T(8,128)(2,1)} %bitcast.30), calls=%async_computation | async-start | bytes 9437184 | tf_op jit(solution)/shard_map/all_to_all | solution.py:64
  20.2 1.3 collective-permute-start
  84.1 20.7 %collective-permute-start.1 = (bf16[512,1024]{1,0:T(8,128)(2,1)}, bf16[512,1024]{1,0:T(8,128)(2,1)S(1)}, u32[]{:S(2)}, u32[]{:S(2)}) collective-permute-start(bf16[512,1024]{1,0:T(8,128)(2,1)} %sort_tail.1.tail_query_ref.tail_value_ref.tail_ref), channel_id=1, source_target_pairs={{0,2},{1,127},{2,4},{3,1},{4,6},{5,3},{6,8},{7,5},{8,10},{9,7},{10... | collective-permute-start | bytes 3145736 | tf_op jit(solution)/shard_map/ppermute | solution.py:44
  96.4 36.0 %copy-start.1 = (s32[128,128]{1,0:T(8,128)S(1)}, s32[128,128]{1,0:T(8,128)}, u32[]{:S(2)}) copy-start(s32[128,128]{1,0:T(8,128)} %pad.4.table_ref) | copy-start | bytes 196612
  104.8 1.0 copy-start.8
  129.9 17.5 %copy-start = (f32[64,8,128]{2,1,0:T(8,128)}, f32[64,8,128]{2,1,0:T(8,128)S(1)}, u32[]{:S(2)}) copy-start(f32[64,8,128]{2,1,0:T(8,128)S(1)} %all_to_all.20) | copy-start | bytes 786436
  129.9 22.6 %collective-permute-start.3 = (bf16[512,512]{1,0:T(8,128)(2,1)}, bf16[512,512]{1,0:T(8,128)(2,1)S(1)}, u32[]{:S(2)}, u32[]{:S(2)}) collective-permute-start(bf16[512,512]{1,0:T(8,128)(2,1)} %get-tuple-element.34.query_ref.head_query_ref), channel_id=1, source_target_pairs={{0,126},{1,3},{2,0},{3,5},{4,2},{5,7},{6,4},{7,9},{8,6},{9,11},{10... | collective-permute-start | bytes 1572872 | tf_op jit(solution)/shard_map/ppermute | solution.py:44
  132.1 20.4 %collective-permute-start.4 = (bf16[512,512]{1,0:T(8,128)(2,1)}, bf16[512,512]{1,0:T(8,128)(2,1)S(1)}, u32[]{:S(2)}, u32[]{:S(2)}) collective-permute-start(bf16[512,512]{1,0:T(8,128)(2,1)} %get-tuple-element.35.cotangent_ref.head_cotangent_ref), channel_id=1, source_target_pairs={{0,126},{1,3},{2,0},{3,5},{4,2},{5,7},{6,4},{7,9},{8,6},{9,11},{10... | collective-permute-start | bytes 1572872 | tf_op jit(solution)/shard_map/ppermute | solution.py:44
  134.5 18.0 %all-to-all-start.2 = ((f32[64,16,128]{2,1,0:T(8,128)}), f32[64,16,128]{2,1,0:T(8,128)S(1)}, u32[]{:S(2)}, u32[]{:S(2)}) async-start(f32[64,16,128]{2,1,0:T(8,128)} %total_stats.1), calls=%async_computation.2 | async-start | bytes 1048576 | tf_op jit(solution)/shard_map/all_to_all | solution.py:64
  139.7 12.7 %collective-permute-start.2 = (s32[24,128]{1,0:T(8,128)S(1)}, s32[24,128]{1,0:T(8,128)S(1)}, u32[]{:S(2)}, u32[]{:S(2)}) collective-permute-start(s32[24,128]{1,0:T(8,128)S(1)} %slice.19), channel_id=1, source_target_pairs={{0,126},{1,3},{2,0},{3,5},{4,2},{5,7},{6,4},{7,9},{8,6},{9,11},{10... | collective-permute-start | bytes 36872 | tf_op jit(solution)/shard_map/ppermute | solution.py:44
  152.5 0.6 copy-start.11
  152.5 0.8 copy-start.4
  152.5 1.0 copy-start.9
  152.5 1.2 copy-start.10
  166.2 65.9 %copy-start.2 = (s32[128,128]{1,0:T(8,128)S(1)}, s32[128,128]{1,0:T(8,128)}, u32[]{:S(2)}) copy-start(s32[128,128]{1,0:T(8,128)} %pad.4.table_ref) | copy-start | bytes 196612
  166.2 65.8 %copy-start.3 = (f32[512,128]{1,0:T(8,128)S(1)}, f32[512,128]{1,0:T(8,128)}, u32[]{:S(2)}) copy-start(f32[512,128]{1,0:T(8,128)} %get-tuple-element.31.share_ref) | copy-start | bytes 786436
